TPU v7x, 128 devices: a whole 4x4x4 slice. The times are simulated.
128 devices in a mesh: dp: 4 (over y), expert: 32 (over z, x, core).
Axes of the slice: x: 4, y: 4, z: 4, core: 2. Of those that a mesh axis runs over, the one named last changes fastest.
Arguments:
- tokens: bfloat16 [6144, 4096], P(('dp', 'expert')), may hold values from -6 to 6
- out_grad: bfloat16 [6144, 4096], P(('dp', 'expert')), may hold values from -6 to 6
- expert_ids: int32 [6144, 8], P(('dp', 'expert')), may hold values from 0 to 31, all different within a row; in each aligned block of 48 rows (0 to 47, 48 to 95, ...) at most 18 rows name the same one
- route_probs: float32 [6144, 8], P(('dp', 'expert')), may hold values from 0.05 to 1
- w_gate: bfloat16 [32, 4096, 768], P('expert'), may hold values from -0.09375 to 0.09375
- w_up: bfloat16 [32, 4096, 768], P('expert'), may hold values from -0.09375 to 0.09375
- w_down: bfloat16 [32, 768, 4096], P('expert'), may hold values from -0.21875 to 0.21875
Outputs:
- token_grad: bfloat16 [6144, 4096], P(('dp', 'expert'))
- gate_grad: bfloat16 [32, 4096, 768], P('expert', 'dp')
- up_grad: bfloat16 [32, 4096, 768], P('expert', 'dp')
- down_grad: bfloat16 [32, 768, 4096], P('expert', None, 'dp')
Inputs may be any that keep to these rules, and one draw needn't show every extreme that they name: `expert_ids`: each token names 8 different experts; among the tokens of one device no expert is named by more than 18 tokens, and some expert reaches 18.
All inputs are finite; a program needn't handle non-finite values.
Results may differ from a plain program's by a relative error of at most 0.0064.
Values may be sent and summed in bfloat16 or wider, within the bound.
No kernel may reach another device: no remote copies, remote signals or barrier semaphores. Data moves between devices by JAX's collectives and lax.ppermute only.
A program may use at most 256 MiB of HBM per device.

v0:
```python
import jax
import jax.numpy as jnp
from jax import lax
from jax.sharding import PartitionSpec as P


def contract(left, right):
    return lax.dot_general(
        left, right, (((0,), (0,)), ((), ())), preferred_element_type=jnp.float32
    )


def on_device(tokens, out_grad, expert_ids, route_probs, w_gate, w_up, w_down):
    tok_rows, width = tokens.shape
    topk = expert_ids.shape[1]
    groups = lax.axis_size("expert")
    capacity = 3 * tok_rows * topk // (2 * groups)
    nrows = tok_rows * topk
    hidden_width = w_gate.shape[2]
    ids = expert_ids.reshape(nrows)
    onehot = (ids[:, None] == jnp.arange(groups, dtype=jnp.int32)[None, :]).astype(jnp.int32)
    before = jnp.cumsum(onehot, axis=0) - onehot
    slot = jnp.sum(before * onehot, axis=1)
    place = ids * capacity + slot
    match = place[None, :] == jnp.arange(groups * capacity, dtype=jnp.int32)[:, None]
    live = jnp.any(match, axis=1)
    src_row = jnp.sum(jnp.where(match, jnp.arange(nrows, dtype=jnp.int32)[None, :], 0), axis=1)
    src_tok = src_row // topk
    probs = route_probs.reshape(nrows)
    send_x = jnp.where(live[:, None], tokens[src_tok], jnp.zeros((), tokens.dtype)).reshape(
        groups, capacity, width
    )
    send_dy = jnp.where(
        live[:, None], out_grad[src_tok].astype(jnp.float32) * probs[src_row][:, None], 0.0
    )
    send_dy = send_dy.astype(jnp.bfloat16).reshape(groups, capacity, width)
    wgate = w_gate[0]
    wup = w_up[0]
    wdown = w_down[0]
    inputs = lax.all_to_all(send_x, "expert", split_axis=0, concat_axis=0, tiled=True)
    scaled = lax.all_to_all(send_dy, "expert", split_axis=0, concat_axis=0, tiled=True)
    count = inputs.shape[1]
    expert_flat_x = inputs.reshape(-1, width)
    expert_flat_dy = scaled.reshape(-1, width)
    gate = jnp.dot(expert_flat_x, wgate, preferred_element_type=jnp.float32)
    upval = jnp.dot(expert_flat_x, wup, preferred_element_type=jnp.float32)
    sgate = jax.nn.silu(gate)
    hidden = (sgate * upval).astype(jnp.bfloat16)
    dhidden = lax.dot_general(
        expert_flat_dy, wdown, (((1,), (1,)), ((), ())), preferred_element_type=jnp.float32
    )
    sigma = jax.nn.sigmoid(gate)
    dgate = (dhidden * upval * sigma * (1.0 + gate * (1.0 - sigma))).astype(jnp.bfloat16)
    dup = (dhidden * sgate).astype(jnp.bfloat16)
    row_grad = lax.dot_general(
        dgate, wgate, (((1,), (1,)), ((), ())), preferred_element_type=jnp.float32
    )
    row_grad = row_grad + lax.dot_general(
        dup, wup, (((1,), (1,)), ((), ())), preferred_element_type=jnp.float32
    )
    row_grad = row_grad.astype(jnp.bfloat16).reshape(groups, count, width)
    back = lax.all_to_all(row_grad, "expert", split_axis=0, concat_axis=0, tiled=True)
    shape_ff = (groups, count, hidden_width)
    back, recv_x, recv_dy, hidden, dgate, dup = (
        back,
        inputs,
        scaled,
        hidden.reshape(shape_ff),
        dgate.reshape(shape_ff),
        dup.reshape(shape_ff),
    )
    gathered = back.reshape(groups * capacity, width)[place].astype(jnp.float32)
    token_grad = jnp.sum(gathered.reshape(tok_rows, topk, width), axis=1).astype(jnp.bfloat16)
    flat_x = recv_x.reshape(-1, width)
    flat_dy = recv_dy.reshape(-1, width)
    flat_h = hidden.reshape(-1, hidden_width)
    flat_dg = dgate.reshape(-1, hidden_width)
    flat_du = dup.reshape(-1, hidden_width)
    summed = lax.psum_scatter(
        jnp.concatenate(
            [contract(flat_x, flat_dg), contract(flat_x, flat_du), contract(flat_dy, flat_h)],
            axis=1,
        ),
        "dp",
        scatter_dimension=0,
        tiled=True,
    )
    gate_grad = summed[:, :hidden_width].astype(jnp.bfloat16)
    up_grad = summed[:, hidden_width : 2 * hidden_width].astype(jnp.bfloat16)
    down_grad = summed[:, 2 * hidden_width :].T.astype(jnp.bfloat16)
    return (token_grad, gate_grad[None], up_grad[None], down_grad[None])


def solution(mesh):
    in_specs = (
        P(("dp", "expert"), None),
        P(("dp", "expert"), None),
        P(("dp", "expert"), None),
        P(("dp", "expert"), None),
        P("expert", None, None),
        P("expert", None, None),
        P("expert", None, None),
    )
    out_specs = (
        P(("dp", "expert"), None),
        P("expert", "dp", None),
        P("expert", "dp", None),
        P("expert", None, "dp"),
    )
    return jax.shard_map(
        on_device, mesh=mesh, in_specs=in_specs, out_specs=out_specs, check_vma=False
    )
```

profile of v0, /device:TPU:1, one launch (start us, length us, event | category | flops | bytes accessed | tf_op | source)
XLA Modules:
  0.0 595.2 jit_solution(1747490220288359178)
XLA Ops:
  7.2 0.8 copy.20
  8.0 0.1 reshape.173
  8.1 0.1 eq.39
  8.2 0.9 reduce-window.6
  9.1 0.2 slice_reduce_fusion
  9.3 0.1 fusion.18
  9.5 0.2 fusion.14
  9.7 0.4 copy-done.5
  10.0 0.2 select_reduce_fusion
  10.2 0.1 broadcast_in_dim.56
  10.4 5.2 gather_fusion.2
  15.6 7.6 %gather.19 = bf16[32,18,4096]{2,1,0:T(8,128)(2,1)} reshape(bf16[576,4096]{1,0:T(8,128)(2,1)} %gather_fusion.2) | data formatting | bytes 9437184 | tf_op jit(solution)/shard_map/gather | solution.py:30
  23.1 6.0 %broadcast_select_fusion = bf16[32,18,4096]{2,1,0:T(8,128)(2,1)} fusion(bf16[32,18,4096]{2,1,0:T(8,128)(2,1)} %gather.19, pred[32,18]{1,0:T(8,128)(4,1)S(1)} %broadcast_in_dim.56), kind=kLoop, calls=%fused_computation.17 | loop fusion | flops 2359296 | bytes 9437760 | tf_op jit(solution)/shard_map/jit(_where)/select_n | solution.py:30
  29.1 9.6 %all-to-all-start.1 = ((bf16[32,18,4096]{2,1,0:T(8,128)(2,1)}), bf16[32,18,4096]{2,1,0:T(8,128)(2,1)}, u32[]{:S(2)}, u32[]{:S(2)}) async-start(bf16[32,18,4096]{2,1,0:T(8,128)(2,1)} %broadcast_select_fusion), calls=%async_computation.1 | async-start | bytes 12582912 | tf_op jit(solution)/shard_map/all_to_all | solution.py:40
  38.8 0.1 copy.23
  38.8 0.1 reshape.175
  38.9 4.0 gather_fusion.1
  42.9 0.1 mul.63
  43.0 5.1 gather_fusion
  48.2 8.4 %reshape.180 = f32[32,18,4096]{2,1,0:T(8,128)} reshape(bf16[576,4096]{1,0:T(8,128)(2,1)} %gather_fusion) | data formatting | bytes 14155776 | tf_op jit(solution)/shard_map/convert_element_type | solution.py:34
  56.6 10.0 %select_convert_fusion = bf16[32,18,4096]{2,1,0:T(8,128)(2,1)} fusion(f32[32,18,4096]{2,1,0:T(8,128)} %reshape.180, f32[32,18]{1,0:T(8,128)S(1)} %mul.63, pred[32,18]{1,0:T(8,128)(4,1)S(1)} %broadcast_in_dim.56), kind=kLoop, calls=%fused_computation.5 | loop fusion | flops 7077888 | bytes 14158656 | tf_op jit(solution)/shard_map/convert_element_type | solution.py:36
  66.6 45.0 %all-to-all-done.1 = bf16[32,18,4096]{2,1,0:T(8,128)(2,1)} async-done(((bf16[32,18,4096]{2,1,0:T(8,128)(2,1)}), bf16[32,18,4096]{2,1,0:T(8,128)(2,1)}, u32[]{:S(2)}, u32[]{:S(2)}) %all-to-all-start.1) | async-done | bytes 4718624 | tf_op jit(solution)/shard_map/all_to_all | solution.py:40
  111.7 9.7 %all-to-all-start = ((bf16[32,18,4096]{2,1,0:T(8,128)(2,1)}), bf16[32,18,4096]{2,1,0:T(8,128)(2,1)}, u32[]{:S(2)}, u32[]{:S(2)}) async-start(bf16[32,18,4096]{2,1,0:T(8,128)(2,1)} %select_convert_fusion), calls=%async_computation | async-start | bytes 12582912 | tf_op jit(solution)/shard_map/all_to_all | solution.py:41
  121.4 0.5 reduce-scatter.2.cloned.1.call-start
  121.9 7.9 %reshape.177 = bf16[576,4096]{1,0:T(8,128)(2,1)} reshape(bf16[32,18,4096]{2,1,0:T(8,128)(2,1)} %all-to-all-done.1) | data formatting | bytes 9437184 | tf_op jit(solution)/shard_map/reshape | solution.py:43
  129.9 9.4 %fusion.2 = f32[576,768]{1,0:T(8,128)} fusion(bf16[576,4096]{1,0:T(8,128)(2,1)} %reshape.177, bf16[1,4096,768]{2,1,0:T(8,128)(2,1)} %param.11), kind=kOutput, calls=%fused_computation.9 | convolution fusion | flops 3623878656 | bytes 12779520 | tf_op jit(solution)/shard_map/dot_general | solution.py:45
  139.2 5.1 fusion.6
  144.4 50.1 %all-to-all-done = bf16[32,18,4096]{2,1,0:T(8,128)(2,1)} async-done(((bf16[32,18,4096]{2,1,0:T(8,128)(2,1)}), bf16[32,18,4096]{2,1,0:T(8,128)(2,1)}, u32[]{:S(2)}, u32[]{:S(2)}) %all-to-all-start) | async-done | bytes 4718624 | tf_op jit(solution)/shard_map/all_to_all | solution.py:41
  194.4 7.9 %reshape.176 = bf16[576,4096]{1,0:T(8,128)(2,1)} reshape(bf16[32,18,4096]{2,1,0:T(8,128)(2,1)} %all-to-all-done) | data formatting | bytes 9437184 | tf_op jit(solution)/shard_map/reshape | solution.py:44
  202.4 11.8 %fusion.13 = f32[4096,768]{0,1:T(8,128)} fusion(bf16[576,4096]{1,0:T(8,128)(2,1)} %reshape.176, f32[576,768]{1,0:T(8,128)} %fusion.6, f32[576,768]{1,0:T(8,128)} %fusion.2), kind=kOutput, calls=%fused_computation.27 | convolution fusion | flops 3626532864 | bytes 20840448 | tf_op jit(solution)/shard_map/dot_general | solution.py:8
  214.2 4.3 multiply_convert_fusion.1
  218.6 8.1 %fusion.25 = f32[4096,768]{0,1:T(8,128)} fusion(bf16[576,4096]{1,0:T(8,128)(2,1)S(1)} %bitcast.58, bf16[576,768]{1,0:T(8,128)(2,1)S(1)} %get-tuple-element.21), kind=kOutput, calls=%fused_computation.57 | convolution fusion | flops 3623878656 | bytes 18186240 | tf_op jit(solution)/shard_map/dot_general | solution.py:8
  226.7 8.1 %fusion.24 = f32[4096,768]{0,1:T(8,128)} fusion(bf16[576,4096]{1,0:T(8,128)(2,1)S(1)} %bitcast.58, bf16[576,768]{1,0:T(8,128)(2,1)S(1)} %get-tuple-element.22), kind=kOutput, calls=%fused_computation.56 | convolution fusion | flops 3623878656 | bytes 18186240 | tf_op jit(solution)/shard_map/dot_general | solution.py:8
  234.9 25.7 %pad_maximum_fusion = f32[4096,2304]{0,1:T(8,128)} fusion(f32[4096,768]{0,1:T(8,128)} %fusion.13, f32[4096,768]{0,1:T(8,128)} %fusion.25, f32[4096,768]{0,1:T(8,128)} %fusion.24), kind=kLoop, calls=%fused_computation.4 | loop fusion | flops 18874368 | bytes 75497472 | tf_op jit(solution)/shard_map/concatenate | solution.py:80
  260.6 6.1 %fusion = f32[576,4096]{1,0:T(8,128)S(1)} fusion(bf16[576,768]{1,0:T(8,128)(2,1)S(1)} %get-tuple-element.22, bf16[1,4096,768]{2,1,0:T(8,128)(2,1)} %param.11), kind=kOutput, calls=%fused_computation.7 | convolution fusion | flops 3623878656 | bytes 16613376 | tf_op jit(solution)/shard_map/dot_general | solution.py:55
  266.7 8.2 %add_convert_fusion = bf16[576,4096]{1,0:T(8,128)(2,1)} fusion(f32[576,4096]{1,0:T(8,128)S(1)} %fusion, bf16[576,768]{1,0:T(8,128)(2,1)S(1)} %copy-done.12, bf16[1,4096,768]{2,1,0:T(8,128)(2,1)} %param.12), kind=kOutput, calls=%fused_computation.6 | convolution fusion | flops 3628597248 | bytes 21331968 | tf_op jit(solution)/shard_map/dot_general | solution.py:58
  275.0 7.8 %reshape.178 = bf16[32,18,4096]{2,1,0:T(8,128)(2,1)} reshape(bf16[576,4096]{1,0:T(8,128)(2,1)} %add_convert_fusion) | data formatting | bytes 9437184 | tf_op jit(solution)/shard_map/reshape | solution.py:61
  282.8 10.2 %all-to-all-start.2 = ((bf16[32,18,4096]{2,1,0:T(8,128)(2,1)}), bf16[32,18,4096]{2,1,0:T(8,128)(2,1)}, u32[]{:S(2)}, u32[]{:S(2)}) async-start(bf16[32,18,4096]{2,1,0:T(8,128)(2,1)} %reshape.178), calls=%async_computation.2 | async-start | bytes 12582912 | tf_op jit(solution)/shard_map/all_to_all | solution.py:62
  293.0 0.1 mul.74
  293.2 72.8 %all-to-all-done.2 = bf16[32,18,4096]{2,1,0:T(8,128)(2,1)} async-done(((bf16[32,18,4096]{2,1,0:T(8,128)(2,1)}), bf16[32,18,4096]{2,1,0:T(8,128)(2,1)}, u32[]{:S(2)}, u32[]{:S(2)}) %all-to-all-start.2) | async-done | bytes 4718624 | tf_op jit(solution)/shard_map/all_to_all | solution.py:62
  366.0 7.7 %reshape.179 = bf16[576,4096]{1,0:T(8,128)(2,1)} reshape(bf16[32,18,4096]{2,1,0:T(8,128)(2,1)} %all-to-all-done.2) | data formatting | bytes 9437184 | tf_op jit(solution)/shard_map/reshape | solution.py:72
  373.7 10.5 %gather_fusion.3 = bf16[384,4096]{1,0:T(8,128)(2,1)S(1)} fusion(bf16[576,4096]{1,0:T(8,128)(2,1)} %reshape.179, s32[1024]{0:T(1024)S(1)} %pad_clamp_fusion), kind=kCustom, calls=%fused_computation.3 | custom fusion | bytes 6292992 | tf_op jit(solution)/shard_map/gather | solution.py:72
  384.2 2.9 bitcast_reduce_fusion
  387.1 191.9 %reduce-scatter.2.cloned.1.call-done = f32[1024,2304]{0,1:T(8,128)} async-done(((f32[4096,2304]{0,1:T(8,128)}), f32[1024,2304]{0,1:T(8,128)}) %reduce-scatter.2.cloned.1.call-update) | async-done | bytes 9437200 | tf_op jit(solution)/shard_map/reduce_scatter | solution.py:79
  578.9 4.4 convert.7
  583.4 1.7 slice_bitcast_fusion
  585.0 1.6 copy.26
  586.6 1.6 copy.25
  (50 shorter events, 0.3 us)
Async XLA Ops:
  7.2 3.2 copy-start
  9.4 0.6 copy-start.5
  29.1 9.6 %copy-start.8 = (f32[48,8]{0,1:T(8,128)S(1)}, f32[48,8]{0,1:T(8,128)}, u32[]{:S(2)}) copy-start(f32[48,8]{0,1:T(8,128)} %param.10) | copy-start | bytes 4612
  29.1 82.6 %all-to-all-start.1 = ((bf16[32,18,4096]{2,1,0:T(8,128)(2,1)}), bf16[32,18,4096]{2,1,0:T(8,128)(2,1)}, u32[]{:S(2)}, u32[]{:S(2)}) async-start(bf16[32,18,4096]{2,1,0:T(8,128)(2,1)} %broadcast_select_fusion), calls=%async_computation.1 | async-start | bytes 12582912 | tf_op jit(solution)/shard_map/all_to_all | solution.py:40
  38.7 4.3 copy-start.2
  111.7 82.8 %all-to-all-start = ((bf16[32,18,4096]{2,1,0:T(8,128)(2,1)}), bf16[32,18,4096]{2,1,0:T(8,128)(2,1)}, u32[]{:S(2)}, u32[]{:S(2)}) async-start(bf16[32,18,4096]{2,1,0:T(8,128)(2,1)} %select_convert_fusion), calls=%async_computation | async-start | bytes 12582912 | tf_op jit(solution)/shard_map/all_to_all | solution.py:41
  121.4 457.5 %reduce-scatter.2.cloned.1.call-start = ((), (), s32[]{:S(2)}) async-start(), calls=%async_computation.4 | async-start | bytes 47185920 | tf_op jit(solution)/shard_map/reduce_scatter | solution.py:79
  121.9 17.3 %slice-start.4 = ((s8[6291456]{0:T(1024)(128)(4,1)}), s8[2097152]{0:T(1024)(128)(4,1)S(1)}, s32[]{:S(2)}) async-start(s8[6291456]{0:T(1024)(128)(4,1)} %bitcast.62), calls=%async_computation.9 | async-start | bytes 4194304
  129.9 9.4 %copy-start.3 = (bf16[576,4096]{1,0:T(8,128)(2,1)S(1)}, bf16[576,4096]{1,0:T(8,128)(2,1)}, u32[]{:S(2)}) copy-start(bf16[576,4096]{1,0:T(8,128)(2,1)} %reshape.177) | copy-start | bytes 14155780
  129.9 9.4 %slice-start.5 = ((s8[6291456]{0:T(1024)(128)(4,1)}), s8[4194304]{0:T(1024)(128)(4,1)S(1)}, s32[]{:S(2)}) async-start(s8[6291456]{0:T(1024)(128)(4,1)} %bitcast.62), calls=%async_computation.10 | async-start | bytes 8388608
  194.4 19.7 %slice-start.2 = ((s8[6291456]{0:T(1024)(128)(4,1)}), s8[2097152]{0:T(1024)(128)(4,1)S(1)}, s32[]{:S(2)}) async-start(s8[6291456]{0:T(1024)(128)(4,1)} %bitcast.60), calls=%async_computation.7 | async-start | bytes 4194304
  202.3 11.8 %copy-start.4 = (bf16[576,4096]{1,0:T(8,128)(2,1)S(1)}, bf16[576,4096]{1,0:T(8,128)(2,1)}, u32[]{:S(2)}) copy-start(bf16[576,4096]{1,0:T(8,128)(2,1)} %reshape.176) | copy-start | bytes 14155780
  202.3 11.8 %slice-start.3 = ((s8[6291456]{0:T(1024)(128)(4,1)}), s8[4194304]{0:T(1024)(128)(4,1)S(1)}, s32[]{:S(2)}) async-start(s8[6291456]{0:T(1024)(128)(4,1)} %bitcast.60), calls=%async_computation.8 | async-start | bytes 8388608
  202.3 11.8 %copy-start.9 = (f32[576,768]{1,0:T(8,128)S(1)}, f32[576,768]{1,0:T(8,128)}, u32[]{:S(2)}) copy-start(f32[576,768]{1,0:T(8,128)} %fusion.2) | copy-start | bytes 5308420
  202.3 11.9 %copy-start.10 = (f32[576,768]{1,0:T(8,128)S(1)}, f32[576,768]{1,0:T(8,128)}, u32[]{:S(2)}) copy-start(f32[576,768]{1,0:T(8,128)} %fusion.6) | copy-start | bytes 5308420
  202.3 16.2 %slice-start = ((s8[4718592]{0:T(1024)(128)(4,1)}), s8[4194304]{0:T(1024)(128)(4,1)S(1)}, s32[]{:S(2)}) async-start(s8[4718592]{0:T(1024)(128)(4,1)} %bitcast.57), calls=%async_computation.5 | async-start | bytes 8388608
  214.2 4.4 slice-start.1
  218.6 8.2 %copy-start.11 = (bf16[576,768]{1,0:T(8,128)(2,1)}, bf16[576,768]{1,0:T(8,128)(2,1)S(1)}, u32[]{:S(2)}) copy-start(bf16[576,768]{1,0:T(8,128)(2,1)S(1)} %get-tuple-element.21) | copy-start | bytes 2654212
  260.6 6.1 %copy-start.12 = (bf16[576,768]{1,0:T(8,128)(2,1)S(1)}, bf16[576,768]{1,0:T(8,128)(2,1)}, u32[]{:S(2)}) copy-start(bf16[576,768]{1,0:T(8,128)(2,1)} %copy-done.11) | copy-start | bytes 2654212
  282.8 10.2 %copy-start.7 = (s32[48,8]{0,1:T(8,128)S(1)}, s32[48,8]{0,1:T(8,128)}, u32[]{:S(2)}) copy-start(s32[48,8]{0,1:T(8,128)} %param.9) | copy-start | bytes 4612
  282.8 10.4 %copy-start.6 = (s32[384]{0:T(512)S(1)}, s32[384]{0:T(512)}, u32[]{:S(2)}) copy-start(s32[384]{0:T(512)} %copy-done.5) | copy-start | bytes 4612
  282.8 83.2 %all-to-all-start.2 = ((bf16[32,18,4096]{2,1,0:T(8,128)(2,1)}), bf16[32,18,4096]{2,1,0:T(8,128)(2,1)}, u32[]{:S(2)}, u32[]{:S(2)}) async-start(bf16[32,18,4096]{2,1,0:T(8,128)(2,1)} %reshape.178), calls=%async_computation.2 | async-start | bytes 12582912 | tf_op jit(solution)/shard_map/all_to_all | solution.py:62
  583.3 4.8 copy-start.1
Sparse Core Ops, SparseCore 0:
  260.8 318.1 reduce-scatter.1
where the time goes:
time: 603 us; the launch traced here: 595 us
  waiting for transfers between devices  360 us (60%)
  local copies, waits for them, and re-layouts  79.1 us (13%)
  matrix products  61.2 us (10%)
  other arithmetic  50.5 us (8%)
  starting transfers between devices  30 us (5%)
  between operations  14.6 us (2%)
    reduce_scatter x1, waiting for transfers between devices, on_device(): lax.psum_scatter(jnp.concatenate([contract(flat_x, flat_dg), contract(fla...  192 us
    all_to_all x1, waiting for transfers between devices, on_device(): lax.all_to_all(row_grad, 'expert', split_axis=0, concat_axis=0, tiled=True)  72.8 us
    all_to_all x1, waiting for transfers between devices, on_device(): lax.all_to_all(send_dy, 'expert', split_axis=0, concat_axis=0, tiled=True)  50.1 us
    all_to_all x1, waiting for transfers between devices, on_device(): lax.all_to_all(send_x, 'expert', split_axis=0, concat_axis=0, tiled=True)  45 us
    dot_general x3, matrix products, contract(): lax.dot_general(left, right, (((0,), (0,)), ((), ())), preferred_element_...  28.1 us
    concatenate x1, other arithmetic, on_device(): jnp.concatenate([contract(flat_x, flat_dg), contract(flat_x, flat_du), co...  25.7 us
    gather x2, local copies, waits for them, and re-layouts, on_device(): tokens[src_tok]  12.8 us
  transfers between devices with their start and end apart: 4, of which 4 were waited for; matrix products, arithmetic and copies ran while one was open for 16% of the time, Pallas kernels for 0%

commit v1 on v0

v1 whole, which is shorter than its diff:
```python
import functools

import jax
import jax.numpy as jnp
from jax import lax
from jax.experimental import pallas as pl
from jax.experimental.pallas import tpu as pltpu
from jax.sharding import PartitionSpec as P

BF16 = jnp.bfloat16
F32 = jnp.float32
OFFSETS = (0, -1, 1, 2)
NT = (((1,), (1,)), ((), ()))
TN = (((0,), (0,)), ((), ()))
NN = (((1,), (0,)), ((), ()))


def dot(a, b, dims=NN):
    return lax.dot_general(a, b, dims, preferred_element_type=F32)


def expert_pairs(ring, shift):
    pairs = []
    for e in range(32):
        z, x, c = e // 8, (e // 2) % 4, e % 2
        if (ring == 1) == (c == 0):
            dst = ((z + shift) % 4) * 8 + x * 2 + c
        else:
            dst = z * 8 + ((x + shift) % 4) * 2 + c
        pairs.append((e, dst))
    return pairs


def step(v, ring, shift):
    return lax.ppermute(v, "expert", expert_pairs(ring, shift))


def swap_core(v):
    return lax.ppermute(v, "expert", [(e, e ^ 1) for e in range(32)])


def ring_blocks(v, ring):
    before = step(v, ring, 1)
    after = step(v, ring, -1)
    far0 = step(before[0], ring, 1)
    far1 = step(after[1], ring, -1)
    return v, before, after, far0, far1


def ring_stack(v, ring):
    own, before, after, far0, far1 = ring_blocks(v, ring)
    far = jnp.stack([far0, far1])
    return jnp.concatenate([own, before, after, far], axis=-2)


def plane_gather(v):
    return ring_blocks(ring_stack(v, 1), 2)


def ring_reduce(parts, ring):
    own, before, after, far = parts
    half = far.shape[-1] // 2
    got_b = step(far[..., :half], ring, -1)
    got_a = step(far[..., half:], ring, 1)

    def add(a, b):
        return (a.astype(F32) + b.astype(F32)).astype(BF16)

    before = jnp.concatenate([add(before[..., :half], got_b), before[..., half:]], axis=-1)
    after = jnp.concatenate([after[..., :half], add(after[..., half:], got_a)], axis=-1)
    from_after = step(before, ring, -1)
    from_before = step(after, ring, 1)
    total = own.astype(F32) + from_after.astype(F32) + from_before.astype(F32)
    return total


def tile_of(t, core, half):
    return jnp.where(t < half, core * half + t, (1 - core) * half + t - half)


def forward_kernel(
    place, slot_own, slot_sib, prob, o0, o1, o2, ox, oy, s0, s1, s2, sx, sy, wg, wu, wd,
    h_ref, xi_ref, yi_ref, hot_own, hot_sib, prob_row, xs, ys, gate, up, dh, *, half, cap,
):
    t = pl.program_id(0)
    core, grp = place[0], place[1]
    rows = gate.shape[0]
    part = rows // 4
    width = xs.shape[1]

    @pl.when(t == 0)
    def _():
        total = jnp.zeros((rows, 1), F32)
        for p in range(4):
            r = lax.broadcasted_iota(jnp.int32, (part, slot_own.shape[1]), 0) + part * p
            hit = slot_own[p : p + 1, :] == r
            hot_own[p] = jnp.where(hit, 1.0, 0.0).astype(BF16)
            prob_row[part * p : part * (p + 1), :] = jnp.sum(
                jnp.where(hit, prob[p : p + 1, :], 0.0), axis=1, keepdims=True
            )
            r = lax.broadcasted_iota(jnp.int32, (rows, slot_own.shape[1]), 0)
            hot_sib[p] = jnp.where(slot_sib[p : p + 1, :] == r, 1.0, 0.0).astype(BF16)
        gate[...] = jnp.zeros_like(gate)
        up[...] = jnp.zeros_like(up)
        dh[...] = jnp.zeros_like(dh)

    @pl.when(t < half)
    def _():
        blocks = ((o0[0], o0[1]), (o1[0], o1[1]), (o2[0], o2[1]), (ox[...], oy[...]))
        for p, (bx, by) in enumerate(blocks):
            xs[part * p : part * (p + 1), :] = dot(hot_own[p], bx)
            ys[part * p : part * (p + 1), :] = dot(hot_own[p], by)

    @pl.when(t >= half)
    def _():
        blocks = ((s0[0], s0[1]), (s1[0], s1[1]), (s2[0], s2[1]), (sx[...], sy[...]))
        ax = ay = None
        for p, (bx, by) in enumerate(blocks):
            dx, dy = dot(hot_sib[p], bx), dot(hot_sib[p], by)
            ax, ay = (dx, dy) if ax is None else (ax + dx, ay + dy)
        xs[...] = ax
        ys[...] = ay

    xg = xs[...].astype(BF16)
    yg = (ys[...] * prob_row[...]).astype(BF16)
    gate[...] += dot(xg, wg[...])
    up[...] += dot(xg, wu[...])
    dh[...] += dot(yg, wd[...], NT)
    per_group = 2 * half // 4
    rel = tile_of(t, core, half) - grp * per_group

    @pl.when((rel >= 0) & (rel < per_group))
    def _():
        at = pl.ds(pl.multiple_of(rel * width, width), width)
        xi_ref[:, at] = xg
        yi_ref[:, at] = yg

    @pl.when(t == 2 * half - 1)
    def _():
        ff = gate.shape[1]
        g, u, d = gate[...], up[...], dh[...]
        s = jax.nn.sigmoid(g)
        sg = g * s
        h_ref[:, 0:ff] = (d * u * s * (1.0 + g * (1.0 - s))).astype(BF16)
        h_ref[:, ff : 2 * ff] = (d * sg).astype(BF16)
        h_ref[:, 2 * ff :] = (sg * u).astype(BF16)


def forward(place, slot_own, slot_sib, prob, own, sib, wg, wu, wd, rows, cap):
    width, ff = wg.shape
    half = 4
    tile = width // (2 * half)
    toks = slot_own.shape[1]

    def own_t(t):
        return jnp.minimum(t, half - 1)

    def sib_t(t):
        return jnp.maximum(t - half, 0)

    full = lambda a: pl.BlockSpec(a.shape, lambda t, s: (0,) * a.ndim)
    big_own = pl.BlockSpec((2, toks, tile), lambda t, s: (0, 0, own_t(t)))
    one_own = pl.BlockSpec((toks, tile), lambda t, s: (0, own_t(t)))
    big_sib = pl.BlockSpec((2, toks, tile), lambda t, s: (0, 0, sib_t(t)))
    one_sib = pl.BlockSpec((toks, tile), lambda t, s: (0, sib_t(t)))
    w_in = pl.BlockSpec((tile, ff), lambda t, s: (tile_of(t, s[0], half), 0))
    w_out = pl.BlockSpec((ff, tile), lambda t, s: (0, tile_of(t, s[0], half)))
    flops = 2 * rows * width * ff * 3 + 2 * rows * 4 * toks * width * 2
    return pl.pallas_call(
        functools.partial(forward_kernel, half=half, cap=cap),
        grid_spec=pltpu.PrefetchScalarGridSpec(
            num_scalar_prefetch=1,
            grid=(2 * half,),
            in_specs=[full(slot_own), full(slot_sib), full(prob)]
            + [big_own] * 3 + [one_own] * 2 + [big_sib] * 3 + [one_sib] * 2
            + [w_in, w_in, w_out],
            out_specs=[
                pl.BlockSpec((rows, 3 * ff), lambda t, s: (0, 0)),
                pl.BlockSpec((rows, width // 4), lambda t, s: (0, 0)),
                pl.BlockSpec((rows, width // 4), lambda t, s: (0, 0)),
            ],
            scratch_shapes=[
                pltpu.VMEM((4, rows // 4, toks), BF16),
                pltpu.VMEM((4, rows, toks), BF16),
                pltpu.VMEM((rows, 1), F32),
                pltpu.VMEM((rows, tile), F32),
                pltpu.VMEM((rows, tile), F32),
                pltpu.VMEM((rows, ff), F32),
                pltpu.VMEM((rows, ff), F32),
                pltpu.VMEM((rows, ff), F32),
            ],
        ),
        out_shape=[
            jax.ShapeDtypeStruct((rows, 3 * ff), BF16),
            jax.ShapeDtypeStruct((rows, width // 4), BF16),
            jax.ShapeDtypeStruct((rows, width // 4), BF16),
        ],
        compiler_params=pltpu.CompilerParams(vmem_limit_bytes=36 * 2**20),
        cost_estimate=pl.CostEstimate(
            flops=flops, bytes_accessed=3 * 2 * width * ff + 16 * toks * width, transcendentals=0
        ),
        name="forward",
    )(place, slot_own, slot_sib, prob, *own, *sib, wg, wu, wd)


def rowgrad_kernel(place, slot_own, slot_sib, h, wg, wu, own_ref, sib_ref, hot_own, hot_sib, *, half):
    t = pl.program_id(0)
    rows, ff = h.shape[0], h.shape[1] // 2
    toks = slot_own.shape[1]

    @pl.when(t == 0)
    def _():
        for p in range(4):
            r = lax.broadcasted_iota(jnp.int32, (toks, rows), 1)
            hot_own[p] = jnp.where(slot_own[p] == r, 1.0, 0.0).astype(BF16)
            hot_sib[p] = jnp.where(slot_sib[p] == r, 1.0, 0.0).astype(BF16)

    grad = dot(h[:, 0:ff], wg[...], NT) + dot(h[:, ff:], wu[...], NT)
    grad = grad.astype(BF16)

    @pl.when(t < half)
    def _():
        for p in range(4):
            own_ref[p] = dot(hot_own[p], grad).astype(BF16)

    @pl.when(t >= half)
    def _():
        for p in range(4):
            sib_ref[p] = dot(hot_sib[p], grad).astype(BF16)


def rowgrad(place, slot_own, slot_sib, h, wg, wu):
    width, ff = wg.shape
    rows = h.shape[0]
    half = 4
    tile = width // (2 * half)
    toks = slot_own.shape[1]
    full = lambda a: pl.BlockSpec(a.shape, lambda t, s: (0,) * a.ndim)
    w_in = pl.BlockSpec((tile, ff), lambda t, s: (tile_of(t, s[0], half), 0))
    shape = jax.ShapeDtypeStruct((4, toks, width // 2), BF16)
    return pl.pallas_call(
        functools.partial(rowgrad_kernel, half=half),
        grid_spec=pltpu.PrefetchScalarGridSpec(
            num_scalar_prefetch=1,
            grid=(2 * half,),
            in_specs=[
                full(slot_own), full(slot_sib),
                pl.BlockSpec((rows, 2 * ff), lambda t, s: (0, 0)), w_in, w_in,
            ],
            out_specs=[
                pl.BlockSpec((4, toks, tile), lambda t, s: (0, 0, jnp.minimum(t, half - 1))),
                pl.BlockSpec((4, toks, tile), lambda t, s: (0, 0, jnp.maximum(t - half, 0))),
            ],
            scratch_shapes=[
                pltpu.VMEM((4, toks, rows), BF16),
                pltpu.VMEM((4, toks, rows), BF16),
            ],
        ),
        out_shape=[shape, shape],
        compiler_params=pltpu.CompilerParams(vmem_limit_bytes=36 * 2**20),
        cost_estimate=pl.CostEstimate(
            flops=2 * rows * width * ff * 2 + 2 * rows * 4 * toks * width,
            bytes_accessed=2 * 2 * width * ff + 8 * toks * width,
            transcendentals=0,
        ),
        name="rowgrad",
    )(place, slot_own, slot_sib, h, wg, wu)


def weight_kernel(
    place, slot_own, slot_sib, prob, xi0, yi0, xi1, yi1, h0, h1,
    o0, o1, o2, ox, oy, s0, s1, s2, sx, sy,
    gate_ref, up_ref, down_ref, xs, ys, prob_row, acc_g, acc_u, acc_d,
):
    s = pl.program_id(0)
    core = place[0]
    rows = xi0.shape[0]
    part = rows // 4
    toks = slot_own.shape[-1]
    wide = o0.shape[-1]
    ff = acc_g.shape[1]

    @pl.when(s == 0)
    def _():
        xs[0:rows] = xi0[...]
        xs[rows:] = xi1[...]
        ys[0:rows] = yi0[...]
        ys[rows:] = yi1[...]

    @pl.when(s > 0)
    def _():
        mine = pl.ds(pl.multiple_of(core * wide, wide), wide)
        other = pl.ds(pl.multiple_of((1 - core) * wide, wide), wide)
        for k in range(2):
            base = k * rows
            own = ((o0[0, k, 0], o0[1, k, 0]), (o1[0, k, 0], o1[1, k, 0]), (o2[0, k, 0], o2[1, k, 0]), (ox[k, 0], oy[k, 0]))
            sib = ((s0[0, k, 0], s0[1, k, 0]), (s1[0, k, 0], s1[1, k, 0]), (s2[0, k, 0], s2[1, k, 0]), (sx[k, 0], sy[k, 0]))
            gx, gy, scale = [], [], []
            ax = ay = None
            for p in range(4):
                r = lax.broadcasted_iota(jnp.int32, (part, toks), 0) + part * p
                hit = slot_own[0, k, p : p + 1, :] == r
                scale.append(jnp.sum(jnp.where(hit, prob[0, k, p : p + 1, :], 0.0), axis=1, keepdims=True))
                hot = jnp.where(hit, 1.0, 0.0).astype(BF16)
                gx.append(dot(hot, own[p][0]))
                gy.append(dot(hot, own[p][1]))
                r = lax.broadcasted_iota(jnp.int32, (rows, toks), 0)
                hot = jnp.where(slot_sib[0, k, p : p + 1, :] == r, 1.0, 0.0).astype(BF16)
                dx, dy = dot(hot, sib[p][0]), dot(hot, sib[p][1])
                ax, ay = (dx, dy) if ax is None else (ax + dx, ay + dy)
            for p in range(4):
                prob_row[part * p : part * (p + 1), :] = scale[p]
            scaled = prob_row[...]
            at = slice(base, base + rows)
            xs[at, mine] = jnp.concatenate(gx, axis=0).astype(BF16)
            xs[at, other] = ax.astype(BF16)
            ys[at, mine] = (jnp.concatenate(gy, axis=0) * scaled).astype(BF16)
            ys[at, other] = (ay * scaled).astype(BF16)

    x0, x1 = xs[0:rows], xs[rows:]
    y0, y1 = ys[0:rows], ys[rows:]
    add_g = dot(x0, h0[0, :, 0:ff], TN) + dot(x1, h1[0, :, 0:ff], TN)
    add_u = dot(x0, h0[0, :, ff : 2 * ff], TN) + dot(x1, h1[0, :, ff : 2 * ff], TN)
    add_d = dot(h0[0, :, 2 * ff :], y0, TN) + dot(h1[0, :, 2 * ff :], y1, TN)

    @pl.when(s == 0)
    def _():
        acc_g[...] = add_g
        acc_u[...] = add_u
        acc_d[...] = add_d

    @pl.when((s > 0) & (s < 3))
    def _():
        acc_g[...] += add_g
        acc_u[...] += add_u
        acc_d[...] += add_d

    @pl.when(s == 3)
    def _():
        gate_ref[...] = (acc_g[...] + add_g).astype(BF16)
        up_ref[...] = (acc_u[...] + add_u).astype(BF16)
        down_ref[...] = (acc_d[...] + add_d).astype(BF16)


def weights(place, slot_own, slot_sib, prob, xi, yi, hs, own, sib, ff):
    rows, wide = xi[0].shape
    toks = slot_own.shape[-1]
    cols = wide // 2
    full = lambda a: pl.BlockSpec(a.shape, lambda s, q: (0,) * a.ndim)
    meta = pl.BlockSpec((1, 2, 4, toks), lambda s, q: (s, 0, 0, 0))
    h_spec = pl.BlockSpec((1, rows, 3 * ff), lambda s, q: (lax.rem(q[1] + s, 4), 0, 0))
    big = pl.BlockSpec((2, 2, 1, toks, cols), lambda s, q: (0, 0, jnp.maximum(s - 1, 0), 0, 0))
    one = pl.BlockSpec((2, 1, toks, cols), lambda s, q: (0, jnp.maximum(s - 1, 0), 0, 0))
    return pl.pallas_call(
        weight_kernel,
        grid_spec=pltpu.PrefetchScalarGridSpec(
            num_scalar_prefetch=1,
            grid=(4,),
            in_specs=[meta, meta, meta] + [full(xi[0])] * 4 + [h_spec, h_spec]
            + [big] * 3 + [one] * 2 + [big] * 3 + [one] * 2,
            out_specs=[
                pl.BlockSpec((wide, ff), lambda s, q: (0, 0)),
                pl.BlockSpec((wide, ff), lambda s, q: (0, 0)),
                pl.BlockSpec((ff, wide), lambda s, q: (0, 0)),
            ],
            scratch_shapes=[
                pltpu.VMEM((2 * rows, wide), BF16),
                pltpu.VMEM((2 * rows, wide), BF16),
                pltpu.VMEM((rows, 1), F32),
                pltpu.VMEM((wide, ff), F32),
                pltpu.VMEM((wide, ff), F32),
                pltpu.VMEM((ff, wide), F32),
            ],
        ),
        out_shape=[
            jax.ShapeDtypeStruct((wide, ff), BF16),
            jax.ShapeDtypeStruct((wide, ff), BF16),
            jax.ShapeDtypeStruct((ff, wide), BF16),
        ],
        compiler_params=pltpu.CompilerParams(vmem_limit_bytes=52 * 2**20),
        cost_estimate=pl.CostEstimate(
            flops=2 * 8 * rows * wide * ff * 3 + 2 * 6 * rows * 4 * toks * wide * 2,
            bytes_accessed=8 * rows * 3 * ff * 2 + 24 * 4 * toks * wide,
            transcendentals=0,
        ),
        name="weight_grads",
    )(place, slot_own, slot_sib, prob, xi[0], yi[0], xi[1], yi[1], hs[0], hs[1], *own, *sib)


def on_device(tokens, out_grad, expert_ids, route_probs, w_gate, w_up, w_down):
    toks, width = tokens.shape
    topk = expert_ids.shape[1]
    groups = lax.axis_size("expert")
    cap = 3 * toks * topk // (2 * groups)
    wg, wu, wd = w_gate[0], w_up[0], w_down[0]
    ff = wg.shape[1]
    rows = 16 * cap
    grp = lax.axis_index("dp")
    expert = lax.axis_index("expert")
    z, x, core = expert // 8, (expert // 2) % 4, expert % 2
    first = core == 0
    place = jnp.stack([core, grp]).astype(jnp.int32)

    meta = jnp.concatenate([expert_ids.T.astype(F32), route_probs.T], axis=0)
    meta = lax.all_gather(meta, ("dp", "expert"))
    hit = meta[:, :topk, :] == expert.astype(F32)
    chosen = jnp.any(hit, axis=1)
    prob = jnp.sum(jnp.where(hit, meta[:, topk:, :], 0.0), axis=1)
    lower = jnp.triu(jnp.ones((toks, toks), BF16), 1)
    rank = dot(chosen.astype(BF16), lower).astype(jnp.int32)
    rank = jnp.where(chosen, rank, -(10**6))
    offs = jnp.array(OFFSETS, jnp.int32)
    r2, r1 = offs[:, None], offs[None, :]
    bz = jnp.where(first, z + r1, z + r2) % 4
    bx = jnp.where(first, x + r2, x + r1) % 4
    chip = (bz * 8 + bx * 2).reshape(16)
    dev = (
        ((grp + jnp.arange(4)) % 4)[:, None, None] * 32
        + jnp.arange(2)[None, :, None]
        + chip[None, None, :]
    )
    rank = rank[dev]
    prob = prob[dev].reshape(4, 2, 4, 4 * toks)
    slot = rank + cap * jnp.arange(16, dtype=jnp.int32)[:, None]
    slot_sib = slot.reshape(4, 2, 4, 4, toks).swapaxes(2, 3).reshape(4, 2, 4, 4 * toks)
    slot = slot.reshape(4, 2, 4, 4 * toks)

    both = jnp.stack([tokens, out_grad])

    def by_core(v):
        half = v.shape[-1] // 2
        mine = lax.dynamic_slice_in_dim(v, core * half, half, v.ndim - 1)
        other = lax.dynamic_slice_in_dim(v, (1 - core) * half, half, v.ndim - 1)
        got = swap_core(other)
        return jnp.where(first, mine, got), jnp.where(first, got, mine)

    chunks = by_core(both)

    quarter = width // 4
    other_groups = []
    for g in (1, 2, 3):
        r = 4 - g
        part = lax.dynamic_slice_in_dim(both, ((grp + r) % 4) * quarter, quarter, 2)
        other_groups.append(lax.ppermute(part, "dp", [(s, (s + r) % 4) for s in range(4)]))
    cols = jnp.stack(by_core(jnp.stack(other_groups, axis=1)), axis=1)

    hs, xi, yi, partial = [], [], [], []
    for k in range(2):
        own = plane_gather(chunks[k])
        sib = tuple(swap_core(p) for p in own)
        h, xk, yk = forward(place, slot[0, k], slot_sib[0, k], prob[0, k], own, sib, wg, wu, wd, rows, cap)
        hs.append(lax.all_gather(h, "dp"))
        xi.append(xk)
        yi.append(yk)
        partial.append(rowgrad(place, slot[0, k][..., None], slot_sib[0, k][..., None], h, wg, wu))

    own_c = plane_gather(cols)
    sib_c = tuple(swap_core(p) for p in own_c)

    sums = []
    for mine, other in partial:
        got = swap_core(other)
        total = (mine.astype(F32) + got.astype(F32)).astype(BF16)
        total = ring_reduce([total[p] for p in range(4)], 2).astype(BF16)
        total = total.reshape(4, toks, -1)
        sums.append(ring_reduce([total[p] for p in range(4)], 1).astype(BF16))
    keep = jnp.where(first, sums[0], sums[1])
    got = swap_core(jnp.where(first, sums[1], sums[0]))
    token_grad = jnp.concatenate([jnp.where(first, keep, got), jnp.where(first, got, keep)], axis=1)

    gate_grad, up_grad, down_grad = weights(
        place, slot, slot_sib, prob, xi, yi, hs, own_c, sib_c, ff
    )
    return token_grad, gate_grad[None], up_grad[None], down_grad[None]


def solution(mesh):
    in_specs = (
        P(("dp", "expert"), None),
        P(("dp", "expert"), None),
        P(("dp", "expert"), None),
        P(("dp", "expert"), None),
        P("expert", None, None),
        P("expert", None, None),
        P("expert", None, None),
    )
    out_specs = (
        P(("dp", "expert"), None),
        P("expert", "dp", None),
        P("expert", "dp", None),
        P("expert", None, "dp"),
    )
    return jax.shard_map(
        on_device, mesh=mesh, in_specs=in_specs, out_specs=out_specs, check_vma=False
    )
```

time: 603 us -> 419 us (0.69)
  waiting for transfers between devices: 360 us -> 128 us
  Pallas kernels: 0 us -> 99.4 us
  matrix products: 61.2 us -> 0.19 us
  starting transfers between devices: 30 us -> 74.6 us
  local copies, waits for them, and re-layouts: 79.1 us -> 34.7 us
  blocking collectives: 0 us -> 38.4 us
  other arithmetic: 50.5 us -> 19.9 us
    reduce_scatter x1 -> x0, waiting for transfers between devices: 192 us -> none  [on_device(): lax.psum_scatter(jnp.concatenate([contract(flat_x, flat_dg), contract(fla...]
    all_to_all x3 -> x0, waiting for transfers between devices: 168 us -> none  [the longest x1 72.8 us: on_device(): lax.all_to_all(row_grad, 'expert', split_axis=0, concat_axis=0, tiled=True)]
    ppermute x0 -> x63, waiting for transfers between devices: none -> 128 us  [the longest x40 108 us: step(): return lax.ppermute(v, 'expert', expert_pairs(ring, shift))]
    pallas_call x0 -> x5, Pallas kernels: none -> 99.4 us  [the longest x1 36.2 us: weights(): pl.pallas_call(weight_kernel, grid_spec=pltpu.PrefetchScalarGridSpec(num_...]
    ppermute x0 -> x63, starting transfers between devices: none -> 74.5 us  [the longest x40 42.7 us: step(): return lax.ppermute(v, 'expert', expert_pairs(ring, shift))]
    dot_general x8 -> x1, matrix products: 61.2 us -> 0.19 us  [dot(): return lax.dot_general(a, b, dims, preferred_element_type=F32)]
    all_gather x0 -> x1, blocking collectives: none -> 38.4 us  [on_device(): meta = lax.all_gather(meta, ('dp', 'expert'))]
    reshape x6 -> x2, local copies, waits for them, and re-layouts: 31.5 us -> 0.19 us  [the longest x1 0.1 us: on_device(): slot.reshape(4, 2, 4, 4, toks).swapaxes(2, 3).reshape(4, 2, 4, 4 * toks)]
  transfers between devices with their start and end apart: 4 -> 65, of which waited for: 4 -> 26; matrix products, arithmetic and copies ran while one was open for 16% -> 9% of each run, Pallas kernels for 0% -> 15%
where the time goes in v1:
time: 419 us; the launch traced here: 411 us
  waiting for transfers between devices  128 us (31%)
  Pallas kernels  99.4 us (24%)
  starting transfers between devices  74.6 us (18%)
  blocking collectives  38.4 us (9%)
  local copies, waits for them, and re-layouts  34.7 us (8%)
  other arithmetic  19.9 us (5%)
  between operations  15.4 us (4%)
    ppermute x40, waiting for transfers between devices, step(): return lax.ppermute(v, 'expert', expert_pairs(ring, shift))  108 us
    ppermute x40, starting transfers between devices, step(): return lax.ppermute(v, 'expert', expert_pairs(ring, shift))  42.7 us
    all_gather x1, blocking collectives, on_device(): meta = lax.all_gather(meta, ('dp', 'expert'))  38.4 us
    pallas_call x1, Pallas kernels, weights(): pl.pallas_call(weight_kernel, grid_spec=pltpu.PrefetchScalarGridSpec(num_...  36.2 us
    pallas_call x2, Pallas kernels, forward(): pl.pallas_call(functools.partial(forward_kernel, half=half, cap=cap), gri...  36.1 us
    ppermute x20, starting transfers between devices, swap_core(): return lax.ppermute(v, 'expert', [(e, e ^ 1) for e in range(32)])  27.6 us
    pallas_call x2, Pallas kernels, rowgrad(): pl.pallas_call(functools.partial(rowgrad_kernel, half=half), grid_spec=pl...  27.1 us
    ppermute x3, waiting for transfers between devices, on_device(): lax.ppermute(part, 'dp', [(s, (s + r) % 4) for s in range(4)])  16.6 us
  transfers between devices with their start and end apart: 65, of which 26 were waited for; matrix products, arithmetic and copies ran while one was open for 9% of the time, Pallas kernels for 15%

profile of v1, /device:TPU:1, one launch (start us, length us, event | category | flops | bytes accessed | tf_op | source)
XLA Modules:
  0.0 410.5 jit_solution(3647201833384718220)
XLA Ops:
  13.3 2.6 collective-permute-start.2
  15.9 38.4 %all-gather = f32[2048,48]{1,0:T(8,128)S(1)} all-gather(f32[16,48]{1,0:T(8,128)S(1)} %pad_maximum_fusion.11), channel_id=2, replica_groups=mesh['dp'=4,'expert'=32] {'dp','expert'}, dimensions={0}, use_global_device_ids=true | all-gather | bytes 396288 | tf_op jit(solution)/shard_map/all_gather | solution.py:405
  57.1 5.4 %collective-permute-done.1 = bf16[2,48,2048]{2,1,0:T(8,128)(2,1)S(1)} collective-permute-done((bf16[2,48,2048]{2,1,0:T(8,128)(2,1)S(1)}, bf16[2,48,2048]{2,1,0:T(8,128)(2,1)S(1)}, u32[]{:S(2)}, u32[]{:S(2)}) %collective-permute-start.1) | collective-permute-done | bytes 393248 | tf_op jit(solution)/shard_map/ppermute | solution.py:35
  63.2 5.5 %collective-permute-done.3 = bf16[48,2048]{1,0:T(8,128)(2,1)S(1)} collective-permute-done((bf16[48,2048]{1,0:T(8,128)(2,1)S(1)}, bf16[48,2048]{1,0:T(8,128)(2,1)S(1)}, u32[]{:S(2)}, u32[]{:S(2)}) %collective-permute-start.3) | collective-permute-done | bytes 196640 | tf_op jit(solution)/shard_map/ppermute | solution.py:35
  69.2 2.7 collective-permute-start.6
  73.2 2.5 collective-permute-start.9
  75.6 14.0 %collective-permute-done.5.o1 = bf16[2,192,2048]{2,1,0:T(8,128)(2,1)S(1)} collective-permute-done((bf16[2,192,2048]{2,1,0:T(8,128)(2,1)S(1)}, bf16[2,192,2048]{2,1,0:T(8,128)(2,1)S(1)}, u32[]{:S(2)}, u32[]{:S(2)}) %collective-permute-start.5) | collective-permute-done | bytes 1572896 | tf_op jit(solution)/shard_map/ppermute | solution.py:35
  90.6 2.8 collective-permute-done.6.o2
  95.5 3.2 collective-permute-start.8
  98.7 2.5 collective-permute-start.10
  103.7 3.1 collective-permute-start.12
  108.0 3.1 collective-permute-start.13
  112.8 3.9 collective-permute-start.26
  116.7 18.4 %forward.2 = (bf16[288,2304]{1,0:T(8,128)(2,1)}, bf16[288,1024]{1,0:T(8,128)(2,1)S(1)}, bf16[288,1024]{1,0:T(8,128)(2,1)S(1)}) custom-call(s32[2]{0:T(128)S(1)} %pad_add_fusion.place, s32[4,192]{1,0:T(4,128)S(1)} %get-tuple-element.73.slot_own, s32[4,192]{1,0:T(4,128)S(1)} %get-tuple-element.69.slot_sib, f32[4,192]{1,0:T(4,128)S(1)} %get-tuple-element.67.prob, ...), custom_call_target="tpu_custom_call" | custom-call | flops 9059696640 | bytes 31457280 | tf_op jit(solution)/shard_map/forward/pallas_call | solution.py:169
  137.9 6.0 %collective-permute-done.25 = bf16[48,2048]{1,0:T(8,128)(2,1)S(1)} collective-permute-done((bf16[48,2048]{1,0:T(8,128)(2,1)S(1)}, bf16[48,2048]{1,0:T(8,128)(2,1)S(1)}, u32[]{:S(2)}, u32[]{:S(2)}) %collective-permute-start.25) | collective-permute-done | bytes 196640 | tf_op jit(solution)/shard_map/ppermute | solution.py:35
  143.9 2.7 maximum_maximum_fusion.2.o0
  146.7 2.7 collective-permute-start.28
  150.1 2.4 collective-permute-start.47
  153.5 7.7 %collective-permute-done.48 = bf16[2,48,1024]{2,1,0:T(8,128)(2,1)S(1)} collective-permute-done((bf16[2,48,1024]{2,1,0:T(8,128)(2,1)S(1)}, bf16[2,48,1024]{2,1,0:T(8,128)(2,1)S(1)}, u32[]{:S(2)}, u32[]{:S(2)}) %collective-permute-start.48) | collective-permute-done | bytes 196640 | tf_op jit(solution)/shard_map/ppermute | solution.py:444
  161.2 8.7 %collective-permute-done.47 = bf16[2,48,1024]{2,1,0:T(8,128)(2,1)S(1)} collective-permute-done((bf16[2,48,1024]{2,1,0:T(8,128)(2,1)S(1)}, bf16[2,48,1024]{2,1,0:T(8,128)(2,1)S(1)}, u32[]{:S(2)}, u32[]{:S(2)}) %collective-permute-start.47) | collective-permute-done | bytes 196640 | tf_op jit(solution)/shard_map/ppermute | solution.py:444
  170.2 2.7 collective-permute-start.49
  175.6 2.7 collective-permute-start.30
  182.3 4.5 %collective-permute-done.29.ox = bf16[192,2048]{1,0:T(8,128)(2,1)} collective-permute-done((bf16[192,2048]{1,0:T(8,128)(2,1)S(1)}, bf16[192,2048]{1,0:T(8,128)(2,1)}, u32[]{:S(2)}, u32[]{:S(2)}) %collective-permute-start.29) | collective-permute-done | bytes 786464 | tf_op jit(solution)/shard_map/ppermute | solution.py:35
  190.9 2.8 copy-done.13
  193.7 13.6 %rowgrad.2 = (bf16[4,192,2048]{2,1,0:T(8,128)(2,1)S(1)}, bf16[4,192,2048]{2,1,0:T(8,128)(2,1)}) custom-call(s32[2]{0:T(128)S(1)} %pad_add_fusion.place, s32[4,192,1]{2,1,0:T(8,128)S(1)} %copy-done.5, s32[4,192,1]{2,1,0:T(8,128)S(1)} %copy-done.6, bf16[288,2304]{1,0:T(8,128)(2,1)} %get-tuple-element.17.h, bf16[4096,768]{1,0:T(8,128)(2,1)S(1)} %bitcast.114, ...), custom_call_target="tpu_custom_call" | custom-call | flops 5435817984 | bytes 18874368 | tf_op jit(solution)/shard_map/rowgrad/pallas_call | solution.py:241
  208.3 3.7 collective-permute-start.51
  211.9 17.7 %forward.3 = (bf16[288,2304]{1,0:T(8,128)(2,1)S(1)}, bf16[288,1024]{1,0:T(8,128)(2,1)S(1)}, bf16[288,1024]{1,0:T(8,128)(2,1)S(1)}) custom-call(s32[2]{0:T(128)S(1)} %pad_add_fusion.place, s32[4,192]{1,0:T(4,128)S(1)} %get-tuple-element.72.slot_own, s32[4,192]{1,0:T(4,128)S(1)} %get-tuple-element.68.slot_sib, f32[4,192]{1,0:T(4,128)S(1)} %get-tuple-element.66.prob, ...), custom_call_target="tpu_custom_call" | custom-call | flops 9059696640 | bytes 31457280 | tf_op jit(solution)/shard_map/forward/pallas_call | solution.py:169
  234.7 2.8 copy-done.14
  237.4 13.5 %rowgrad.3 = (bf16[4,192,2048]{2,1,0:T(8,128)(2,1)S(1)}, bf16[4,192,2048]{2,1,0:T(8,128)(2,1)}) custom-call(s32[2]{0:T(128)S(1)} %pad_add_fusion.place, s32[4,192,1]{2,1,0:T(8,128)S(1)} %copy.38.slot_own, s32[4,192,1]{2,1,0:T(8,128)S(1)} %copy-done.4, bf16[288,2304]{1,0:T(8,128)(2,1)S(1)} %copy-done.3, bf16[4096,768]{1,0:T(8,128)(2,1)S(1)} %bitcast.115, ...), custom_call_target="tpu_custom_call" | custom-call | flops 5435817984 | bytes 18874368 | tf_op jit(solution)/shard_map/rowgrad/pallas_call | solution.py:241
  252.1 2.5 collective-permute-start.53
  254.6 6.7 %collective-permute-done.50 = bf16[2,2,3,48,512]{4,3,2,1,0:T(8,128)(2,1)S(1)} collective-permute-done((bf16[2,2,3,48,512]{4,3,2,1,0:T(8,128)(2,1)}, bf16[2,2,3,48,512]{4,3,2,1,0:T(8,128)(2,1)S(1)}, u32[]{:S(2)}, u32[]{:S(2)}) %collective-permute-start.50) | collective-permute-done | bytes 589856 | tf_op jit(solution)/shard_map/ppermute | solution.py:35
  261.5 7.1 %collective-permute-done.52 = bf16[2,3,48,512]{3,2,1,0:T(8,128)(2,1)S(1)} collective-permute-done((bf16[2,3,48,512]{3,2,1,0:T(8,128)(2,1)S(1)}, bf16[2,3,48,512]{3,2,1,0:T(8,128)(2,1)S(1)}, u32[]{:S(2)}, u32[]{:S(2)}) %collective-permute-start.52) | collective-permute-done | bytes 294944 | tf_op jit(solution)/shard_map/ppermute | solution.py:35
  268.5 2.9 maximum_maximum_fusion.o0
  271.5 2.7 collective-permute-start.55
  274.2 2.8 add_convert_fusion.1
  277.5 2.7 collective-permute-start.15
  280.2 3.3 add_convert_fusion
  284.0 21.2 %collective-permute-done.17 = bf16[192,1024]{1,0:T(8,128)(2,1)S(1)} collective-permute-done((bf16[192,1024]{1,0:T(8,128)(2,1)S(1)}, bf16[192,1024]{1,0:T(8,128)(2,1)S(1)}, u32[]{:S(2)}, u32[]{:S(2)}) %collective-permute-start.17) | collective-permute-done | bytes 393248 | tf_op jit(solution)/shard_map/ppermute | solution.py:35
  307.1 2.3 collective-permute-done.39
  309.8 2.4 collective-permute-done.37
  312.4 2.7 collective-permute-start.38
  318.2 2.7 collective-permute-done.16
  321.4 4.9 %collective-permute-done.40 = bf16[192,2048]{1,0:T(8,128)(2,1)S(1)} collective-permute-done((bf16[192,2048]{1,0:T(8,128)(2,1)S(1)}, bf16[192,2048]{1,0:T(8,128)(2,1)S(1)}, u32[]{:S(2)}, u32[]{:S(2)}) %collective-permute-start.40) | collective-permute-done | bytes 786464 | tf_op jit(solution)/shard_map/ppermute | solution.py:35
  326.4 3.6 collective-permute-done.38
  337.0 2.6 collective-permute-start.42
  341.1 5.3 %collective-permute-start.58 = (bf16[2,2,3,192,512]{4,3,2,1,0:T(8,128)(2,1)}, bf16[2,2,3,192,512]{4,3,2,1,0:T(8,128)(2,1)}, u32[]{:S(2)}, u32[]{:S(2)}) collective-permute-start(bf16[2,2,3,192,512]{4,3,2,1,0:T(8,128)(2,1)} %maximum_maximum_fusion.o0), channel_id=1, source_target_pairs={{0,1},{1,0},{2,3},{3,2},{4,5},{5,4},{6,7},{7,6},{8,9},{9,8},{10,11... | collective-permute-start | bytes 7077896 | tf_op jit(solution)/shard_map/ppermute | solution.py:39
  349.2 12.5 %collective-permute-done.57.oy = bf16[2,3,192,512]{3,2,1,0:T(8,128)(2,1)S(1)} collective-permute-done((bf16[2,3,192,512]{3,2,1,0:T(8,128)(2,1)S(1)}, bf16[2,3,192,512]{3,2,1,0:T(8,128)(2,1)S(1)}, u32[]{:S(2)}, u32[]{:S(2)}) %collective-permute-start.57) | collective-permute-done | bytes 1179680 | tf_op jit(solution)/shard_map/ppermute | solution.py:35
  367.0 36.2 %weight_grads.1 = (bf16[1024,768]{1,0:T(8,128)(2,1)}, bf16[1024,768]{1,0:T(8,128)(2,1)}, bf16[768,1024]{1,0:T(8,128)(2,1)}) custom-call(s32[2]{0:T(128)S(1)} %pad_add_fusion.place, s32[4,2,4,192]{3,2,1,0:T(4,128)S(1)} %bitcast.111, s32[4,2,4,192]{3,2,1,0:T(4,128)S(1)} %copy-done.8, f32[4,2,4,192]{3,2,1,0:T(4,128)S(1)} %copy-done.10, ...), custom_call_target="tpu_custom_call" | custom-call | flops 16307453952 | bytes 29491200 | tf_op jit(solution)/shard_map/weight_grads/pallas_call | solution.py:354
  (252 shorter events, 66.0 us)
Async XLA Ops:
  7.2 359.8 %all-gather.6.cloned.1.call-start = ((), (), s32[]{:S(2)}) async-start(), calls=%async_computation | async-start | bytes 6635520 | tf_op jit(solution)/shard_map/all_gather | solution.py:452
  13.3 41.7 %collective-permute-start.2 = (bf16[2,48,2048]{2,1,0:T(8,128)(2,1)S(1)}, bf16[2,48,2048]{2,1,0:T(8,128)(2,1)S(1)}, u32[]{:S(2)}, u32[]{:S(2)}) collective-permute-start(bf16[2,48,2048]{2,1,0:T(8,128)(2,1)S(1)} %get-tuple-element.42), channel_id=1, source_target_pairs={{0,24},{1,7},{2,26},{3,1},{4,28},{5,3},{6,30},{7,5},{8,0},{9,15},{... | collective-permute-start | bytes 1179656 | tf_op jit(solution)/shard_map/ppermute | solution.py:35
  68.8 20.8 %collective-permute-start.5 = (bf16[2,192,2048]{2,1,0:T(8,128)(2,1)S(1)}, bf16[2,192,2048]{2,1,0:T(8,128)(2,1)S(1)}, u32[]{:S(2)}, u32[]{:S(2)}) collective-permute-start(bf16[2,192,2048]{2,1,0:T(8,128)(2,1)S(1)} %maximum_maximum_fusion.1.o0), channel_id=1, source_target_pairs={{0,2},{1,9},{2,4},{3,11},{4,6},{5,13},{6,0},{7,15},{8,10},{9,17},{... | collective-permute-start | bytes 4718600 | tf_op jit(solution)/shard_map/ppermute | solution.py:35
  69.2 24.2 %collective-permute-start.6 = (bf16[2,192,2048]{2,1,0:T(8,128)(2,1)S(1)}, bf16[2,192,2048]{2,1,0:T(8,128)(2,1)}, u32[]{:S(2)}, u32[]{:S(2)}) collective-permute-start(bf16[2,192,2048]{2,1,0:T(8,128)(2,1)S(1)} %maximum_maximum_fusion.1.o0), channel_id=1, source_target_pairs={{0,6},{1,25},{2,0},{3,27},{4,2},{5,29},{6,4},{7,31},{8,14},{9,1},{... | collective-permute-start | bytes 4718600 | tf_op jit(solution)/shard_map/ppermute | solution.py:35
  73.1 28.1 %collective-permute-start.24 = (bf16[2,48,2048]{2,1,0:T(8,128)(2,1)}, bf16[2,48,2048]{2,1,0:T(8,128)(2,1)}, u32[]{:S(2)}, u32[]{:S(2)}) collective-permute-start(bf16[2,48,2048]{2,1,0:T(8,128)(2,1)} %get-tuple-element.41), channel_id=1, source_target_pairs={{0,24},{1,7},{2,26},{3,1},{4,28},{5,3},{6,30},{7,5},{8,0},{9,15},{... | collective-permute-start | bytes 1179656 | tf_op jit(solution)/shard_map/ppermute | solution.py:35
  73.2 39.6 %collective-permute-start.9 = (bf16[2,192,2048]{2,1,0:T(8,128)(2,1)S(1)}, bf16[2,192,2048]{2,1,0:T(8,128)(2,1)}, u32[]{:S(2)}, u32[]{:S(2)}) collective-permute-start(bf16[2,192,2048]{2,1,0:T(8,128)(2,1)S(1)} %maximum_maximum_fusion.1.o0), channel_id=1, source_target_pairs={{0,1},{1,0},{2,3},{3,2},{4,5},{5,4},{6,7},{7,6},{8,9},{9,8},{10,11... | collective-permute-start | bytes 4718600 | tf_op jit(solution)/shard_map/ppermute | solution.py:39
  90.6 13.1 %collective-permute-start.7 = (bf16[192,2048]{1,0:T(8,128)(2,1)}, bf16[192,2048]{1,0:T(8,128)(2,1)}, u32[]{:S(2)}, u32[]{:S(2)}) collective-permute-start(bf16[192,2048]{1,0:T(8,128)(2,1)} %slice_bitcast_fusion.13), channel_id=1, source_target_pairs={{0,2},{1,9},{2,4},{3,11},{4,6},{5,13},{6,0},{7,15},{8,10},{9,17},{... | collective-permute-start | bytes 2359304 | tf_op jit(solution)/shard_map/ppermute | solution.py:35
  95.5 12.5 %collective-permute-start.8 = (bf16[192,2048]{1,0:T(8,128)(2,1)}, bf16[192,2048]{1,0:T(8,128)(2,1)}, u32[]{:S(2)}, u32[]{:S(2)}) collective-permute-start(bf16[192,2048]{1,0:T(8,128)(2,1)} %slice_bitcast_fusion.12), channel_id=1, source_target_pairs={{0,6},{1,25},{2,0},{3,27},{4,2},{5,29},{6,4},{7,31},{8,14},{9,1},{... | collective-permute-start | bytes 2359304 | tf_op jit(solution)/shard_map/ppermute | solution.py:35
  98.7 14.1 %collective-permute-start.10 = (bf16[2,192,2048]{2,1,0:T(8,128)(2,1)S(1)}, bf16[2,192,2048]{2,1,0:T(8,128)(2,1)}, u32[]{:S(2)}, u32[]{:S(2)}) collective-permute-start(bf16[2,192,2048]{2,1,0:T(8,128)(2,1)S(1)} %collective-permute-done.5.o1), channel_id=1, source_target_pairs={{0,1},{1,0},{2,3},{3,2},{4,5},{5,4},{6,7},{7,6},{8,9},{9,8},{10,11... | collective-permute-start | bytes 4718600 | tf_op jit(solution)/shard_map/ppermute | solution.py:39
  101.2 15.5 %collective-permute-start.11 = (bf16[2,192,2048]{2,1,0:T(8,128)(2,1)}, bf16[2,192,2048]{2,1,0:T(8,128)(2,1)}, u32[]{:S(2)}, u32[]{:S(2)}) collective-permute-start(bf16[2,192,2048]{2,1,0:T(8,128)(2,1)} %collective-permute-done.6.o2), channel_id=1, source_target_pairs={{0,1},{1,0},{2,3},{3,2},{4,5},{5,4},{6,7},{7,6},{8,9},{9,8},{10,11... | collective-permute-start | bytes 4718600 | tf_op jit(solution)/shard_map/ppermute | solution.py:39
  103.7 13.0 %collective-permute-start.12 = (bf16[192,2048]{1,0:T(8,128)(2,1)}, bf16[192,2048]{1,0:T(8,128)(2,1)S(1)}, u32[]{:S(2)}, u32[]{:S(2)}) collective-permute-start(bf16[192,2048]{1,0:T(8,128)(2,1)} %collective-permute-done.7.ox), channel_id=1, source_target_pairs={{0,1},{1,0},{2,3},{3,2},{4,5},{5,4},{6,7},{7,6},{8,9},{9,8},{10,11... | collective-permute-start | bytes 2359304 | tf_op jit(solution)/shard_map/ppermute | solution.py:39
  112.8 24.1 %collective-permute-start.23 = (bf16[2,48,2048]{2,1,0:T(8,128)(2,1)}, bf16[2,48,2048]{2,1,0:T(8,128)(2,1)}, u32[]{:S(2)}, u32[]{:S(2)}) collective-permute-start(bf16[2,48,2048]{2,1,0:T(8,128)(2,1)} %get-tuple-element.41), channel_id=1, source_target_pairs={{0,8},{1,3},{2,10},{3,5},{4,12},{5,7},{6,14},{7,1},{8,16},{9,11},{... | collective-permute-start | bytes 1179656 | tf_op jit(solution)/shard_map/ppermute | solution.py:35
  112.8 25.1 %collective-permute-start.26 = (bf16[48,2048]{1,0:T(8,128)(2,1)}, bf16[48,2048]{1,0:T(8,128)(2,1)S(1)}, u32[]{:S(2)}, u32[]{:S(2)}) collective-permute-start(bf16[48,2048]{1,0:T(8,128)(2,1)} %slice_bitcast_fusion.16), channel_id=1, source_target_pairs={{0,24},{1,7},{2,26},{3,1},{4,28},{5,3},{6,30},{7,5},{8,0},{9,15},{... | collective-permute-start | bytes 589832 | tf_op jit(solution)/shard_map/ppermute | solution.py:35
  136.8 230.2 %all-gather.8.cloned.1.call-start = ((), (), s32[]{:S(2)}) async-start(), calls=%async_computation.1 | async-start | bytes 6635520 | tf_op jit(solution)/shard_map/all_gather | solution.py:452
  146.7 26.4 %collective-permute-start.27 = (bf16[2,192,2048]{2,1,0:T(8,128)(2,1)}, bf16[2,192,2048]{2,1,0:T(8,128)(2,1)}, u32[]{:S(2)}, u32[]{:S(2)}) collective-permute-start(bf16[2,192,2048]{2,1,0:T(8,128)(2,1)} %maximum_maximum_fusion.2.o0), channel_id=1, source_target_pairs={{0,2},{1,9},{2,4},{3,11},{4,6},{5,13},{6,0},{7,15},{8,10},{9,17},{... | collective-permute-start | bytes 4718600 | tf_op jit(solution)/shard_map/ppermute | solution.py:35
  146.7 27.7 %collective-permute-start.28 = (bf16[2,192,2048]{2,1,0:T(8,128)(2,1)}, bf16[2,192,2048]{2,1,0:T(8,128)(2,1)}, u32[]{:S(2)}, u32[]{:S(2)}) collective-permute-start(bf16[2,192,2048]{2,1,0:T(8,128)(2,1)} %maximum_maximum_fusion.2.o0), channel_id=1, source_target_pairs={{0,6},{1,25},{2,0},{3,27},{4,2},{5,29},{6,4},{7,31},{8,14},{9,1},{... | collective-permute-start | bytes 4718600 | tf_op jit(solution)/shard_map/ppermute | solution.py:35
  149.4 11.8 %collective-permute-start.48 = (bf16[2,48,1024]{2,1,0:T(8,128)(2,1)S(1)}, bf16[2,48,1024]{2,1,0:T(8,128)(2,1)S(1)}, u32[]{:S(2)}, u32[]{:S(2)}) collective-permute-start(bf16[2,48,1024]{2,1,0:T(8,128)(2,1)S(1)} %get-tuple-element.47), channel_id=1, source_target_pairs={{0,32},{32,64},{64,96},{96,0},{1,33},{33,65},{65,97},{97,1},{2,34}... | collective-permute-start | bytes 589832 | tf_op jit(solution)/shard_map/ppermute | solution.py:444
  150.1 19.8 %collective-permute-start.47 = (bf16[2,48,1024]{2,1,0:T(8,128)(2,1)S(1)}, bf16[2,48,1024]{2,1,0:T(8,128)(2,1)S(1)}, u32[]{:S(2)}, u32[]{:S(2)}) collective-permute-start(bf16[2,48,1024]{2,1,0:T(8,128)(2,1)S(1)} %get-tuple-element.46), channel_id=1, source_target_pairs={{0,64},{32,96},{64,0},{96,32},{1,65},{33,97},{65,1},{97,33},{2,66}... | collective-permute-start | bytes 589832 | tf_op jit(solution)/shard_map/ppermute | solution.py:444
  152.5 17.6 %collective-permute-start.46 = (bf16[2,48,1024]{2,1,0:T(8,128)(2,1)S(1)}, bf16[2,48,1024]{2,1,0:T(8,128)(2,1)S(1)}, u32[]{:S(2)}, u32[]{:S(2)}) collective-permute-start(bf16[2,48,1024]{2,1,0:T(8,128)(2,1)S(1)} %get-tuple-element.45), channel_id=1, source_target_pairs={{0,96},{32,0},{64,32},{96,64},{1,97},{33,1},{65,33},{97,65},{2,98}... | collective-permute-start | bytes 589832 | tf_op jit(solution)/shard_map/ppermute | solution.py:444
  173.0 34.4 %collective-permute-start.31 = (bf16[2,192,2048]{2,1,0:T(8,128)(2,1)}, bf16[2,192,2048]{2,1,0:T(8,128)(2,1)}, u32[]{:S(2)}, u32[]{:S(2)}) collective-permute-start(bf16[2,192,2048]{2,1,0:T(8,128)(2,1)} %maximum_maximum_fusion.2.o0), channel_id=1, source_target_pairs={{0,1},{1,0},{2,3},{3,2},{4,5},{5,4},{6,7},{7,6},{8,9},{9,8},{10,11... | collective-permute-start | bytes 4718600 | tf_op jit(solution)/shard_map/ppermute | solution.py:39
  174.3 12.5 %collective-permute-start.29 = (bf16[192,2048]{1,0:T(8,128)(2,1)S(1)}, bf16[192,2048]{1,0:T(8,128)(2,1)}, u32[]{:S(2)}, u32[]{:S(2)}) collective-permute-start(bf16[192,2048]{1,0:T(8,128)(2,1)S(1)} %slice_bitcast_fusion.7), channel_id=1, source_target_pairs={{0,2},{1,9},{2,4},{3,11},{4,6},{5,13},{6,0},{7,15},{8,10},{9,17},{... | collective-permute-start | bytes 2359304 | tf_op jit(solution)/shard_map/ppermute | solution.py:35
  175.6 12.5 %collective-permute-start.30 = (bf16[192,2048]{1,0:T(8,128)(2,1)S(1)}, bf16[192,2048]{1,0:T(8,128)(2,1)}, u32[]{:S(2)}, u32[]{:S(2)}) collective-permute-start(bf16[192,2048]{1,0:T(8,128)(2,1)S(1)} %slice_bitcast_fusion.6), channel_id=1, source_target_pairs={{0,6},{1,25},{2,0},{3,27},{4,2},{5,29},{6,4},{7,31},{8,14},{9,1},{... | collective-permute-start | bytes 2359304 | tf_op jit(solution)/shard_map/ppermute | solution.py:35
  178.3 30.0 %collective-permute-start.32 = (bf16[2,192,2048]{2,1,0:T(8,128)(2,1)}, bf16[2,192,2048]{2,1,0:T(8,128)(2,1)}, u32[]{:S(2)}, u32[]{:S(2)}) collective-permute-start(bf16[2,192,2048]{2,1,0:T(8,128)(2,1)} %collective-permute-done.27.o1), channel_id=1, source_target_pairs={{0,1},{1,0},{2,3},{3,2},{4,5},{5,4},{6,7},{7,6},{8,9},{9,8},{10,11... | collective-permute-start | bytes 4718600 | tf_op jit(solution)/shard_map/ppermute | solution.py:39
  179.3 32.6 %collective-permute-start.33 = (bf16[2,192,2048]{2,1,0:T(8,128)(2,1)}, bf16[2,192,2048]{2,1,0:T(8,128)(2,1)}, u32[]{:S(2)}, u32[]{:S(2)}) collective-permute-start(bf16[2,192,2048]{2,1,0:T(8,128)(2,1)} %collective-permute-done.28.o2), channel_id=1, source_target_pairs={{0,1},{1,0},{2,3},{3,2},{4,5},{5,4},{6,7},{7,6},{8,9},{9,8},{10,11... | collective-permute-start | bytes 4718600 | tf_op jit(solution)/shard_map/ppermute | solution.py:39
  186.8 25.1 %collective-permute-start.34 = (bf16[192,2048]{1,0:T(8,128)(2,1)}, bf16[192,2048]{1,0:T(8,128)(2,1)S(1)}, u32[]{:S(2)}, u32[]{:S(2)}) collective-permute-start(bf16[192,2048]{1,0:T(8,128)(2,1)} %collective-permute-done.29.ox), channel_id=1, source_target_pairs={{0,1},{1,0},{2,3},{3,2},{4,5},{5,4},{6,7},{7,6},{8,9},{9,8},{10,11... | collective-permute-start | bytes 2359304 | tf_op jit(solution)/shard_map/ppermute | solution.py:39
  188.1 23.9 %collective-permute-start.35 = (bf16[192,2048]{1,0:T(8,128)(2,1)}, bf16[192,2048]{1,0:T(8,128)(2,1)S(1)}, u32[]{:S(2)}, u32[]{:S(2)}) collective-permute-start(bf16[192,2048]{1,0:T(8,128)(2,1)} %collective-permute-done.30.oy), channel_id=1, source_target_pairs={{0,1},{1,0},{2,3},{3,2},{4,5},{5,4},{6,7},{7,6},{8,9},{9,8},{10,11... | collective-permute-start | bytes 2359304 | tf_op jit(solution)/shard_map/ppermute | solution.py:39
  207.4 66.8 %collective-permute-start.14 = (bf16[4,192,2048]{2,1,0:T(8,128)(2,1)}, bf16[4,192,2048]{2,1,0:T(8,128)(2,1)}, u32[]{:S(2)}, u32[]{:S(2)}) collective-permute-start(bf16[4,192,2048]{2,1,0:T(8,128)(2,1)} %get-tuple-element.19), channel_id=1, source_target_pairs={{0,1},{1,0},{2,3},{3,2},{4,5},{5,4},{6,7},{7,6},{8,9},{9,8},{10,11... | collective-permute-start | bytes 9437192 | tf_op jit(solution)/shard_map/ppermute | solution.py:39
  208.3 42.7 %collective-permute-start.51 = (bf16[2,2,3,48,512]{4,3,2,1,0:T(8,128)(2,1)}, bf16[2,2,3,48,512]{4,3,2,1,0:T(8,128)(2,1)}, u32[]{:S(2)}, u32[]{:S(2)}) collective-permute-start(bf16[2,2,3,48,512]{4,3,2,1,0:T(8,128)(2,1)} %pad_maximum_fusion.5), channel_id=1, source_target_pairs={{0,24},{1,7},{2,26},{3,1},{4,28},{5,3},{6,30},{7,5},{8,0},{9,15},{... | collective-permute-start | bytes 1769480 | tf_op jit(solution)/shard_map/ppermute | solution.py:35
  250.9 29.3 %collective-permute-start.36 = (bf16[4,192,2048]{2,1,0:T(8,128)(2,1)}, bf16[4,192,2048]{2,1,0:T(8,128)(2,1)}, u32[]{:S(2)}, u32[]{:S(2)}) collective-permute-start(bf16[4,192,2048]{2,1,0:T(8,128)(2,1)} %get-tuple-element.22), channel_id=1, source_target_pairs={{0,1},{1,0},{2,3},{3,2},{4,5},{5,4},{6,7},{7,6},{8,9},{9,8},{10,11... | collective-permute-start | bytes 9437192 | tf_op jit(solution)/shard_map/ppermute | solution.py:39
  250.9 10.4 %collective-permute-start.50 = (bf16[2,2,3,48,512]{4,3,2,1,0:T(8,128)(2,1)}, bf16[2,2,3,48,512]{4,3,2,1,0:T(8,128)(2,1)S(1)}, u32[]{:S(2)}, u32[]{:S(2)}) collective-permute-start(bf16[2,2,3,48,512]{4,3,2,1,0:T(8,128)(2,1)} %pad_maximum_fusion.5), channel_id=1, source_target_pairs={{0,8},{1,3},{2,10},{3,5},{4,12},{5,7},{6,14},{7,1},{8,16},{9,11},{... | collective-permute-start | bytes 1769480 | tf_op jit(solution)/shard_map/ppermute | solution.py:35
  271.5 41.0 %collective-permute-start.54 = (bf16[2,2,3,192,512]{4,3,2,1,0:T(8,128)(2,1)}, bf16[2,2,3,192,512]{4,3,2,1,0:T(8,128)(2,1)}, u32[]{:S(2)}, u32[]{:S(2)}) collective-permute-start(bf16[2,2,3,192,512]{4,3,2,1,0:T(8,128)(2,1)} %maximum_maximum_fusion.o0), channel_id=1, source_target_pairs={{0,2},{1,9},{2,4},{3,11},{4,6},{5,13},{6,0},{7,15},{8,10},{9,17},{... | collective-permute-start | bytes 7077896 | tf_op jit(solution)/shard_map/ppermute | solution.py:35
  271.5 65.6 %collective-permute-start.55 = (bf16[2,2,3,192,512]{4,3,2,1,0:T(8,128)(2,1)}, bf16[2,2,3,192,512]{4,3,2,1,0:T(8,128)(2,1)}, u32[]{:S(2)}, u32[]{:S(2)}) collective-permute-start(bf16[2,2,3,192,512]{4,3,2,1,0:T(8,128)(2,1)} %maximum_maximum_fusion.o0), channel_id=1, source_target_pairs={{0,6},{1,25},{2,0},{3,27},{4,2},{5,29},{6,4},{7,31},{8,14},{9,1},{... | collective-permute-start | bytes 7077896 | tf_op jit(solution)/shard_map/ppermute | solution.py:35
  277.3 27.9 %collective-permute-start.17 = (bf16[192,1024]{1,0:T(8,128)(2,1)S(1)}, bf16[192,1024]{1,0:T(8,128)(2,1)S(1)}, u32[]{:S(2)}, u32[]{:S(2)}) collective-permute-start(bf16[192,1024]{1,0:T(8,128)(2,1)S(1)} %get-tuple-element.63), channel_id=1, source_target_pairs={{0,2},{1,9},{2,4},{3,11},{4,6},{5,13},{6,0},{7,15},{8,10},{9,17},{... | collective-permute-start | bytes 1179656 | tf_op jit(solution)/shard_map/ppermute | solution.py:35
  277.5 27.9 %collective-permute-start.15 = (bf16[192,1024]{1,0:T(8,128)(2,1)S(1)}, bf16[192,1024]{1,0:T(8,128)(2,1)S(1)}, u32[]{:S(2)}, u32[]{:S(2)}) collective-permute-start(bf16[192,1024]{1,0:T(8,128)(2,1)S(1)} %get-tuple-element.62), channel_id=1, source_target_pairs={{0,6},{1,25},{2,0},{3,27},{4,2},{5,29},{6,4},{7,31},{8,14},{9,1},{... | collective-permute-start | bytes 1179656 | tf_op jit(solution)/shard_map/ppermute | solution.py:35
  283.9 25.6 %collective-permute-start.39 = (bf16[192,1024]{1,0:T(8,128)(2,1)S(1)}, bf16[192,1024]{1,0:T(8,128)(2,1)S(1)}, u32[]{:S(2)}, u32[]{:S(2)}) collective-permute-start(bf16[192,1024]{1,0:T(8,128)(2,1)S(1)} %get-tuple-element.55), channel_id=1, source_target_pairs={{0,2},{1,9},{2,4},{3,11},{4,6},{5,13},{6,0},{7,15},{8,10},{9,17},{... | collective-permute-start | bytes 1179656 | tf_op jit(solution)/shard_map/ppermute | solution.py:35
  305.4 12.5 %collective-permute-start.18 = (bf16[192,2048]{1,0:T(8,128)(2,1)S(1)}, bf16[192,2048]{1,0:T(8,128)(2,1)S(1)}, u32[]{:S(2)}, u32[]{:S(2)}) collective-permute-start(bf16[192,2048]{1,0:T(8,128)(2,1)S(1)} %pad_maximum_fusion.1), channel_id=1, source_target_pairs={{0,2},{1,9},{2,4},{3,11},{4,6},{5,13},{6,0},{7,15},{8,10},{9,17},{... | collective-permute-start | bytes 2359304 | tf_op jit(solution)/shard_map/ppermute | solution.py:35
  309.4 11.4 %collective-permute-start.16 = (bf16[192,2048]{1,0:T(8,128)(2,1)S(1)}, bf16[192,2048]{1,0:T(8,128)(2,1)S(1)}, u32[]{:S(2)}, u32[]{:S(2)}) collective-permute-start(bf16[192,2048]{1,0:T(8,128)(2,1)S(1)} %pad_maximum_fusion), channel_id=1, source_target_pairs={{0,6},{1,25},{2,0},{3,27},{4,2},{5,29},{6,4},{7,31},{8,14},{9,1},{... | collective-permute-start | bytes 2359304 | tf_op jit(solution)/shard_map/ppermute | solution.py:35
  312.2 14.1 %collective-permute-start.40 = (bf16[192,2048]{1,0:T(8,128)(2,1)S(1)}, bf16[192,2048]{1,0:T(8,128)(2,1)S(1)}, u32[]{:S(2)}, u32[]{:S(2)}) collective-permute-start(bf16[192,2048]{1,0:T(8,128)(2,1)S(1)} %pad_maximum_fusion.3), channel_id=1, source_target_pairs={{0,2},{1,9},{2,4},{3,11},{4,6},{5,13},{6,0},{7,15},{8,10},{9,17},{... | collective-permute-start | bytes 2359304 | tf_op jit(solution)/shard_map/ppermute | solution.py:35
  312.4 17.5 %collective-permute-start.38 = (bf16[192,2048]{1,0:T(8,128)(2,1)S(1)}, bf16[192,2048]{1,0:T(8,128)(2,1)S(1)}, u32[]{:S(2)}, u32[]{:S(2)}) collective-permute-start(bf16[192,2048]{1,0:T(8,128)(2,1)S(1)} %pad_maximum_fusion.2), channel_id=1, source_target_pairs={{0,6},{1,25},{2,0},{3,27},{4,2},{5,29},{6,4},{7,31},{8,14},{9,1},{... | collective-permute-start | bytes 2359304 | tf_op jit(solution)/shard_map/ppermute | solution.py:35
  317.9 31.1 %collective-permute-start.56 = (bf16[2,3,192,512]{3,2,1,0:T(8,128)(2,1)S(1)}, bf16[2,3,192,512]{3,2,1,0:T(8,128)(2,1)S(1)}, u32[]{:S(2)}, u32[]{:S(2)}) collective-permute-start(bf16[2,3,192,512]{3,2,1,0:T(8,128)(2,1)S(1)} %slice_bitcast_fusion.1), channel_id=1, source_target_pairs={{0,2},{1,9},{2,4},{3,11},{4,6},{5,13},{6,0},{7,15},{8,10},{9,17},{... | collective-permute-start | bytes 3538952 | tf_op jit(solution)/shard_map/ppermute | solution.py:35
  334.7 11.7 %collective-permute-start.20 = (bf16[48,2048]{1,0:T(8,128)(2,1)S(1)}, bf16[48,2048]{1,0:T(8,128)(2,1)S(1)}, u32[]{:S(2)}, u32[]{:S(2)}) collective-permute-start(bf16[48,2048]{1,0:T(8,128)(2,1)S(1)} %pad_maximum_fusion.7), channel_id=1, source_target_pairs={{0,24},{1,7},{2,26},{3,1},{4,28},{5,3},{6,30},{7,5},{8,0},{9,15},{... | collective-permute-start | bytes 589832 | tf_op jit(solution)/shard_map/ppermute | solution.py:35
  336.8 9.6 %collective-permute-start.44 = (bf16[48,2048]{1,0:T(8,128)(2,1)S(1)}, bf16[48,2048]{1,0:T(8,128)(2,1)S(1)}, u32[]{:S(2)}, u32[]{:S(2)}) collective-permute-start(bf16[48,2048]{1,0:T(8,128)(2,1)S(1)} %pad_maximum_fusion.10), channel_id=1, source_target_pairs={{0,8},{1,3},{2,10},{3,5},{4,12},{5,7},{6,14},{7,1},{8,16},{9,11},{... | collective-permute-start | bytes 589832 | tf_op jit(solution)/shard_map/ppermute | solution.py:35
  337.0 11.4 %collective-permute-start.42 = (bf16[48,2048]{1,0:T(8,128)(2,1)S(1)}, bf16[48,2048]{1,0:T(8,128)(2,1)S(1)}, u32[]{:S(2)}, u32[]{:S(2)}) collective-permute-start(bf16[48,2048]{1,0:T(8,128)(2,1)S(1)} %pad_maximum_fusion.9), channel_id=1, source_target_pairs={{0,24},{1,7},{2,26},{3,1},{4,28},{5,3},{6,30},{7,5},{8,0},{9,15},{... | collective-permute-start | bytes 589832 | tf_op jit(solution)/shard_map/ppermute | solution.py:35
  341.1 22.8 %collective-permute-start.58 = (bf16[2,2,3,192,512]{4,3,2,1,0:T(8,128)(2,1)}, bf16[2,2,3,192,512]{4,3,2,1,0:T(8,128)(2,1)}, u32[]{:S(2)}, u32[]{:S(2)}) collective-permute-start(bf16[2,2,3,192,512]{4,3,2,1,0:T(8,128)(2,1)} %maximum_maximum_fusion.o0), channel_id=1, source_target_pairs={{0,1},{1,0},{2,3},{3,2},{4,5},{5,4},{6,7},{7,6},{8,9},{9,8},{10,11... | collective-permute-start | bytes 7077896 | tf_op jit(solution)/shard_map/ppermute | solution.py:39
  346.4 15.3 %collective-permute-start.57 = (bf16[2,3,192,512]{3,2,1,0:T(8,128)(2,1)S(1)}, bf16[2,3,192,512]{3,2,1,0:T(8,128)(2,1)S(1)}, u32[]{:S(2)}, u32[]{:S(2)}) collective-permute-start(bf16[2,3,192,512]{3,2,1,0:T(8,128)(2,1)S(1)} %slice_bitcast_fusion), channel_id=1, source_target_pairs={{0,6},{1,25},{2,0},{3,27},{4,2},{5,29},{6,4},{7,31},{8,14},{9,1},{... | collective-permute-start | bytes 3538952 | tf_op jit(solution)/shard_map/ppermute | solution.py:35
  346.4 17.5 %collective-permute-start.59 = (bf16[2,2,3,192,512]{4,3,2,1,0:T(8,128)(2,1)}, bf16[2,2,3,192,512]{4,3,2,1,0:T(8,128)(2,1)}, u32[]{:S(2)}, u32[]{:S(2)}) collective-permute-start(bf16[2,2,3,192,512]{4,3,2,1,0:T(8,128)(2,1)} %collective-permute-done.54.o1), channel_id=1, source_target_pairs={{0,1},{1,0},{2,3},{3,2},{4,5},{5,4},{6,7},{7,6},{8,9},{9,8},{10,11... | collective-permute-start | bytes 7077896 | tf_op jit(solution)/shard_map/ppermute | solution.py:39
  348.4 15.4 %collective-permute-start.60 = (bf16[2,2,3,192,512]{4,3,2,1,0:T(8,128)(2,1)}, bf16[2,2,3,192,512]{4,3,2,1,0:T(8,128)(2,1)}, u32[]{:S(2)}, u32[]{:S(2)}) collective-permute-start(bf16[2,2,3,192,512]{4,3,2,1,0:T(8,128)(2,1)} %collective-permute-done.55.o2), channel_id=1, source_target_pairs={{0,1},{1,0},{2,3},{3,2},{4,5},{5,4},{6,7},{7,6},{8,9},{9,8},{10,11... | collective-permute-start | bytes 7077896 | tf_op jit(solution)/shard_map/ppermute | solution.py:39
  349.0 13.7 %collective-permute-start.45 = (bf16[48,2048]{1,0:T(8,128)(2,1)S(1)}, bf16[48,2048]{1,0:T(8,128)(2,1)S(1)}, u32[]{:S(2)}, u32[]{:S(2)}) collective-permute-start(bf16[48,2048]{1,0:T(8,128)(2,1)S(1)} %get-tuple-element.30), channel_id=1, source_target_pairs={{0,1},{1,0},{2,3},{3,2},{4,5},{5,4},{6,7},{7,6},{8,9},{9,8},{10,11... | collective-permute-start | bytes 589832 | tf_op jit(solution)/shard_map/ppermute | solution.py:39
  (53 other events, 567.5 us)
Sparse Core Ops, SparseCore 0:
  136.9 63.7 all-gather.5
  274.3 55.1 all-gather.7

commit v2 on v0

v2 whole, which is shorter than its diff:
```python
import functools

import jax
import jax.numpy as jnp
from jax import lax
from jax.experimental import pallas as pl
from jax.experimental.pallas import tpu as pltpu
from jax.sharding import PartitionSpec as P

BF16 = jnp.bfloat16
F32 = jnp.float32
OFFSETS = (0, -1, 1, 2)
META_ROWS = 64
HALF = 2
NT = (((1,), (1,)), ((), ()))
TN = (((0,), (0,)), ((), ()))
NN = (((1,), (0,)), ((), ()))


def dot(a, b, dims=NN):
    return lax.dot_general(a, b, dims, preferred_element_type=F32)


def after(v, *events):
    return lax.optimization_barrier((v, events))[0]


def expert_pairs(ring, shift):
    pairs = []
    for e in range(32):
        z, x, c = e // 8, (e // 2) % 4, e % 2
        if (ring == 1) == (c == 0):
            dst = ((z + shift) % 4) * 8 + x * 2 + c
        else:
            dst = z * 8 + ((x + shift) % 4) * 2 + c
        pairs.append((e, dst))
    return pairs


def step(v, ring, shift):
    return lax.ppermute(v, "expert", expert_pairs(ring, shift))


def swap_core(v):
    return lax.ppermute(v, "expert", [(e, e ^ 1) for e in range(32)])


def near(v, ring):
    return step(v, ring, 1), step(v, ring, -1)


def far(prev, succ, ring):
    return step(prev[0], ring, 1), step(succ[1], ring, -1)


def group_gather(h):
    up = [(s, (s + 1) % 4) for s in range(4)]
    down = [(s, (s - 1) % 4) for s in range(4)]
    half = h.shape[0] // 2
    prev = lax.ppermute(h, "dp", up)
    succ = lax.ppermute(h, "dp", down)
    far0 = lax.ppermute(prev[:half], "dp", up)
    far1 = lax.ppermute(succ[half:], "dp", down)
    return [h, succ, far0, far1, prev]


def tile_of(t, core, half):
    return jnp.where(t < half, core * half + t, (1 - core) * half + t - half)


def one_hot(slots, rows):
    r = lax.broadcasted_iota(jnp.int32, (rows, slots.shape[1]), 0)
    return jnp.where(slots == r, 1.0, 0.0).astype(BF16)


def row_probs(slots, prob, rows):
    r = lax.broadcasted_iota(jnp.int32, (rows, slots.shape[1]), 0)
    return jnp.sum(jnp.where(slots == r, prob, 0.0), axis=1, keepdims=True)


def forward_kernel(
    place, slot_own, slot_sib, prob, o0, o1, o2, ox, oy, s0, s1, s2, sx, sy, wg, wu, wd,
    h_ref, xi_ref, yi_ref, hot, prob_row, cat, xs, ys, gate, up, dh, *, half,
):
    t = pl.program_id(0)
    chunks, rows = hot.shape[1], hot.shape[2]
    toks = o0.shape[2]
    width = cat.shape[1]

    @pl.when(t == 0)
    def _():
        for k in range(chunks):
            hot[0, k] = one_hot(slot_own[k], rows)
            hot[1, k] = one_hot(slot_sib[k], rows)
            prob_row[rows * k : rows * (k + 1), :] = row_probs(slot_own[k], prob[k], rows)
        gate[...] = jnp.zeros_like(gate)
        up[...] = jnp.zeros_like(up)
        dh[...] = jnp.zeros_like(dh)

    def gather(side, b0, b1, b2, bx, by):
        for k in range(chunks):
            at = slice(rows * k, rows * (k + 1))
            for v, last in enumerate((bx, by)):
                for p, b in enumerate((b0, b1, b2)):
                    cat[toks * p : toks * (p + 1), :] = b[v, k]
                cat[3 * toks :, :] = last[k]
                got = dot(hot[side, k], cat[...])
                if v == 0:
                    xs[at, :] = got.astype(BF16)
                else:
                    ys[at, :] = (got * prob_row[at, :]).astype(BF16)

    @pl.when(t < half)
    def _():
        gather(0, o0, o1, o2, ox, oy)

    @pl.when(t >= half)
    def _():
        gather(1, s0, s1, s2, sx, sy)

    gate[...] += dot(xs[...], wg[...])
    up[...] += dot(xs[...], wu[...])
    dh[...] += dot(ys[...], wd[...], NT)
    per_group = 2 * half // 4
    rel = tile_of(t, place[0], half) - place[1] * per_group

    @pl.when((rel >= 0) & (rel < per_group))
    def _():
        at = pl.ds(pl.multiple_of(rel * width, width), width)
        xi_ref[:, at] = xs[...]
        yi_ref[:, at] = ys[...]

    @pl.when(t == 2 * half - 1)
    def _():
        ff = gate.shape[1]
        g, u, d = gate[...], up[...], dh[...]
        s = jax.nn.sigmoid(g)
        sg = g * s
        h_ref[:, 0:ff] = (d * u * s * (1.0 + g * (1.0 - s))).astype(BF16)
        h_ref[:, ff : 2 * ff] = (d * sg).astype(BF16)
        h_ref[:, 2 * ff :] = (sg * u).astype(BF16)


def whole(a):
    return pl.BlockSpec(a.shape, lambda *_: (0,) * a.ndim)


def forward(place, slot_own, slot_sib, prob, own, sib, wg, wu, wd, rows, half=4):
    width, ff = wg.shape
    tile = width // (2 * half)
    chunks, toks = own[0].shape[1:3]
    total = chunks * rows

    def own_t(t):
        return jnp.minimum(t, half - 1)

    def sib_t(t):
        return jnp.maximum(t - half, 0)

    big_own = pl.BlockSpec((2, chunks, toks, tile), lambda t, s: (0, 0, 0, own_t(t)))
    one_own = pl.BlockSpec((chunks, toks, tile), lambda t, s: (0, 0, own_t(t)))
    big_sib = pl.BlockSpec((2, chunks, toks, tile), lambda t, s: (0, 0, 0, sib_t(t)))
    one_sib = pl.BlockSpec((chunks, toks, tile), lambda t, s: (0, 0, sib_t(t)))
    w_in = pl.BlockSpec((tile, ff), lambda t, s: (tile_of(t, s[0], half), 0))
    w_out = pl.BlockSpec((ff, tile), lambda t, s: (0, tile_of(t, s[0], half)))
    return pl.pallas_call(
        functools.partial(forward_kernel, half=half),
        grid_spec=pltpu.PrefetchScalarGridSpec(
            num_scalar_prefetch=1,
            grid=(2 * half,),
            in_specs=[whole(slot_own), whole(slot_sib), whole(prob)]
            + [big_own] * 3 + [one_own] * 2 + [big_sib] * 3 + [one_sib] * 2
            + [w_in, w_in, w_out],
            out_specs=[
                pl.BlockSpec((total, 3 * ff), lambda t, s: (0, 0)),
                pl.BlockSpec((total, width // 4), lambda t, s: (0, 0)),
                pl.BlockSpec((total, width // 4), lambda t, s: (0, 0)),
            ],
            scratch_shapes=[
                pltpu.VMEM((2, chunks, rows, 4 * toks), BF16),
                pltpu.VMEM((total, 1), F32),
                pltpu.VMEM((4 * toks, tile), BF16),
                pltpu.VMEM((total, tile), BF16),
                pltpu.VMEM((total, tile), BF16),
                pltpu.VMEM((total, ff), F32),
                pltpu.VMEM((total, ff), F32),
                pltpu.VMEM((total, ff), F32),
            ],
        ),
        out_shape=[
            jax.ShapeDtypeStruct((total, 3 * ff), BF16),
            jax.ShapeDtypeStruct((total, width // 4), BF16),
            jax.ShapeDtypeStruct((total, width // 4), BF16),
        ],
        compiler_params=pltpu.CompilerParams(vmem_limit_bytes=50 * 2**20),
        cost_estimate=pl.CostEstimate(
            flops=2 * total * width * ff * 3 + 2 * total * 4 * toks * width * 2,
            bytes_accessed=3 * 2 * width * ff + 16 * chunks * toks * width,
            transcendentals=0,
        ),
        name="forward",
    )(place, slot_own, slot_sib, prob, *own, *sib, wg, wu, wd)


def rowgrad_kernel(h, wg, wu, out_ref, grad, pieces, *, cap):
    t = pl.program_id(0)
    ff = h.shape[1] // 2
    devices = out_ref.shape[0]
    grad[...] = dot(h[:, 0:ff], wg[...], NT) + dot(h[:, ff:], wu[...], NT)
    for q in range(4):

        @pl.when(t == q)
        def _():
            for n in range(devices):
                at = cap * (n // 2 + devices // 2 * (n % 2))
                pieces[n, cap * q : cap * (q + 1), :] = grad[at : at + cap, :]

    @pl.when(t == 3)
    def _():
        out_ref[...] = pieces[...].astype(BF16)


def rowgrad(h, wg, wu, cap):
    width, ff = wg.shape
    rows = h.shape[0]
    devices, tile = rows // cap, width // 4
    w_in = pl.BlockSpec((tile, ff), lambda t: (t, 0))
    shape = (devices, 4 * cap, tile)
    return pl.pallas_call(
        functools.partial(rowgrad_kernel, cap=cap),
        grid=(4,),
        in_specs=[pl.BlockSpec((rows, 2 * ff), lambda t: (0, 0)), w_in, w_in],
        out_specs=pl.BlockSpec(shape, lambda t: (0, 0, 0)),
        scratch_shapes=[pltpu.VMEM((rows, tile), F32), pltpu.VMEM(shape, F32)],
        out_shape=jax.ShapeDtypeStruct(shape, BF16),
        compiler_params=pltpu.CompilerParams(vmem_limit_bytes=40 * 2**20),
        cost_estimate=pl.CostEstimate(
            flops=2 * rows * width * ff * 2,
            bytes_accessed=2 * 2 * width * ff + 2 * rows * width,
            transcendentals=0,
        ),
        name="rowgrad",
    )(h, wg, wu)


def gather_kernel(slot, prob, xi, yi, blocks, out_ref, cat, xs, ys):
    i, j = pl.program_id(0), pl.program_id(1)
    total, wide = xi.shape
    chips, chunks, toks = blocks.shape[0], blocks.shape[1], blocks.shape[4]
    rows = total // chunks

    @pl.when((i == 0) & (j == 0))
    def _():
        xs[0:total] = xi[...]
        ys[0:total] = yi[...]

    @pl.when((i > 0) | (j > 0))
    def _():
        for k in range(chunks):
            slots = slot[0, k]
            hot = one_hot(slots, rows)
            scale = row_probs(slots, prob[0, k], rows)
            at = pl.ds(pl.multiple_of(j * total + k * rows, rows), rows)
            for n in range(chips):
                cat[toks * n : toks * (n + 1), :] = blocks[n, k, 0, 0]
            xs[at, :] = dot(hot, cat[...]).astype(BF16)
            for n in range(chips):
                cat[toks * n : toks * (n + 1), :] = blocks[n, k, 0, 1]
            ys[at, :] = (dot(hot, cat[...]) * scale).astype(BF16)

    @pl.when(j == 1)
    def _():
        out_ref[0:wide] = xs[...].T
        out_ref[wide:] = ys[...].T


def gather_columns(slot, prob, xi, yi, blocks):
    total, wide = xi.shape
    chips, chunks, _, _, toks, _ = blocks.shape
    meta = pl.BlockSpec((1, chunks, 1, chips * toks), lambda i, j: (2 * i + j, 0, 0, 0))
    return pl.pallas_call(
        gather_kernel,
        grid=(2, 2),
        in_specs=[
            meta, meta, whole(xi), whole(yi),
            pl.BlockSpec(
                (chips, chunks, 1, 2, toks, wide),
                lambda i, j: (0, 0, jnp.maximum(2 * i + j - 1, 0), 0, 0, 0),
            ),
        ],
        out_specs=pl.BlockSpec((2 * wide, 2 * total), lambda i, j: (0, i)),
        scratch_shapes=[
            pltpu.VMEM((chips * toks, wide), BF16),
            pltpu.VMEM((2 * total, wide), BF16),
            pltpu.VMEM((2 * total, wide), BF16),
        ],
        out_shape=jax.ShapeDtypeStruct((2 * wide, 4 * total), BF16),
        compiler_params=pltpu.CompilerParams(vmem_limit_bytes=50 * 2**20),
        cost_estimate=pl.CostEstimate(
            flops=2 * 3 * total * chips * toks * wide * 2,
            bytes_accessed=12 * chunks * chips * toks * wide + 16 * total * wide,
            transcendentals=0,
        ),
        name="gather_columns",
    )(slot, prob, xi, yi, blocks)


def weight_kernel(xy, *refs):
    hs, (gate_ref, up_ref, down_ref, cat) = refs[:-4], refs[-4:]
    m, n = pl.program_id(0), pl.program_id(1)

    @pl.when(n == 0)
    def _():
        at = 0
        for h in hs:
            cat[at : at + h.shape[0], :] = h[...]
            at += h.shape[0]

    res = dot(xy[...], cat[...])

    @pl.when(m == 0)
    def _():
        gate_ref[...] = res.astype(BF16)

    @pl.when(m == 1)
    def _():
        up_ref[...] = res.astype(BF16)

    @pl.when(m == 2)
    def _():
        down_ref[...] = res.astype(BF16).T


def weights(xy, hs, parts=2):
    wide, depth = xy.shape[0] // 2, xy.shape[1]
    ff = hs[0].shape[1] // 3
    bm = wide // parts

    def at(matrix):
        def index(m, n):
            return jnp.where(m == matrix, n, jnp.where(m < matrix, 0, parts - 1))
        return index

    return pl.pallas_call(
        weight_kernel,
        grid=(3, parts),
        in_specs=[pl.BlockSpec((bm, depth), lambda m, n: (jnp.where(m == 2, parts, 0) + n, 0))]
        + [pl.BlockSpec((h.shape[0], ff), lambda m, n: (0, m)) for h in hs],
        out_specs=[
            pl.BlockSpec((bm, ff), lambda m, n: (at(0)(m, n), 0)),
            pl.BlockSpec((bm, ff), lambda m, n: (at(1)(m, n), 0)),
            pl.BlockSpec((ff, bm), lambda m, n: (0, at(2)(m, n))),
        ],
        scratch_shapes=[pltpu.VMEM((depth, ff), BF16)],
        out_shape=[
            jax.ShapeDtypeStruct((wide, ff), BF16),
            jax.ShapeDtypeStruct((wide, ff), BF16),
            jax.ShapeDtypeStruct((ff, wide), BF16),
        ],
        compiler_params=pltpu.CompilerParams(vmem_limit_bytes=52 * 2**20),
        cost_estimate=pl.CostEstimate(
            flops=2 * depth * wide * ff * 3, bytes_accessed=depth * (8 * wide + 6 * ff), transcendentals=0
        ),
        name="weight_grads",
    )(xy, *hs)


def on_device(tokens, out_grad, expert_ids, route_probs, w_gate, w_up, w_down):
    toks, width = tokens.shape
    topk = expert_ids.shape[1]
    groups = lax.axis_size("expert")
    cap = 3 * toks * topk // (2 * groups)
    wg, wu, wd = w_gate[0], w_up[0], w_down[0]
    ff = wg.shape[1]
    rows = 16 * cap
    grp = lax.axis_index("dp")
    expert = lax.axis_index("expert")
    z, x, core = expert // 8, (expert // 2) % 4, expert % 2
    first = core == 0
    place = jnp.stack([core, grp]).astype(jnp.int32)
    both = jnp.stack([tokens, out_grad])

    def by_core(v):
        half = v.shape[-1] // 2
        mine = lax.dynamic_slice_in_dim(v, core * half, half, v.ndim - 1)
        other = lax.dynamic_slice_in_dim(v, (1 - core) * half, half, v.ndim - 1)
        got = swap_core(other)
        return jnp.where(first, mine, got), jnp.where(first, got, mine)

    named = expert_ids[:, :, None] == jnp.arange(groups, dtype=jnp.int32)
    chosen = jnp.any(named, axis=1)
    weight = jnp.sum(jnp.where(named, route_probs[:, :, None], 0.0), axis=1)
    lower = jnp.tril(jnp.ones((toks, toks), BF16), -1)
    rank = jnp.where(chosen, dot(lower, chosen.astype(BF16)), -1000.0)
    meta = jnp.stack([rank.T, weight.T], axis=1).reshape(2 * groups, toks)
    meta = jnp.pad(meta, ((0, META_ROWS - 2 * groups), (0, 128 - toks)))
    meta = lax.all_gather(meta, "expert").reshape(groups, META_ROWS // 2, 2, 128)
    meta = lax.dynamic_slice_in_dim(meta, expert, 1, 1)[:, 0, :, :toks]

    mine = jnp.stack(by_core(both), axis=1)
    col = jnp.concatenate([mine, *near(mine, 1), step(mine, 1, 2)], axis=-2)
    prev, succ = near(col, 2)

    metas = [meta]
    for g in (1, 2, 3):
        r = 4 - g
        metas.append(lax.ppermute(after(meta, col), "dp", [(s, (s + r) % 4) for s in range(4)]))
    metas = jnp.stack(metas).reshape(4, 16, 2, 2, toks)
    base = cap * jnp.arange(16, dtype=jnp.int32)[:, None]
    slots = (metas[:, :, :, 0].astype(jnp.int32) + base[None, :, None]).swapaxes(1, 2)
    slots = slots.reshape(4, 2, 1, 16 * toks)
    probs = metas[:, :, :, 1].swapaxes(1, 2).reshape(4, 2, 1, 16 * toks)
    meta = meta.reshape(16, 2, 2, toks)
    offs = jnp.array(OFFSETS, jnp.int32)
    r2, r1 = offs[:, None], offs[None, :]
    bz = jnp.where(first, z + r1, z + r2) % 4
    bx = jnp.where(first, x + r2, x + r1) % 4
    chip = bz * 4 + bx
    order = jnp.concatenate([chip.reshape(16), chip.T.reshape(16)])
    local = meta[order].reshape(2, 16, 2, 2, toks)
    local_slots = local[:, :, :, 0].astype(jnp.int32) + (cap * order).reshape(2, 16, 1, 1)
    local_slots = local_slots.swapaxes(1, 2).reshape(2, 2, 1, 16 * toks)
    local_probs = local[0, :, :, 1].swapaxes(0, 1).reshape(2, 1, 16 * toks)

    quarter = width // 4
    other_groups = []
    for g in (1, 2, 3):
        r = 4 - g
        part = lax.dynamic_slice_in_dim(after(both, col), ((grp + r) % 4) * quarter, quarter, 2)
        other_groups.append(lax.ppermute(part, "dp", [(s, (s + r) % 4) for s in range(4)]))
    cols = jnp.stack(other_groups).reshape(6 * toks, quarter)
    sib_col = swap_core(col)
    far0, far1 = far(after(prev, cols, metas, sib_col), after(succ, cols, metas, sib_col), 2)
    cols = lax.all_gather(after(cols, far0, far1), "expert", tiled=True)
    cols = cols.reshape(16, 2, 3, 2, toks, quarter)
    early = (sib_col, swap_core(prev), swap_core(succ))
    late = tuple(swap_core(after(p, early)) for p in (far0, far1))
    own, sib = (col, prev, succ, far0, far1), early + late

    h, xi, yi = forward(
        place, local_slots[0], local_slots[1], local_probs, own, sib, wg, wu, wd, rows
    )
    hs = group_gather(h)
    back = lax.all_to_all(rowgrad(h, wg, wu, cap), "expert", 0, 0, tiled=True)
    slots = after(slots, hs[1], hs[4])
    xy = gather_columns(slots, probs, xi, yi, cols)
    gate_grad, up_grad, down_grad = weights(xy, hs)
    back = after(back, gate_grad)
    piece = cap * jnp.arange(4, dtype=F32)
    pick = rank + piece[:, None, None]
    pick = pick[..., None] == jnp.arange(4 * cap, dtype=F32)
    pick = pick.astype(BF16).reshape(4 * toks, groups * 4 * cap)
    token_grad = dot(pick, back.reshape(groups * 4 * cap, quarter)).astype(BF16)
    token_grad = token_grad.reshape(4, toks, quarter).swapaxes(0, 1).reshape(toks, width)

    return token_grad, gate_grad[None], up_grad[None], down_grad[None]


def solution(mesh):
    in_specs = (
        P(("dp", "expert"), None),
        P(("dp", "expert"), None),
        P(("dp", "expert"), None),
        P(("dp", "expert"), None),
        P("expert", None, None),
        P("expert", None, None),
        P("expert", None, None),
    )
    out_specs = (
        P(("dp", "expert"), None),
        P("expert", "dp", None),
        P("expert", "dp", None),
        P("expert", None, "dp"),
    )
    return jax.shard_map(
        on_device, mesh=mesh, in_specs=in_specs, out_specs=out_specs, check_vma=False
    )
```

time: 603 us -> 300 us (0.50)
  waiting for transfers between devices: 360 us -> 127 us
  Pallas kernels: 0 us -> 77.8 us
  matrix products: 61.2 us -> 3.61 us
  local copies, waits for them, and re-layouts: 79.1 us -> 24.5 us
  other arithmetic: 50.5 us -> 6.99 us
  starting transfers between devices: 30 us -> 43.1 us
    reduce_scatter x1 -> x0, waiting for transfers between devices: 192 us -> none  [on_device(): lax.psum_scatter(jnp.concatenate([contract(flat_x, flat_dg), contract(fla...]
    all_to_all x3 -> x1, waiting for transfers between devices: 168 us -> 0.01 us  [on_device(): back = lax.all_to_all(rowgrad(h, wg, wu, cap), 'expert', 0, 0, tiled=True)]
    ppermute x0 -> x23, waiting for transfers between devices: none -> 94.9 us  [the longest x7 34.8 us: step(): return lax.ppermute(v, 'expert', expert_pairs(ring, shift))]
    pallas_call x0 -> x4, Pallas kernels: none -> 77.8 us  [the longest x1 30.8 us: forward(): pl.pallas_call(functools.partial(forward_kernel, half=half), grid_spec=pl...]
    dot_general x8 -> x2, matrix products: 61.2 us -> 3.61 us  [dot(): return lax.dot_general(a, b, dims, preferred_element_type=F32)]
    ppermute x0 -> x23, starting transfers between devices: none -> 35.6 us  [the longest x7 11.2 us: step(): return lax.ppermute(v, 'expert', expert_pairs(ring, shift))]
    all_gather x0 -> x2, waiting for transfers between devices: none -> 32.2 us  [the longest x1 32.2 us: on_device(): lax.all_gather(meta, 'expert').reshape(groups, META_ROWS // 2, 2, 128)]
    gather x5 -> x2, local copies, waits for them, and re-layouts: 32.3 us -> 0.64 us  [on_device(): local = meta[order].reshape(2, 16, 2, 2, toks)]
  transfers between devices with their start and end apart: 4 -> 26, of which waited for: 4 -> 16; matrix products, arithmetic and copies ran while one was open for 16% -> 6% of each run, Pallas kernels for 0% -> 26%
where the time goes in v2:
time: 300 us; the launch traced here: 298 us
  waiting for transfers between devices  127 us (42%)
  Pallas kernels  77.8 us (26%)
  starting transfers between devices  43.1 us (14%)
  local copies, waits for them, and re-layouts  24.5 us (8%)
  between operations  14.4 us (5%)
  other arithmetic  6.99 us (2%)
  matrix products  3.61 us (1%)
    ppermute x7, waiting for transfers between devices, step(): return lax.ppermute(v, 'expert', expert_pairs(ring, shift))  34.8 us
    ppermute x1, waiting for transfers between devices, group_gather(): prev = lax.ppermute(h, 'dp', up)  34.5 us
    all_gather x1, waiting for transfers between devices, on_device(): lax.all_gather(meta, 'expert').reshape(groups, META_ROWS // 2, 2, 128)  32.2 us
    pallas_call x1, Pallas kernels, forward(): pl.pallas_call(functools.partial(forward_kernel, half=half), grid_spec=pl...  30.8 us
    pallas_call x1, Pallas kernels, weights(): pl.pallas_call(weight_kernel, grid=(3, parts), in_specs=[pl.BlockSpec((bm...  19.5 us
    pallas_call x1, Pallas kernels, gather_columns(): pl.pallas_call(gather_kernel, grid=(2, 2), in_specs=[meta, meta, whole(xi...  16.3 us
    ppermute x6, waiting for transfers between devices, swap_core(): return lax.ppermute(v, 'expert', [(e, e ^ 1) for e in range(32)])  13.7 us
    ppermute x7, starting transfers between devices, step(): return lax.ppermute(v, 'expert', expert_pairs(ring, shift))  11.2 us
  transfers between devices with their start and end apart: 26, of which 16 were waited for; matrix products, arithmetic and copies ran while one was open for 6% of the time, Pallas kernels for 26%

profile of v2, /device:TPU:1, one launch (start us, length us, event | category | flops | bytes accessed | tf_op | source)
XLA Modules:
  0.0 297.5 jit_solution(1622907469912107653)
XLA Ops:
  7.2 1.1 fusion.1
  8.3 1.5 collective-permute-start
  9.8 1.3 collective-permute-done
  11.1 1.4 select_bitcast_fusion.1
  12.7 2.9 collective-permute-start.3
  17.1 8.4 %collective-permute-done.3 = bf16[2,2,48,2048]{3,2,1,0:T(8,128)(2,1)S(1)} collective-permute-done((bf16[2,2,48,2048]{3,2,1,0:T(8,128)(2,1)S(1)}, bf16[2,2,48,2048]{3,2,1,0:T(8,128)(2,1)S(1)}, u32[]{:S(2)}, u32[]{:S(2)}) %collective-permute-start.3) | collective-permute-done | bytes 786464 | tf_op jit(solution)/shard_map/ppermute | solution.py:41
  25.4 8.6 %collective-permute-done.2 = bf16[2,2,48,2048]{3,2,1,0:T(8,128)(2,1)S(1)} collective-permute-done((bf16[2,2,48,2048]{3,2,1,0:T(8,128)(2,1)S(1)}, bf16[2,2,48,2048]{3,2,1,0:T(8,128)(2,1)S(1)}, u32[]{:S(2)}, u32[]{:S(2)}) %collective-permute-start.2) | collective-permute-done | bytes 786464 | tf_op jit(solution)/shard_map/ppermute | solution.py:41
  34.0 1.8 pad_maximum_fusion.o0
  35.9 1.6 collective-permute-start.4
  37.5 2.4 collective-permute-start.12
  40.1 2.4 collective-permute-start.5
  43.4 1.4 collective-permute-start.8
  44.8 2.6 collective-permute-start.7
  47.4 4.2 %collective-permute-done.8 = bf16[2,48,1024]{2,1,0:T(8,128)(2,1)S(1)} collective-permute-done((bf16[2,48,1024]{2,1,0:T(8,128)(2,1)S(1)}, bf16[2,48,1024]{2,1,0:T(8,128)(2,1)S(1)}, u32[]{:S(2)}, u32[]{:S(2)}) %collective-permute-start.8) | collective-permute-done | bytes 196640 | tf_op jit(solution)/shard_map/ppermute | solution.py:430
  51.6 1.7 collective-permute-start.6
  53.2 32.2 %all-gather.6.cloned.1.call-done = f32[2048,128]{1,0:T(8,128)} async-done(((f32[64,128]{1,0:T(8,128)}), f32[2048,128]{1,0:T(8,128)}) %all-gather.6.cloned.1.call-update) | async-done | bytes 1048592 | tf_op jit(solution)/shard_map/all_gather | solution.py:397
  86.2 1.3 collective-permute-start.11
  87.5 2.5 collective-permute-start.10
  90.2 1.3 collective-permute-start.9
  93.1 1.5 slice_bitcast_fusion.1
  95.6 1.5 slice_bitcast_fusion
  97.1 1.9 collective-permute-start.14
  99.0 16.5 %collective-permute-done.13.ox = bf16[2,192,2048]{2,1,0:T(8,128)(2,1)S(1)} collective-permute-done((bf16[2,192,2048]{2,1,0:T(8,128)(2,1)S(1)}, bf16[2,192,2048]{2,1,0:T(8,128)(2,1)S(1)}, u32[]{:S(2)}, u32[]{:S(2)}) %collective-permute-start.13) | collective-permute-done | bytes 1572896 | tf_op jit(solution)/shard_map/ppermute | solution.py:41
  115.5 1.3 collective-permute-done.14.oy
  116.9 3.8 %collective-permute-start.15 = (bf16[2,2,192,2048]{3,2,1,0:T(8,128)(2,1)}, bf16[2,2,192,2048]{3,2,1,0:T(8,128)(2,1)}, u32[]{:S(2)}, u32[]{:S(2)}) collective-permute-start(bf16[2,2,192,2048]{3,2,1,0:T(8,128)(2,1)} %collective-permute-done.4.o1), channel_id=1, source_target_pairs={{0,1},{1,0},{2,3},{3,2},{4,5},{5,4},{6,7},{7,6},{8,9},{9,8},{10,11... | collective-permute-start | bytes 9437192 | tf_op jit(solution)/shard_map/ppermute | solution.py:45
  121.6 4.7 %collective-permute-done.15.s1 = bf16[2,2,192,2048]{3,2,1,0:T(8,128)(2,1)} collective-permute-done((bf16[2,2,192,2048]{3,2,1,0:T(8,128)(2,1)}, bf16[2,2,192,2048]{3,2,1,0:T(8,128)(2,1)}, u32[]{:S(2)}, u32[]{:S(2)}) %collective-permute-start.15) | collective-permute-done | bytes 3145760 | tf_op jit(solution)/shard_map/ppermute | solution.py:45
  126.3 4.5 %collective-permute-done.16.s2 = bf16[2,2,192,2048]{3,2,1,0:T(8,128)(2,1)} collective-permute-done((bf16[2,2,192,2048]{3,2,1,0:T(8,128)(2,1)}, bf16[2,2,192,2048]{3,2,1,0:T(8,128)(2,1)}, u32[]{:S(2)}, u32[]{:S(2)}) %collective-permute-start.16) | collective-permute-done | bytes 3145760 | tf_op jit(solution)/shard_map/ppermute | solution.py:45
  131.2 1.1 copy-done.3
  134.3 2.5 collective-permute-done.18.sy
  136.8 1.4 copy-done.4
  138.2 30.8 %forward.1 = (bf16[576,2304]{1,0:T(8,128)(2,1)}, bf16[576,1024]{1,0:T(8,128)(2,1)S(1)}, bf16[576,1024]{1,0:T(8,128)(2,1)S(1)}) custom-call(s32[2]{0:T(128)S(1)} %pad_add_fusion.place, s32[2,1,768]{2,1,0:T(1,128)S(1)} %squeeze.32.slot_own, s32[2,1,768]{2,1,0:T(1,128)S(1)} %squeeze.33.slot_sib, f32[2,1,768]{2,1,0:T(1,128)S(1)} %reshape.448.prob, ...), custom_call_target="tpu_custom_call" | custom-call | flops 18119393280 | bytes 44040192 | tf_op jit(solution)/shard_map/forward/pallas_call | solution.py:166
  169.1 2.8 collective-permute-start.19
  171.9 2.9 copy-done.1
  174.8 1.9 copy-done.2
  176.7 11.1 %rowgrad.1 = bf16[32,72,1024]{2,1,0:T(8,128)(2,1)S(1)} custom-call(bf16[576,2304]{1,0:T(8,128)(2,1)S(1)} %copy-done.2, bf16[4096,768]{1,0:T(8,128)(2,1)S(1)} %bitcast.97, bf16[4096,768]{1,0:T(8,128)(2,1)} %bitcast.127), custom_call_target="tpu_custom_call" | custom-call | flops 7247757312 | bytes 17301504 | tf_op jit(solution)/shard_map/rowgrad/pallas_call | solution.py:229
  187.8 2.2 copy-done
  190.0 7.4 %all-to-all-start = ((bf16[32,72,1024]{2,1,0:T(8,128)(2,1)}), bf16[32,72,1024]{2,1,0:T(8,128)(2,1)}, u32[]{:S(2)}, u32[]{:S(2)}) async-start(bf16[32,72,1024]{2,1,0:T(8,128)(2,1)} %copy-done), calls=%async_computation | async-start | bytes 9437184 | tf_op jit(solution)/shard_map/all_to_all | solution.py:444
  197.6 34.5 %collective-permute-done.20.refs_4_ = bf16[576,2304]{1,0:T(8,128)(2,1)} collective-permute-done((bf16[576,2304]{1,0:T(8,128)(2,1)}, bf16[576,2304]{1,0:T(8,128)(2,1)}, u32[]{:S(2)}, u32[]{:S(2)}) %collective-permute-start.20) | collective-permute-done | bytes 2654240 | tf_op jit(solution)/shard_map/ppermute | solution.py:60
  232.1 2.5 slice.54
  234.6 2.5 slice.55
  237.0 2.7 collective-permute-start.22
  239.7 1.0 iota_compare_fusion
  240.7 2.8 eq.54
  243.9 16.3 %gather_columns.1.xy = bf16[2048,2304]{1,0:T(8,128)(2,1)} custom-call(s32[4,2,1,768]{3,2,1,0:T(1,128)S(1)} %reshape.450.slot, f32[4,2,1,768]{3,2,1,0:T(1,128)S(1)} %reshape.451.prob, bf16[576,1024]{1,0:T(8,128)(2,1)S(1)} %get-tuple-element.27.xi, bf16[576,1024]{1,0:T(8,128)(2,1)S(1)} %get-tuple-element.28.yi, bf16[16,2,3,2,48,1024]{5,4,3,2,1,0:T(8,128)(2,1)} %bitcast.98), custom_call_target="tpu_custom_call" | custom-call | flops 5435817984 | bytes 28311552 | tf_op jit(solution)/shard_map/gather_columns/pallas_call | solution.py:281
  260.2 5.2 %collective-permute-done.21.refs_2_ = bf16[288,2304]{1,0:T(8,128)(2,1)} collective-permute-done((bf16[288,2304]{1,0:T(8,128)(2,1)}, bf16[288,2304]{1,0:T(8,128)(2,1)}, u32[]{:S(2)}, u32[]{:S(2)}) %collective-permute-start.21) | collective-permute-done | bytes 1327136 | tf_op jit(solution)/shard_map/ppermute | solution.py:62
  265.5 1.5 collective-permute-done.22.refs_3_
  266.9 19.5 %weight_grads.1 = (bf16[1024,768]{1,0:T(8,128)(2,1)}, bf16[1024,768]{1,0:T(8,128)(2,1)}, bf16[768,1024]{1,0:T(8,128)(2,1)}) custom-call(bf16[2048,2304]{1,0:T(8,128)(2,1)} %gather_columns.1.xy, bf16[576,2304]{1,0:T(8,128)(2,1)} %get-tuple-element.25.h.refs_0_, bf16[576,2304]{1,0:T(8,128)(2,1)} %collective-permute-done.19.refs_1_, ...), custom_call_target="tpu_custom_call" | custom-call | flops 10871635968 | bytes 29491200 | tf_op jit(solution)/shard_map/weight_grads/pallas_call | solution.py:344
  286.5 3.4 %convolution_convert_fusion = bf16[192,1024]{1,0:T(8,128)(2,1)S(1)} fusion(pred[192,2304]{1,0:T(32,128)(4,1)S(1)} %copy-done.7, bf16[2304,1024]{1,0:T(8,128)(2,1)} %bitcast.41), kind=kOutput, calls=%fused_computation.5 | convolution fusion | flops 906166272 | bytes 5554176 | tf_op jit(solution)/shard_map/dot_general | solution.py:21
  (92 shorter events, 10.9 us)
Async XLA Ops:
  7.2 78.3 %all-gather.6.cloned.1.call-start = ((), (), s32[]{:S(2)}) async-start(), calls=%async_computation.2 | async-start | bytes 1081344 | tf_op jit(solution)/shard_map/all_gather | solution.py:397
  8.3 2.9 collective-permute-start
  12.6 27.2 %copy-start.8 = (s32[48,8]{0,1:T(8,128)S(1)}, s32[48,8]{0,1:T(8,128)}, u32[]{:S(2)}) copy-start(s32[48,8]{0,1:T(8,128)} %param.10) | copy-start | bytes 4612
  12.6 29.8 %copy-start.9 = (f32[48,8]{0,1:T(8,128)S(1)}, f32[48,8]{0,1:T(8,128)}, u32[]{:S(2)}) copy-start(f32[48,8]{0,1:T(8,128)} %param.11) | copy-start | bytes 4612
  12.7 30.6 %copy-start.5 = (bf16[48,4096]{1,0:T(8,128)(2,1)S(1)}, bf16[48,4096]{1,0:T(8,128)(2,1)}, u32[]{:S(2)}) copy-start(bf16[48,4096]{1,0:T(8,128)(2,1)} %param.8) | copy-start | bytes 1179652
  12.7 30.6 %copy-start.6 = (bf16[48,4096]{1,0:T(8,128)(2,1)S(1)}, bf16[48,4096]{1,0:T(8,128)(2,1)}, u32[]{:S(2)}) copy-start(bf16[48,4096]{1,0:T(8,128)(2,1)} %param.9) | copy-start | bytes 1179652
  12.7 12.8 %collective-permute-start.3 = (bf16[2,2,48,2048]{3,2,1,0:T(8,128)(2,1)S(1)}, bf16[2,2,48,2048]{3,2,1,0:T(8,128)(2,1)S(1)}, u32[]{:S(2)}, u32[]{:S(2)}) collective-permute-start(bf16[2,2,48,2048]{3,2,1,0:T(8,128)(2,1)S(1)} %pad_maximum_fusion.2), channel_id=1, source_target_pairs={{0,16},{1,5},{2,18},{3,7},{4,20},{5,1},{6,22},{7,3},{8,24},{9,13},... | collective-permute-start | bytes 2359304 | tf_op jit(solution)/shard_map/ppermute | solution.py:41
  15.6 18.5 %collective-permute-start.2 = (bf16[2,2,48,2048]{3,2,1,0:T(8,128)(2,1)S(1)}, bf16[2,2,48,2048]{3,2,1,0:T(8,128)(2,1)S(1)}, u32[]{:S(2)}, u32[]{:S(2)}) collective-permute-start(bf16[2,2,48,2048]{3,2,1,0:T(8,128)(2,1)S(1)} %pad_maximum_fusion.2), channel_id=1, source_target_pairs={{0,24},{1,7},{2,26},{3,1},{4,28},{5,3},{6,30},{7,5},{8,0},{9,15},{... | collective-permute-start | bytes 2359304 | tf_op jit(solution)/shard_map/ppermute | solution.py:41
  16.5 17.6 %collective-permute-start.1 = (bf16[2,2,48,2048]{3,2,1,0:T(8,128)(2,1)S(1)}, bf16[2,2,48,2048]{3,2,1,0:T(8,128)(2,1)S(1)}, u32[]{:S(2)}, u32[]{:S(2)}) collective-permute-start(bf16[2,2,48,2048]{3,2,1,0:T(8,128)(2,1)S(1)} %pad_maximum_fusion.2), channel_id=1, source_target_pairs={{0,8},{1,3},{2,10},{3,5},{4,12},{5,7},{6,14},{7,1},{8,16},{9,11},{... | collective-permute-start | bytes 2359304 | tf_op jit(solution)/shard_map/ppermute | solution.py:41
  35.9 57.2 %collective-permute-start.4 = (bf16[2,2,192,2048]{3,2,1,0:T(8,128)(2,1)}, bf16[2,2,192,2048]{3,2,1,0:T(8,128)(2,1)}, u32[]{:S(2)}, u32[]{:S(2)}) collective-permute-start(bf16[2,2,192,2048]{3,2,1,0:T(8,128)(2,1)} %pad_maximum_fusion.o0), channel_id=1, source_target_pairs={{0,2},{1,9},{2,4},{3,11},{4,6},{5,13},{6,0},{7,15},{8,10},{9,17},{... | collective-permute-start | bytes 9437192 | tf_op jit(solution)/shard_map/ppermute | solution.py:41
  37.5 55.6 %collective-permute-start.12 = (bf16[2,2,192,2048]{3,2,1,0:T(8,128)(2,1)}, bf16[2,2,192,2048]{3,2,1,0:T(8,128)(2,1)}, u32[]{:S(2)}, u32[]{:S(2)}) collective-permute-start(bf16[2,2,192,2048]{3,2,1,0:T(8,128)(2,1)} %pad_maximum_fusion.o0), channel_id=1, source_target_pairs={{0,1},{1,0},{2,3},{3,2},{4,5},{5,4},{6,7},{7,6},{8,9},{9,8},{10,11... | collective-permute-start | bytes 9437192 | tf_op jit(solution)/shard_map/ppermute | solution.py:45
  40.1 55.5 %collective-permute-start.5 = (bf16[2,2,192,2048]{3,2,1,0:T(8,128)(2,1)}, bf16[2,2,192,2048]{3,2,1,0:T(8,128)(2,1)}, u32[]{:S(2)}, u32[]{:S(2)}) collective-permute-start(bf16[2,2,192,2048]{3,2,1,0:T(8,128)(2,1)} %pad_maximum_fusion.o0), channel_id=1, source_target_pairs={{0,6},{1,25},{2,0},{3,27},{4,2},{5,29},{6,4},{7,31},{8,14},{9,1},{... | collective-permute-start | bytes 9437192 | tf_op jit(solution)/shard_map/ppermute | solution.py:41
  43.2 200.7 %all-gather.4.cloned.1.call-start = ((), (), s32[]{:S(2)}) async-start(), calls=%async_computation.1 | async-start | bytes 19464192 | tf_op jit(solution)/shard_map/all_gather | solution.py:434
  43.4 8.2 %collective-permute-start.8 = (bf16[2,48,1024]{2,1,0:T(8,128)(2,1)S(1)}, bf16[2,48,1024]{2,1,0:T(8,128)(2,1)S(1)}, u32[]{:S(2)}, u32[]{:S(2)}) collective-permute-start(bf16[2,48,1024]{2,1,0:T(8,128)(2,1)S(1)} %get-tuple-element.37), channel_id=1, source_target_pairs={{0,32},{32,64},{64,96},{96,0},{1,33},{33,65},{65,97},{97,1},{2,34}... | collective-permute-start | bytes 589832 | tf_op jit(solution)/shard_map/ppermute | solution.py:430
  44.8 41.4 %collective-permute-start.7 = (bf16[2,48,1024]{2,1,0:T(8,128)(2,1)S(1)}, bf16[2,48,1024]{2,1,0:T(8,128)(2,1)S(1)}, u32[]{:S(2)}, u32[]{:S(2)}) collective-permute-start(bf16[2,48,1024]{2,1,0:T(8,128)(2,1)S(1)} %get-tuple-element.38), channel_id=1, source_target_pairs={{0,64},{32,96},{64,0},{96,32},{1,65},{33,97},{65,1},{97,33},{2,66}... | collective-permute-start | bytes 589832 | tf_op jit(solution)/shard_map/ppermute | solution.py:430
  51.6 35.9 %collective-permute-start.6 = (bf16[2,48,1024]{2,1,0:T(8,128)(2,1)S(1)}, bf16[2,48,1024]{2,1,0:T(8,128)(2,1)S(1)}, u32[]{:S(2)}, u32[]{:S(2)}) collective-permute-start(bf16[2,48,1024]{2,1,0:T(8,128)(2,1)S(1)} %get-tuple-element.36), channel_id=1, source_target_pairs={{0,96},{32,0},{64,32},{96,64},{1,97},{33,1},{65,33},{97,65},{2,98}... | collective-permute-start | bytes 589832 | tf_op jit(solution)/shard_map/ppermute | solution.py:430
  86.2 4.0 %collective-permute-start.11 = (f32[32,2,48]{2,0,1:T(8,128)S(1)}, f32[32,2,48]{2,0,1:T(8,128)S(1)}, u32[]{:S(2)}, u32[]{:S(2)}) collective-permute-start(f32[32,2,48]{2,0,1:T(8,128)S(1)} %bitcast.115), channel_id=1, source_target_pairs={{0,32},{32,64},{64,96},{96,0},{1,33},{33,65},{65,97},{97,1},{2,34}... | collective-permute-start | bytes 36872 | tf_op jit(solution)/shard_map/ppermute | solution.py:407
  87.5 4.9 %collective-permute-start.10 = (f32[32,2,48]{2,0,1:T(8,128)S(1)}, f32[32,2,48]{2,0,1:T(8,128)S(1)}, u32[]{:S(2)}, u32[]{:S(2)}) collective-permute-start(f32[32,2,48]{2,0,1:T(8,128)S(1)} %bitcast.116), channel_id=1, source_target_pairs={{0,64},{32,96},{64,0},{96,32},{1,65},{33,97},{65,1},{97,33},{2,66}... | collective-permute-start | bytes 36872 | tf_op jit(solution)/shard_map/ppermute | solution.py:407
  90.2 2.8 collective-permute-start.9
  93.1 27.6 %copy-start.10 = (s32[4]{0:T(128)S(1)}, s32[4]{0:T(128)}, u32[]{:S(2)}) copy-start(s32[4]{0:T(128)} %constant.118.clone) | copy-start | bytes 52
  94.6 20.8 %collective-permute-start.13 = (bf16[2,192,2048]{2,1,0:T(8,128)(2,1)S(1)}, bf16[2,192,2048]{2,1,0:T(8,128)(2,1)S(1)}, u32[]{:S(2)}, u32[]{:S(2)}) collective-permute-start(bf16[2,192,2048]{2,1,0:T(8,128)(2,1)S(1)} %slice_bitcast_fusion.1), channel_id=1, source_target_pairs={{0,2},{1,9},{2,4},{3,11},{4,6},{5,13},{6,0},{7,15},{8,10},{9,17},{... | collective-permute-start | bytes 4718600 | tf_op jit(solution)/shard_map/ppermute | solution.py:41
  97.1 19.7 %collective-permute-start.14 = (bf16[2,192,2048]{2,1,0:T(8,128)(2,1)S(1)}, bf16[2,192,2048]{2,1,0:T(8,128)(2,1)}, u32[]{:S(2)}, u32[]{:S(2)}) collective-permute-start(bf16[2,192,2048]{2,1,0:T(8,128)(2,1)S(1)} %slice_bitcast_fusion), channel_id=1, source_target_pairs={{0,6},{1,25},{2,0},{3,27},{4,2},{5,29},{6,4},{7,31},{8,14},{9,1},{... | collective-permute-start | bytes 4718600 | tf_op jit(solution)/shard_map/ppermute | solution.py:41
  116.9 9.4 %collective-permute-start.15 = (bf16[2,2,192,2048]{3,2,1,0:T(8,128)(2,1)}, bf16[2,2,192,2048]{3,2,1,0:T(8,128)(2,1)}, u32[]{:S(2)}, u32[]{:S(2)}) collective-permute-start(bf16[2,2,192,2048]{3,2,1,0:T(8,128)(2,1)} %collective-permute-done.4.o1), channel_id=1, source_target_pairs={{0,1},{1,0},{2,3},{3,2},{4,5},{5,4},{6,7},{7,6},{8,9},{9,8},{10,11... | collective-permute-start | bytes 9437192 | tf_op jit(solution)/shard_map/ppermute | solution.py:45
  120.7 10.1 %collective-permute-start.16 = (bf16[2,2,192,2048]{3,2,1,0:T(8,128)(2,1)}, bf16[2,2,192,2048]{3,2,1,0:T(8,128)(2,1)}, u32[]{:S(2)}, u32[]{:S(2)}) collective-permute-start(bf16[2,2,192,2048]{3,2,1,0:T(8,128)(2,1)} %collective-permute-done.5.o2), channel_id=1, source_target_pairs={{0,1},{1,0},{2,3},{3,2},{4,5},{5,4},{6,7},{7,6},{8,9},{9,8},{10,11... | collective-permute-start | bytes 9437192 | tf_op jit(solution)/shard_map/ppermute | solution.py:45
  130.8 3.5 %collective-permute-start.17 = (bf16[2,192,2048]{2,1,0:T(8,128)(2,1)S(1)}, bf16[2,192,2048]{2,1,0:T(8,128)(2,1)}, u32[]{:S(2)}, u32[]{:S(2)}) collective-permute-start(bf16[2,192,2048]{2,1,0:T(8,128)(2,1)S(1)} %collective-permute-done.13.ox), channel_id=1, source_target_pairs={{0,1},{1,0},{2,3},{3,2},{4,5},{5,4},{6,7},{7,6},{8,9},{9,8},{10,11... | collective-permute-start | bytes 4718600 | tf_op jit(solution)/shard_map/ppermute | solution.py:45
  131.2 1.1 copy-start.3
  132.3 4.5 %collective-permute-start.18 = (bf16[2,192,2048]{2,1,0:T(8,128)(2,1)}, bf16[2,192,2048]{2,1,0:T(8,128)(2,1)}, u32[]{:S(2)}, u32[]{:S(2)}) collective-permute-start(bf16[2,192,2048]{2,1,0:T(8,128)(2,1)} %collective-permute-done.14.oy), channel_id=1, source_target_pairs={{0,1},{1,0},{2,3},{3,2},{4,5},{5,4},{6,7},{7,6},{8,9},{9,8},{10,11... | collective-permute-start | bytes 4718600 | tf_op jit(solution)/shard_map/ppermute | solution.py:45
  136.8 1.4 copy-start.4
  169.1 65.5 %collective-permute-start.19 = (bf16[576,2304]{1,0:T(8,128)(2,1)}, bf16[576,2304]{1,0:T(8,128)(2,1)}, u32[]{:S(2)}, u32[]{:S(2)}) collective-permute-start(bf16[576,2304]{1,0:T(8,128)(2,1)} %get-tuple-element.25.h.refs_0_), channel_id=1, source_target_pairs={{0,96},{32,0},{64,32},{96,64},{1,97},{33,1},{65,33},{97,65},{2,98}... | collective-permute-start | bytes 7962632 | tf_op jit(solution)/shard_map/ppermute | solution.py:61
  171.9 60.2 %collective-permute-start.20 = (bf16[576,2304]{1,0:T(8,128)(2,1)}, bf16[576,2304]{1,0:T(8,128)(2,1)}, u32[]{:S(2)}, u32[]{:S(2)}) collective-permute-start(bf16[576,2304]{1,0:T(8,128)(2,1)} %get-tuple-element.25.h.refs_0_), channel_id=1, source_target_pairs={{0,32},{32,64},{64,96},{96,0},{1,33},{33,65},{65,97},{97,1},{2,34}... | collective-permute-start | bytes 7962632 | tf_op jit(solution)/shard_map/ppermute | solution.py:60
  171.9 2.9 copy-start.1
  174.8 1.9 copy-start.2
  187.8 2.2 copy-start
  190.0 96.5 %all-to-all-start = ((bf16[32,72,1024]{2,1,0:T(8,128)(2,1)}), bf16[32,72,1024]{2,1,0:T(8,128)(2,1)}, u32[]{:S(2)}, u32[]{:S(2)}) async-start(bf16[32,72,1024]{2,1,0:T(8,128)(2,1)} %copy-done), calls=%async_computation | async-start | bytes 9437184 | tf_op jit(solution)/shard_map/all_to_all | solution.py:444
  234.6 30.9 %collective-permute-start.21 = (bf16[288,2304]{1,0:T(8,128)(2,1)}, bf16[288,2304]{1,0:T(8,128)(2,1)}, u32[]{:S(2)}, u32[]{:S(2)}) collective-permute-start(bf16[288,2304]{1,0:T(8,128)(2,1)} %slice.54), channel_id=1, source_target_pairs={{0,32},{32,64},{64,96},{96,0},{1,33},{33,65},{65,97},{97,1},{2,34}... | collective-permute-start | bytes 3981320 | tf_op jit(solution)/shard_map/ppermute | solution.py:62
  237.0 29.9 %collective-permute-start.22 = (bf16[288,2304]{1,0:T(8,128)(2,1)}, bf16[288,2304]{1,0:T(8,128)(2,1)}, u32[]{:S(2)}, u32[]{:S(2)}) collective-permute-start(bf16[288,2304]{1,0:T(8,128)(2,1)} %slice.55), channel_id=1, source_target_pairs={{0,96},{32,0},{64,32},{96,64},{1,97},{33,1},{65,33},{97,65},{2,98}... | collective-permute-start | bytes 3981320 | tf_op jit(solution)/shard_map/ppermute | solution.py:63
  260.2 26.2 %copy-start.7 = (pred[192,2304]{1,0:T(32,128)(4,1)S(1)}, pred[192,2304]{1,0:T(32,128)(4,1)}, u32[]{:S(2)}) copy-start(pred[192,2304]{1,0:T(32,128)(4,1)} %eq.54) | copy-start | bytes 1327108
Sparse Core Ops, SparseCore 0:
  43.3 42.0 all-gather.5
  117.0 82.1 all-gather.3

commit v3 on v2

v3 whole, which is shorter than its diff:
```python
import functools

import jax
import jax.numpy as jnp
from jax import lax
from jax.experimental import pallas as pl
from jax.experimental.pallas import tpu as pltpu
from jax.sharding import PartitionSpec as P

BF16 = jnp.bfloat16
F32 = jnp.float32
OFFSETS = (0, -1, 1, 2)
HALF = 2
LIGHT = pl.CostEstimate(flops=1, bytes_accessed=1, transcendentals=0)
HEAVY = 4
NT = (((1,), (1,)), ((), ()))
TN = (((0,), (0,)), ((), ()))
NN = (((1,), (0,)), ((), ()))


def dot(a, b, dims=NN):
    return lax.dot_general(a, b, dims, preferred_element_type=F32)


def after(v, *events):
    return lax.optimization_barrier((v, events))[0]


def expert_pairs(ring, shift):
    pairs = []
    for e in range(32):
        z, x, c = e // 8, (e // 2) % 4, e % 2
        if (ring == 1) == (c == 0):
            dst = ((z + shift) % 4) * 8 + x * 2 + c
        else:
            dst = z * 8 + ((x + shift) % 4) * 2 + c
        pairs.append((e, dst))
    return pairs


def step(v, ring, shift):
    return lax.ppermute(v, "expert", expert_pairs(ring, shift))


def swap_core(v):
    return lax.ppermute(v, "expert", [(e, e ^ 1) for e in range(32)])


def near(v, ring):
    return step(v, ring, 1), step(v, ring, -1)


def far(prev, succ, ring):
    return step(prev[0], ring, 1), step(succ[1], ring, -1)


def over_groups(v, shift):
    return lax.ppermute(v, "dp", [(s, (s + shift) % 4) for s in range(4)])


def tile_of(t, core, half):
    return jnp.where(t < half, core * half + t, (1 - core) * half + t - half)


def one_hot(slots, rows):
    r = lax.broadcasted_iota(jnp.int32, (rows, slots.shape[1]), 0)
    return jnp.where(slots == r, 1.0, 0.0).astype(BF16)


def row_probs(slots, prob, rows):
    r = lax.broadcasted_iota(jnp.int32, (rows, slots.shape[1]), 0)
    return jnp.sum(jnp.where(slots == r, prob, 0.0), axis=1, keepdims=True)


def pick_rows(t, half, hot, cat, own, sib, put):
    def gather(side, blocks):
        toks = blocks[0].shape[1]
        for k in range(2):
            for p in range(4):
                cat[toks * p : toks * (p + 1), :] = blocks[4 * k + p][0]
            put(k, dot(hot[side, k], cat[...]))

    @pl.when(t < half)
    def _():
        gather(0, own)

    @pl.when(t >= half)
    def _():
        gather(1, sib)


def keep_columns(t, place, half, rows, out_ref):
    width = rows.shape[1]
    per_group = 2 * half // 4
    rel = tile_of(t, place[0], half) - place[1] * per_group

    @pl.when((rel >= 0) & (rel < per_group))
    def _():
        out_ref[:, pl.ds(pl.multiple_of(rel * width, width), width)] = rows[...]


def hidden_kernel(place, slot_own, slot_sib, *refs, half):
    own, sib = refs[0:8], refs[8:16]
    wg, wu, hid_ref, sg_ref, slope_ref, xi_ref, hot, cat, xs, gate, up = refs[16:]
    t = pl.program_id(0)
    rows = hot.shape[2]

    @pl.when(t == 0)
    def _():
        for k in range(2):
            hot[0, k] = one_hot(slot_own[k], rows)
            hot[1, k] = one_hot(slot_sib[k], rows)
        gate[...] = jnp.zeros_like(gate)
        up[...] = jnp.zeros_like(up)

    def put(k, got):
        xs[rows * k : rows * (k + 1), :] = got.astype(BF16)

    pick_rows(t, half, hot, cat, own, sib, put)
    gate[...] += dot(xs[...], wg[...])
    up[...] += dot(xs[...], wu[...])
    keep_columns(t, place, half, xs, xi_ref)

    @pl.when(t == 2 * half - 1)
    def _():
        g, u = gate[...], up[...]
        s = jax.nn.sigmoid(g)
        sg = g * s
        hid_ref[...] = (sg * u).astype(BF16)
        sg_ref[...] = sg
        slope_ref[...] = u * s * (1.0 + g * (1.0 - s))


def cotangent_kernel(place, slot_own, slot_sib, prob, *refs, half):
    own, sib = refs[0:8], refs[8:16]
    wd, sg, slope, dd_ref, yi_ref, hot, prob_row, cat, ys, dh = refs[16:]
    t = pl.program_id(0)
    rows = hot.shape[2]

    @pl.when(t == 0)
    def _():
        for k in range(2):
            hot[0, k] = one_hot(slot_own[k], rows)
            hot[1, k] = one_hot(slot_sib[k], rows)
            prob_row[rows * k : rows * (k + 1), :] = row_probs(slot_own[k], prob[k], rows)
        dh[...] = jnp.zeros_like(dh)

    def put(k, got):
        at = slice(rows * k, rows * (k + 1))
        ys[at, :] = (got * prob_row[at, :]).astype(BF16)

    pick_rows(t, half, hot, cat, own, sib, put)
    dh[...] += dot(ys[...], wd[...], NT)
    keep_columns(t, place, half, ys, yi_ref)

    @pl.when(t == 2 * half - 1)
    def _():
        dd_ref[0] = (dh[...] * slope[...]).astype(BF16)
        dd_ref[1] = (dh[...] * sg[...]).astype(BF16)


def whole(a):
    return pl.BlockSpec(a.shape, lambda *_: (0,) * a.ndim)


def ring_specs(own, tile, half):
    def spec(block, at):
        array, index = block
        return pl.BlockSpec((1, array.shape[1], tile), lambda t, s: (index, 0, at(t)))

    here = [spec(b, lambda t: jnp.minimum(t, half - 1)) for b in own]
    return here + [spec(b, lambda t: jnp.maximum(t - half, 0)) for b in own]


def hidden_rows(place, slot_own, slot_sib, own, sib, wg, wu, rows, half=4):
    width, ff = wg.shape
    tile = width // (2 * half)
    toks = own[0][0].shape[1]
    total = 2 * rows
    w_in = pl.BlockSpec((tile, ff), lambda t, s: (tile_of(t, s[0], half), 0))
    const = lambda shape: pl.BlockSpec(shape, lambda t, s: (0,) * len(shape))
    outs = [((total, ff), BF16), ((total, ff), F32), ((total, ff), F32), ((total, width // 4), BF16)]
    return pl.pallas_call(
        functools.partial(hidden_kernel, half=half),
        grid_spec=pltpu.PrefetchScalarGridSpec(
            num_scalar_prefetch=1,
            grid=(2 * half,),
            in_specs=[whole(slot_own), whole(slot_sib)] + ring_specs(own, tile, half) + [w_in, w_in],
            out_specs=[const(shape) for shape, _ in outs],
            scratch_shapes=[
                pltpu.VMEM((2, 2, rows, 4 * toks), BF16),
                pltpu.VMEM((4 * toks, tile), BF16),
                pltpu.VMEM((total, tile), BF16),
                pltpu.VMEM((total, ff), F32),
                pltpu.VMEM((total, ff), F32),
            ],
        ),
        out_shape=[jax.ShapeDtypeStruct(shape, kind) for shape, kind in outs],
        compiler_params=pltpu.CompilerParams(vmem_limit_bytes=56 * 2**20),
        cost_estimate=pl.CostEstimate(
            flops=2 * total * width * ff * 2 + 2 * total * 4 * toks * width,
            bytes_accessed=2 * 2 * width * ff + 16 * toks * width,
            transcendentals=0,
        ),
        name="hidden_rows",
    )(place, slot_own, slot_sib, *(b for b, _ in own + sib), wg, wu)


def cotangent_rows(place, slot_own, slot_sib, prob, own, sib, wd, sg, slope, rows, half=4):
    ff, width = wd.shape
    tile = width // (2 * half)
    toks = own[0][0].shape[1]
    total = 2 * rows
    w_out = pl.BlockSpec((ff, tile), lambda t, s: (0, tile_of(t, s[0], half)))
    const = lambda shape: pl.BlockSpec(shape, lambda t, s: (0,) * len(shape))
    outs = [((2, total, ff), BF16), ((total, width // 4), BF16)]
    return pl.pallas_call(
        functools.partial(cotangent_kernel, half=half),
        grid_spec=pltpu.PrefetchScalarGridSpec(
            num_scalar_prefetch=1,
            grid=(2 * half,),
            in_specs=[whole(slot_own), whole(slot_sib), whole(prob)]
            + ring_specs(own, tile, half) + [w_out, whole(sg), whole(slope)],
            out_specs=[const(shape) for shape, _ in outs],
            scratch_shapes=[
                pltpu.VMEM((2, 2, rows, 4 * toks), BF16),
                pltpu.VMEM((total, 1), F32),
                pltpu.VMEM((4 * toks, tile), BF16),
                pltpu.VMEM((total, tile), BF16),
                pltpu.VMEM((total, ff), F32),
            ],
        ),
        out_shape=[jax.ShapeDtypeStruct(shape, kind) for shape, kind in outs],
        compiler_params=pltpu.CompilerParams(vmem_limit_bytes=56 * 2**20),
        cost_estimate=pl.CostEstimate(
            flops=2 * total * width * ff + 2 * total * 4 * toks * width,
            bytes_accessed=2 * width * ff + 16 * toks * width,
            transcendentals=0,
        ),
        name="cotangent_rows",
    )(place, slot_own, slot_sib, prob, *(b for b, _ in own + sib), wd, sg, slope)


def rowgrad_kernel(h, wg, wu, out_ref, grad, pieces, *, cap):
    t = pl.program_id(0)
    devices = out_ref.shape[0]
    grad[...] = dot(h[0], wg[...], NT) + dot(h[1], wu[...], NT)
    for q in range(4):

        @pl.when(t == q)
        def _():
            for n in range(devices):
                at = cap * (n // 2 + devices // 2 * (n % 2))
                pieces[n, cap * q : cap * (q + 1), :] = grad[at : at + cap, :]

    @pl.when(t == 3)
    def _():
        out_ref[...] = pieces[...].astype(BF16)


def rowgrad(h, wg, wu, cap):
    width, ff = wg.shape
    rows = h.shape[1]
    devices, tile = rows // cap, width // 4
    w_in = pl.BlockSpec((tile, ff), lambda t: (t, 0))
    shape = (devices, 4 * cap, tile)
    return pl.pallas_call(
        functools.partial(rowgrad_kernel, cap=cap),
        grid=(4,),
        in_specs=[whole(h), w_in, w_in],
        out_specs=pl.BlockSpec(shape, lambda t: (0, 0, 0)),
        scratch_shapes=[pltpu.VMEM((rows, tile), F32), pltpu.VMEM(shape, F32)],
        out_shape=jax.ShapeDtypeStruct(shape, BF16),
        compiler_params=pltpu.CompilerParams(vmem_limit_bytes=56 * 2**20),
        cost_estimate=pl.CostEstimate(
            flops=2 * rows * width * ff * 2,
            bytes_accessed=2 * 2 * width * ff + 2 * rows * width,
            transcendentals=0,
        ),
        name="rowgrad",
    )(h, wg, wu)


def gather_kernel(slot, prob, xi, yi, blocks, out_ref, cat, xs, ys):
    i, j = pl.program_id(0), pl.program_id(1)
    total, wide = xi.shape
    chips, chunks, toks = blocks.shape[0], blocks.shape[1], blocks.shape[4]
    rows = total // chunks

    @pl.when((i == 0) & (j == 0))
    def _():
        xs[0:total] = xi[...]
        ys[0:total] = yi[...]

    @pl.when((i > 0) | (j > 0))
    def _():
        for k in range(chunks):
            slots = slot[0, k]
            hot = one_hot(slots, rows)
            scale = row_probs(slots, prob[0, k], rows)
            at = pl.ds(pl.multiple_of(j * total + k * rows, rows), rows)
            for n in range(chips):
                cat[toks * n : toks * (n + 1), :] = blocks[n, k, 0, 0]
            xs[at, :] = dot(hot, cat[...]).astype(BF16)
            for n in range(chips):
                cat[toks * n : toks * (n + 1), :] = blocks[n, k, 0, 1]
            ys[at, :] = (dot(hot, cat[...]) * scale).astype(BF16)

    @pl.when(j == 1)
    def _():
        out_ref[0:wide] = xs[...].T
        out_ref[wide:] = ys[...].T


def gather_columns(slot, prob, xi, yi, blocks):
    total, wide = xi.shape
    chips, chunks, _, _, toks, _ = blocks.shape
    meta = pl.BlockSpec((1, chunks, 1, chips * toks), lambda i, j: (2 * i + j, 0, 0, 0))
    return pl.pallas_call(
        gather_kernel,
        grid=(2, 2),
        in_specs=[
            meta, meta, whole(xi), whole(yi),
            pl.BlockSpec(
                (chips, chunks, 1, 2, toks, wide),
                lambda i, j: (0, 0, jnp.maximum(2 * i + j - 1, 0), 0, 0, 0),
            ),
        ],
        out_specs=pl.BlockSpec((2 * wide, 2 * total), lambda i, j: (0, i)),
        scratch_shapes=[
            pltpu.VMEM((chips * toks, wide), BF16),
            pltpu.VMEM((2 * total, wide), BF16),
            pltpu.VMEM((2 * total, wide), BF16),
        ],
        out_shape=jax.ShapeDtypeStruct((2 * wide, 4 * total), BF16),
        compiler_params=pltpu.CompilerParams(vmem_limit_bytes=56 * 2**20),
        cost_estimate=LIGHT,
        name="gather_columns",
    )(slot, prob, xi, yi, blocks)


def weight_kernel(xy, *refs, count):
    outs, cat = refs[-1 - count : -1], refs[-1]
    m = pl.program_id(0)
    at = 0
    for h in refs[: -1 - count]:
        if h.ndim == 3:
            cat[at : at + h.shape[1], :] = h[0]
            at += h.shape[1]
        else:
            cat[at : at + h.shape[0], :] = h[...]
            at += h.shape[0]
    res = dot(xy[...], cat[...]).astype(BF16)
    for i, out in enumerate(outs):

        @pl.when(m == i)
        def _():
            out[...] = res if out.shape == res.shape else res.T


def weights(xy, side, hs, count, flip):
    wide, depth = xy.shape[0] // 2, xy.shape[1]
    ff = hs[0][0].shape[-1]
    shape = (ff, wide) if flip else (wide, ff)

    def spec(block):
        array, rows, index = block
        if array.ndim == 3:
            return pl.BlockSpec((1, rows, ff), lambda m: (index(m), 0, 0))
        return pl.BlockSpec((rows, ff), lambda m: (index(m), 0))

    return pl.pallas_call(
        functools.partial(weight_kernel, count=count),
        grid=(count,),
        in_specs=[pl.BlockSpec((wide, depth), lambda m: (side, 0))] + [spec(h) for h in hs],
        out_specs=[pl.BlockSpec(shape, lambda m: (0, 0))] * count,
        scratch_shapes=[pltpu.VMEM((depth, ff), BF16)],
        out_shape=[jax.ShapeDtypeStruct(shape, BF16)] * count,
        compiler_params=pltpu.CompilerParams(vmem_limit_bytes=56 * 2**20),
        cost_estimate=pl.CostEstimate(
            flops=HEAVY * 2 * depth * wide * ff * count, bytes_accessed=depth * (2 * wide + 2 * ff * count), transcendentals=0
        ),
        name="weight_grads",
    )(xy, *(h for h, _, _ in hs))


def on_device(tokens, out_grad, expert_ids, route_probs, w_gate, w_up, w_down):
    toks, width = tokens.shape
    topk = expert_ids.shape[1]
    groups = lax.axis_size("expert")
    cap = 3 * toks * topk // (2 * groups)
    wg, wu, wd = w_gate[0], w_up[0], w_down[0]
    ff = wg.shape[1]
    rows = 16 * cap
    grp = lax.axis_index("dp")
    expert = lax.axis_index("expert")
    z, x, core = expert // 8, (expert // 2) % 4, expert % 2
    first = core == 0
    place = jnp.stack([core, grp]).astype(jnp.int32)
    both = jnp.stack([tokens, out_grad])

    def by_core(v):
        half = v.shape[-1] // 2
        mine = lax.dynamic_slice_in_dim(v, core * half, half, v.ndim - 1)
        other = lax.dynamic_slice_in_dim(v, (1 - core) * half, half, v.ndim - 1)
        got = swap_core(other)
        return jnp.where(first, mine, got), jnp.where(first, got, mine)

    named = expert_ids[:, :, None] == jnp.arange(groups, dtype=jnp.int32)
    chosen = jnp.any(named, axis=1)
    weight = jnp.sum(jnp.where(named, route_probs[:, :, None], 0.0), axis=1)
    lower = jnp.tril(jnp.ones((toks, toks), BF16), -1)
    rank = jnp.where(chosen, dot(lower, chosen.astype(BF16)), -1000.0)
    mine = jnp.stack(by_core(both), axis=1)
    blocks = (mine, *near(mine, 1), step(mine, 1, 2))
    col_x, col_y = (jnp.concatenate([b[v] for b in blocks], axis=-2) for v in (0, 1))

    meta = lax.all_to_all(jnp.stack([rank.T, weight.T], axis=1), "expert", 0, 0, tiled=True)
    col_x, col_y = after((col_x, col_y), meta)
    prev_x, succ_x = near(col_x, 2)

    quarter = width // 4
    part0 = lax.reduce_precision(meta[:, 1], 8, 7)
    part1 = lax.reduce_precision(meta[:, 1] - part0, 8, 7)
    part2 = meta[:, 1] - part0 - part1
    words = jnp.stack([meta[:, 0], part0, part1, part2]).astype(BF16)
    lines = words.size // quarter
    words = words.reshape(lines, quarter)
    cols, tables = [], [meta]
    for g in (1, 2, 3):
        r = 4 - g
        part = lax.dynamic_slice_in_dim(after(both, col_x), ((grp + r) % 4) * quarter, quarter, 2)
        part = jnp.concatenate([part.reshape(2 * toks, quarter), words])
        got = over_groups(part, r)
        cols.append(got[: 2 * toks])
        got = got[2 * toks :].reshape(4, groups, toks).astype(F32)
        tables.append(jnp.stack([got[0], got[1] + got[2] + got[3]], axis=1))
    cols = jnp.concatenate(cols)
    tables = jnp.stack(tables).reshape(4, 16, 2, 2, toks)
    base = cap * jnp.arange(16, dtype=jnp.int32)[:, None]
    slots = (tables[:, :, :, 0].astype(jnp.int32) + base[None, :, None]).swapaxes(1, 2)
    slots = slots.reshape(4, 2, 1, 16 * toks)
    probs = tables[:, :, :, 1].swapaxes(1, 2).reshape(4, 2, 1, 16 * toks)

    ready = lambda v: after(v, sib_x, cols)
    sib_x = swap_core(col_x)
    up = step(ready(jnp.concatenate([prev_x[:1], col_y])), 2, 1)
    down = step(ready(jnp.concatenate([succ_x[1:], col_y])), 2, -1)
    far_y = step(up[1:2], 2, 1), step(down[2:], 2, -1)

    def blocks_x(col, prev, succ, up, down):
        return [(col, 0), (prev, 0), (succ, 0), (up, 0), (col, 1), (prev, 1), (succ, 1), (down, 0)]

    def blocks_y(col, up, down, far0, far1):
        return [(col, 0), (up, 1), (down, 1), (far0, 0), (col, 1), (up, 2), (down, 2), (far1, 0)]

    sib_up, sib_down = swap_core(up), swap_core(down)
    own_x = blocks_x(col_x, prev_x, succ_x, up, down)
    sib_x = blocks_x(sib_x, swap_core(prev_x), swap_core(succ_x), sib_up, sib_down)
    own_y = blocks_y(col_y, up, down, *far_y)

    table = meta.reshape(16, 2, 2, toks)
    offs = jnp.array(OFFSETS, jnp.int32)
    r2, r1 = offs[:, None], offs[None, :]
    bz = jnp.where(first, z + r1, z + r2) % 4
    bx = jnp.where(first, x + r2, x + r1) % 4
    chip = bz * 4 + bx
    order = jnp.concatenate([chip.reshape(16), chip.T.reshape(16)])
    local = table[order].reshape(2, 16, 2, 2, toks)
    local_slots = local[:, :, :, 0].astype(jnp.int32) + (cap * order).reshape(2, 16, 1, 1)
    local_slots = local_slots.swapaxes(1, 2).reshape(2, 2, 1, 16 * toks)
    local_probs = local[0, :, :, 1].swapaxes(0, 1).reshape(2, 1, 16 * toks)

    cols = lax.all_gather(after(cols, up, down), "expert", tiled=True)
    cols = cols.reshape(16, 2, 3, 2, toks, quarter)

    hid, sg, slope, xi = hidden_rows(
        place, local_slots[0], local_slots[1], own_x, sib_x, wg, wu, rows
    )
    hid_prev, hid_succ = over_groups(hid, 1), over_groups(hid, -1)
    sib_far = [swap_core(after(b, hid)) for b in far_y]
    sib_y = blocks_y(swap_core(col_y), sib_up, sib_down, *sib_far)
    dd, yi = cotangent_rows(
        after(place, hid), local_slots[0], local_slots[1], local_probs, own_y, sib_y, wd, sg, slope, rows
    )

    half = hid.shape[0] // 2
    flat = dd.reshape(-1, ff)
    from_prev = over_groups(jnp.concatenate([hid_prev[:half], flat]), 1)
    from_succ = over_groups(jnp.concatenate([hid_succ[half:], flat]), -1)
    grad = rowgrad(dd, wg, wu, cap)
    xy = gather_columns(after(slots, grad), probs, xi, yi, cols)
    far_gate = over_groups(after(from_prev, xy)[half : 3 * half], 1)
    far_up = over_groups(after(from_succ, xy)[3 * half :], -1)

    back = lax.all_to_all(grad, "expert", 0, 0, tiled=True)
    at = lambda i: lambda m: i
    hids = [(hid, 2 * half, at(0)), (hid_succ, 2 * half, at(0)), (from_prev, half, at(0)),
            (from_succ, half, at(0)), (hid_prev, 2 * half, at(0))]
    (down_grad,) = weights(xy, 1, hids, 1, True)
    far_dd = jnp.stack(after((far_gate, far_up), down_grad))
    first_half, second_half = (lambda m: 1 + 2 * m), (lambda m: 2 + 2 * m)
    dds = [(dd, 2 * half, lambda m: m), (from_succ, half, first_half), (from_succ, half, second_half),
           (far_dd, 2 * half, lambda m: m), (from_prev, half, first_half), (from_prev, half, second_half)]
    gate_grad, up_grad = weights(xy, 0, dds, 2, False)
    back = after(back, gate_grad)
    piece = cap * jnp.arange(4, dtype=F32)
    pick = after(rank, xy) + piece[:, None, None]
    pick = pick[..., None] == jnp.arange(4 * cap, dtype=F32)
    pick = pick.astype(BF16).reshape(4 * toks, groups * 4 * cap)
    token_grad = dot(pick, back.reshape(groups * 4 * cap, quarter)).astype(BF16)
    token_grad = token_grad.reshape(4, toks, quarter).swapaxes(0, 1).reshape(toks, width)

    return token_grad, gate_grad[None], up_grad[None], down_grad[None]


def solution(mesh):
    in_specs = (
        P(("dp", "expert"), None),
        P(("dp", "expert"), None),
        P(("dp", "expert"), None),
        P(("dp", "expert"), None),
        P("expert", None, None),
        P("expert", None, None),
        P("expert", None, None),
    )
    out_specs = (
        P(("dp", "expert"), None),
        P("expert", "dp", None),
        P("expert", "dp", None),
        P("expert", None, "dp"),
    )
    return jax.shard_map(
        on_device, mesh=mesh, in_specs=in_specs, out_specs=out_specs, check_vma=False
    )
```

time: 300 us -> 269 us (0.90)
  waiting for transfers between devices: 127 us -> 68.6 us
  Pallas kernels: 77.8 us -> 94.5 us
  other arithmetic: 6.99 us -> 13.5 us
  starting transfers between devices: 43.1 us -> 48.6 us
    all_gather x2 -> x1, waiting for transfers between devices: 32.2 us -> 0.02 us  [on_device(): cols = lax.all_gather(after(cols, up, down), 'expert', tiled=True)]
    ppermute x10 -> x9, waiting for transfers between devices: 46.3 us -> 24.7 us  [over_groups(): return lax.ppermute(v, 'dp', [(s, (s + shift) % 4) for s in range(4)])]
    pallas_call x2 -> x4, Pallas kernels: 50.4 us -> 63 us  [the longest x2 21.9 us: weights(): pl.pallas_call(functools.partial(weight_kernel, count=count), grid=(count...]
    ppermute x6 -> x9, waiting for transfers between devices: 13.7 us -> 6.18 us  [swap_core(): return lax.ppermute(v, 'expert', [(e, e ^ 1) for e in range(32)])]
    unnamed x23 -> x30, local copies, waits for them, and re-layouts: 9.61 us -> 3.43 us
    all_to_all x1 -> x2, starting transfers between devices: 7.42 us -> 13.6 us  [the longest x1 7.68 us: on_device(): lax.all_to_all(jnp.stack([rank.T, weight.T], axis=1), 'expert', 0, 0, til...]
    pallas_call x1, Pallas kernels: 11.1 us -> 14.4 us  [rowgrad(): pl.pallas_call(functools.partial(rowgrad_kernel, cap=cap), grid=(4,), in_...]
    ppermute x7 -> x9, waiting for transfers between devices: 34.8 us -> 37.7 us  [step(): return lax.ppermute(v, 'expert', expert_pairs(ring, shift))]
  transfers between devices with their start and end apart: 26 -> 30, of which waited for: 16 -> 12; matrix products, arithmetic and copies ran while one was open for 6% -> 11% of each run, Pallas kernels for 26% -> 36%
where the time goes in v3:
time: 269 us; the launch traced here: 265 us
  Pallas kernels  94.5 us (35%)
  waiting for transfers between devices  68.6 us (26%)
  starting transfers between devices  48.6 us (18%)
  local copies, waits for them, and re-layouts  22 us (8%)
  between operations  14.6 us (5%)
  other arithmetic  13.5 us (5%)
  matrix products  3.61 us (1%)
    ppermute x9, waiting for transfers between devices, step(): return lax.ppermute(v, 'expert', expert_pairs(ring, shift))  37.7 us
    ppermute x9, waiting for transfers between devices, over_groups(): return lax.ppermute(v, 'dp', [(s, (s + shift) % 4) for s in range(4)])  24.7 us
    pallas_call x2, Pallas kernels, weights(): pl.pallas_call(functools.partial(weight_kernel, count=count), grid=(count...  21.9 us
    pallas_call x1, Pallas kernels, hidden_rows(): pl.pallas_call(functools.partial(hidden_kernel, half=half), grid_spec=plt...  21.9 us
    pallas_call x1, Pallas kernels, cotangent_rows(): pl.pallas_call(functools.partial(cotangent_kernel, half=half), grid_spec=...  19.3 us
    pallas_call x1, Pallas kernels, gather_columns(): pl.pallas_call(gather_kernel, grid=(2, 2), in_specs=[meta, meta, whole(xi...  17.2 us
    pallas_call x1, Pallas kernels, rowgrad(): pl.pallas_call(functools.partial(rowgrad_kernel, cap=cap), grid=(4,), in_...  14.4 us
    ppermute x9, starting transfers between devices, over_groups(): return lax.ppermute(v, 'dp', [(s, (s + shift) % 4) for s in range(4)])  13.7 us
  transfers between devices with their start and end apart: 30, of which 12 were waited for; matrix products, arithmetic and copies ran while one was open for 11% of the time, Pallas kernels for 36%

profile of v3, /device:TPU:1, one launch (start us, length us, event | category | flops | bytes accessed | tf_op | source)
XLA Modules:
  0.0 265.5 jit_solution(13001175955974564558)
XLA Ops:
  7.2 1.1 fusion.5
  8.3 1.5 collective-permute-start
  11.1 1.4 select_bitcast_fusion.1
  12.6 2.9 %collective-permute-start.3 = (bf16[2,2,48,2048]{3,2,1,0:T(8,128)(2,1)S(1)}, bf16[2,2,48,2048]{3,2,1,0:T(8,128)(2,1)S(1)}, u32[]{:S(2)}, u32[]{:S(2)}) collective-permute-start(bf16[2,2,48,2048]{3,2,1,0:T(8,128)(2,1)S(1)} %pad_maximum_fusion.8), channel_id=1, source_target_pairs={{0,16},{1,5},{2,18},{3,7},{4,20},{5,1},{6,22},{7,3},{8,24},{9,13},... | collective-permute-start | bytes 2359304 | tf_op jit(solution)/shard_map/ppermute | solution.py:42
  17.3 7.7 %all-to-all-start = ((f32[32,2,48]{2,1,0:T(2,128)}), f32[32,2,48]{2,1,0:T(2,128)}, u32[]{:S(2)}, u32[]{:S(2)}) async-start(f32[32,2,48]{2,1,0:T(2,128)} %copy.45), calls=%async_computation | async-start | bytes 65536 | tf_op jit(solution)/shard_map/all_to_all | solution.py:418
  25.0 1.5 collective-permute-start.1
  26.6 7.5 %collective-permute-done.2 = bf16[2,2,48,2048]{3,2,1,0:T(8,128)(2,1)S(1)} collective-permute-done((bf16[2,2,48,2048]{3,2,1,0:T(8,128)(2,1)S(1)}, bf16[2,2,48,2048]{3,2,1,0:T(8,128)(2,1)S(1)}, u32[]{:S(2)}, u32[]{:S(2)}) %collective-permute-start.2) | collective-permute-done | bytes 786464 | tf_op jit(solution)/shard_map/ppermute | solution.py:42
  34.2 3.6 %collective-permute-done.1 = bf16[2,2,48,2048]{3,2,1,0:T(8,128)(2,1)S(1)} collective-permute-done((bf16[2,2,48,2048]{3,2,1,0:T(8,128)(2,1)S(1)}, bf16[2,2,48,2048]{3,2,1,0:T(8,128)(2,1)S(1)}, u32[]{:S(2)}, u32[]{:S(2)}) %collective-permute-start.1) | collective-permute-done | bytes 786464 | tf_op jit(solution)/shard_map/ppermute | solution.py:42
  38.2 1.0 collective-permute-start.7
  39.2 1.7 collective-permute-start.8
  40.9 1.9 pad_maximum_fusion.7
  43.6 1.6 collective-permute-start.9
  46.2 1.2 constant_dynamic-slice_fusion.2
  47.4 1.4 collective-permute-start.6
  48.8 2.6 collective-permute-start.5
  51.4 4.4 %collective-permute-done.6 = bf16[102,1024]{1,0:T(8,128)(2,1)S(1)} collective-permute-done((bf16[102,1024]{1,0:T(8,128)(2,1)S(1)}, bf16[102,1024]{1,0:T(8,128)(2,1)S(1)}, u32[]{:S(2)}, u32[]{:S(2)}) %collective-permute-start.6) | collective-permute-done | bytes 208928 | tf_op jit(solution)/shard_map/ppermute | solution.py:58
  55.8 1.4 collective-permute-start.4
  57.3 4.1 %collective-permute-done.5 = bf16[102,1024]{1,0:T(8,128)(2,1)S(1)} collective-permute-done((bf16[102,1024]{1,0:T(8,128)(2,1)S(1)}, bf16[102,1024]{1,0:T(8,128)(2,1)S(1)}, u32[]{:S(2)}, u32[]{:S(2)}) %collective-permute-start.5) | collective-permute-done | bytes 208928 | tf_op jit(solution)/shard_map/ppermute | solution.py:58
  63.0 1.2 slice.212
  64.2 1.2 slice.208
  66.0 2.5 collective-permute-start.11
  68.5 26.5 %collective-permute-done.10.refs_3_.refs_1_.refs_5_ = bf16[3,192,2048]{2,1,0:T(8,128)(2,1)S(1)} collective-permute-done((bf16[3,192,2048]{2,1,0:T(8,128)(2,1)S(1)}, bf16[3,192,2048]{2,1,0:T(8,128)(2,1)S(1)}, u32[]{:S(2)}, u32[]{:S(2)}) %collective-permute-start.10) | collective-permute-done | bytes 2359328 | tf_op jit(solution)/shard_map/ppermute | solution.py:42
  95.1 2.4 collective-permute-start.14
  99.6 1.4 gather_fusion
  102.9 1.2 slice.215
  104.1 3.5 %collective-permute-done.12.refs_9_.refs_13_ = bf16[2,192,2048]{2,1,0:T(8,128)(2,1)} collective-permute-done((bf16[2,192,2048]{2,1,0:T(8,128)(2,1)}, bf16[2,192,2048]{2,1,0:T(8,128)(2,1)}, u32[]{:S(2)}, u32[]{:S(2)}) %collective-permute-start.12) | collective-permute-done | bytes 1572896 | tf_op jit(solution)/shard_map/ppermute | solution.py:46
  107.7 2.1 collective-permute-done.13.refs_10_.refs_14_
  109.8 1.4 collective-permute-start.17
  111.3 21.9 %hidden_rows.1 = (bf16[576,768]{1,0:T(8,128)(2,1)}, f32[576,768]{1,0:T(8,128)}, f32[576,768]{1,0:T(8,128)}, bf16[576,1024]{1,0:T(8,128)(2,1)}) custom-call(s32[2]{0:T(128)} %pad_add_fusion.place, s32[2,1,768]{2,1,0:T(1,128)} %squeeze.72.slot_own, s32[2,1,768]{2,1,0:T(1,128)} %squeeze.73.slot_sib, bf16[2,192,2048]{2,1,0:T(8,128)(2,1)} %copy-done.2, ...), custom_call_target="tpu_custom_call" | custom-call | flops 10871635968 | bytes 25165824 | tf_op jit(solution)/shard_map/hidden_rows/pallas_call | solution.py:183
  133.1 2.4 collective-permute-start.19
  137.1 3.0 %collective-permute-start.23 = (bf16[576,768]{1,0:T(8,128)(2,1)}, bf16[576,768]{1,0:T(8,128)(2,1)S(1)}, u32[]{:S(2)}, u32[]{:S(2)}) collective-permute-start(bf16[576,768]{1,0:T(8,128)(2,1)} %get-tuple-element.33.refs_0_), channel_id=1, source_target_pairs={{0,32},{32,64},{64,96},{96,0},{1,33},{33,65},{65,97},{97,1},{2,34}... | collective-permute-start | bytes 2654216 | tf_op jit(solution)/shard_map/ppermute | solution.py:58
  142.3 19.3 %cotangent_rows.1 = (bf16[2,576,768]{2,1,0:T(8,128)(2,1)}, bf16[576,1024]{1,0:T(8,128)(2,1)}) custom-call(s32[2]{0:T(128)} %pad_add_fusion.place, s32[2,1,768]{2,1,0:T(1,128)} %squeeze.72.slot_own, s32[2,1,768]{2,1,0:T(1,128)} %squeeze.73.slot_sib, f32[2,1,768]{2,1,0:T(1,128)} %reshape.610.prob, bf16[2,192,2048]{2,1,0:T(8,128)(2,1)} %copy-done.1, ...), custom_call_target="tpu_custom_call" | custom-call | flops 7247757312 | bytes 18874368 | tf_op jit(solution)/shard_map/cotangent_rows/pallas_call | solution.py:217
  161.7 2.2 copy-done.4
  163.9 1.7 pad_maximum_fusion.3
  165.5 2.3 collective-permute-start.22
  169.7 14.4 %rowgrad.1 = bf16[32,72,1024]{2,1,0:T(8,128)(2,1)} custom-call(bf16[2,576,768]{2,1,0:T(8,128)(2,1)} %get-tuple-element.39.h.refs_0_, bf16[4096,768]{1,0:T(8,128)(2,1)} %bitcast.120, bf16[4096,768]{1,0:T(8,128)(2,1)} %bitcast.122), custom_call_target="tpu_custom_call" | custom-call | flops 7247757312 | bytes 17301504 | tf_op jit(solution)/shard_map/rowgrad/pallas_call | solution.py:267
  184.1 5.9 %all-to-all-start.1 = ((bf16[32,72,1024]{2,1,0:T(8,128)(2,1)}), bf16[32,72,1024]{2,1,0:T(8,128)(2,1)}, u32[]{:S(2)}, u32[]{:S(2)}) async-start(bf16[32,72,1024]{2,1,0:T(8,128)(2,1)} %rowgrad.1), calls=%async_computation.1 | async-start | bytes 9437184 | tf_op jit(solution)/shard_map/all_to_all | solution.py:496
  190.0 17.2 %gather_columns.1.xy = bf16[2048,2304]{1,0:T(8,128)(2,1)} custom-call(s32[4,2,1,768]{3,2,1,0:T(1,128)} %reshape.607.slot, f32[4,2,1,768]{3,2,1,0:T(1,128)} %reshape.611.prob, bf16[576,1024]{1,0:T(8,128)(2,1)} %get-tuple-element.41.xi, bf16[576,1024]{1,0:T(8,128)(2,1)} %get-tuple-element.42.yi, bf16[16,2,3,2,48,1024]{5,4,3,2,1,0:T(8,128)(2,1)} %bitcast.117), custom_call_target="tpu_custom_call" | custom-call | flops 1 | bytes 1 | tf_op jit(solution)/shard_map/gather_columns/pallas_call | solution.py:319
  208.3 2.1 eq.55
  210.4 7.3 %collective-permute-done.24.refs_2_.refs_4_.refs_5_ = bf16[1440,768]{1,0:T(8,128)(2,1)} collective-permute-done((bf16[1440,768]{1,0:T(8,128)(2,1)}, bf16[1440,768]{1,0:T(8,128)(2,1)}, u32[]{:S(2)}, u32[]{:S(2)}) %collective-permute-start.24) | collective-permute-done | bytes 2211872 | tf_op jit(solution)/shard_map/ppermute | solution.py:58
  217.8 1.2 slice.173
  219.1 1.2 slice.174
  220.3 2.7 %collective-permute-start.26 = (bf16[576,768]{1,0:T(8,128)(2,1)S(1)}, bf16[576,768]{1,0:T(8,128)(2,1)S(1)}, u32[]{:S(2)}, u32[]{:S(2)}) collective-permute-start(bf16[576,768]{1,0:T(8,128)(2,1)S(1)} %slice.174), channel_id=1, source_target_pairs={{0,96},{32,0},{64,32},{96,64},{1,97},{33,1},{65,33},{97,65},{2,98}... | collective-permute-start | bytes 2654216 | tf_op jit(solution)/shard_map/ppermute | solution.py:58
  223.0 8.4 %weight_grads.2 = bf16[768,1024]{1,0:T(8,128)(2,1)} custom-call(bf16[2048,2304]{1,0:T(8,128)(2,1)} %gather_columns.1.xy, bf16[576,768]{1,0:T(8,128)(2,1)} %get-tuple-element.33.refs_0_, bf16[576,768]{1,0:T(8,128)(2,1)} %copy-done.9, bf16[1440,768]{1,0:T(8,128)(2,1)} %collective-permute-done.24.refs_2_.refs_4_.refs_5_, ...), custom_call_target="tpu_custom_call" | custom-call | flops 14495514624 | bytes 8257536 | tf_op jit(solution)/shard_map/weight_grads/pallas_call | solution.py:372
  231.4 8.0 %collective-permute-done.25 = bf16[576,768]{1,0:T(8,128)(2,1)S(1)} collective-permute-done((bf16[576,768]{1,0:T(8,128)(2,1)S(1)}, bf16[576,768]{1,0:T(8,128)(2,1)S(1)}, u32[]{:S(2)}, u32[]{:S(2)}) %collective-permute-start.25) | collective-permute-done | bytes 884768 | tf_op jit(solution)/shard_map/ppermute | solution.py:58
  239.6 1.4 pad_maximum_fusion.4.refs_3_
  240.9 13.5 %weight_grads.3 = (bf16[1024,768]{1,0:T(8,128)(2,1)}, bf16[1024,768]{1,0:T(8,128)(2,1)}) custom-call(bf16[2048,2304]{1,0:T(8,128)(2,1)} %gather_columns.1.xy, bf16[2,576,768]{2,1,0:T(8,128)(2,1)} %get-tuple-element.39.h.refs_0_, bf16[1440,768]{1,0:T(8,128)(2,1)} %collective-permute-done.22.refs_3_.refs_1_.refs_2_, ...), custom_call_target="tpu_custom_call" | custom-call | flops 28991029248 | bytes 11796480 | tf_op jit(solution)/shard_map/weight_grads/pallas_call | solution.py:372
  254.4 3.4 %convolution_convert_fusion = bf16[192,1024]{1,0:T(8,128)(2,1)S(1)} fusion(pred[192,2304]{1,0:T(32,128)(4,1)S(1)} %eq.55, bf16[2304,1024]{1,0:T(8,128)(2,1)} %bitcast.51), kind=kOutput, calls=%fused_computation.9 | convolution fusion | flops 906166272 | bytes 5554176 | tf_op jit(solution)/shard_map/dot_general | solution.py:22
  (136 shorter events, 19.6 us)
Async XLA Ops:
  7.2 8.3 %copy-start.12 = (s32[48,8]{0,1:T(8,128)S(1)}, s32[48,8]{0,1:T(8,128)}, u32[]{:S(2)}) copy-start(s32[48,8]{0,1:T(8,128)} %param.10) | copy-start | bytes 4612
  7.2 8.3 %copy-start.13 = (f32[48,8]{0,1:T(8,128)S(1)}, f32[48,8]{0,1:T(8,128)}, u32[]{:S(2)}) copy-start(f32[48,8]{0,1:T(8,128)} %param.11) | copy-start | bytes 4612
  8.3 2.9 %collective-permute-start = (bf16[2,48,2048]{2,1,0:T(8,128)(2,1)S(1)}, bf16[2,48,2048]{2,1,0:T(8,128)(2,1)S(1)}, u32[]{:S(2)}, u32[]{:S(2)}) collective-permute-start(bf16[2,48,2048]{2,1,0:T(8,128)(2,1)S(1)} %fusion.5), channel_id=1, source_target_pairs={{0,1},{1,0},{2,3},{3,2},{4,5},{5,4},{6,7},{7,6},{8,9},{9,8},{10,11... | collective-permute-start | bytes 1179656 | tf_op jit(solution)/shard_map/ppermute | solution.py:46
  12.6 13.9 %collective-permute-start.3 = (bf16[2,2,48,2048]{3,2,1,0:T(8,128)(2,1)S(1)}, bf16[2,2,48,2048]{3,2,1,0:T(8,128)(2,1)S(1)}, u32[]{:S(2)}, u32[]{:S(2)}) collective-permute-start(bf16[2,2,48,2048]{3,2,1,0:T(8,128)(2,1)S(1)} %pad_maximum_fusion.8), channel_id=1, source_target_pairs={{0,16},{1,5},{2,18},{3,7},{4,20},{5,1},{6,22},{7,3},{8,24},{9,13},... | collective-permute-start | bytes 2359304 | tf_op jit(solution)/shard_map/ppermute | solution.py:42
  15.8 18.4 %collective-permute-start.2 = (bf16[2,2,48,2048]{3,2,1,0:T(8,128)(2,1)S(1)}, bf16[2,2,48,2048]{3,2,1,0:T(8,128)(2,1)S(1)}, u32[]{:S(2)}, u32[]{:S(2)}) collective-permute-start(bf16[2,2,48,2048]{3,2,1,0:T(8,128)(2,1)S(1)} %pad_maximum_fusion.8), channel_id=1, source_target_pairs={{0,24},{1,7},{2,26},{3,1},{4,28},{5,3},{6,30},{7,5},{8,0},{9,15},{... | collective-permute-start | bytes 2359304 | tf_op jit(solution)/shard_map/ppermute | solution.py:42
  17.3 20.9 %all-to-all-start = ((f32[32,2,48]{2,1,0:T(2,128)}), f32[32,2,48]{2,1,0:T(2,128)}, u32[]{:S(2)}, u32[]{:S(2)}) async-start(f32[32,2,48]{2,1,0:T(2,128)} %copy.45), calls=%async_computation | async-start | bytes 65536 | tf_op jit(solution)/shard_map/all_to_all | solution.py:418
  25.0 165.0 %all-gather.2.cloned.1.call-start = ((), (), s32[]{:S(2)}) async-start(), calls=%async_computation.2 | async-start | bytes 19464192 | tf_op jit(solution)/shard_map/all_gather | solution.py:474
  25.0 12.8 %collective-permute-start.1 = (bf16[2,2,48,2048]{3,2,1,0:T(8,128)(2,1)S(1)}, bf16[2,2,48,2048]{3,2,1,0:T(8,128)(2,1)S(1)}, u32[]{:S(2)}, u32[]{:S(2)}) collective-permute-start(bf16[2,2,48,2048]{3,2,1,0:T(8,128)(2,1)S(1)} %pad_maximum_fusion.8), channel_id=1, source_target_pairs={{0,8},{1,3},{2,10},{3,5},{4,12},{5,7},{6,14},{7,1},{8,16},{9,11},{... | collective-permute-start | bytes 2359304 | tf_op jit(solution)/shard_map/ppermute | solution.py:42
  37.8 3.1 %copy-start.3 = (bf16[48,4096]{1,0:T(8,128)(2,1)S(1)}, bf16[48,4096]{1,0:T(8,128)(2,1)}, u32[]{:S(2)}) copy-start(bf16[48,4096]{1,0:T(8,128)(2,1)} %param.8) | copy-start | bytes 1179652
  38.2 19.1 %copy-start.2 = (bf16[2,192,2048]{2,1,0:T(8,128)(2,1)}, bf16[2,192,2048]{2,1,0:T(8,128)(2,1)S(1)}, u32[]{:S(2)}) copy-start(bf16[2,192,2048]{2,1,0:T(8,128)(2,1)S(1)} %get-tuple-element.28.refs_0_.refs_4_) | copy-start | bytes 4718596
  38.2 27.2 %copy-start.1 = (bf16[2,192,2048]{2,1,0:T(8,128)(2,1)}, bf16[2,192,2048]{2,1,0:T(8,128)(2,1)S(1)}, u32[]{:S(2)}) copy-start(bf16[2,192,2048]{2,1,0:T(8,128)(2,1)S(1)} %get-tuple-element.30.refs_0_.refs_4_) | copy-start | bytes 4718596
  38.2 26.0 %collective-permute-start.7 = (bf16[2,192,2048]{2,1,0:T(8,128)(2,1)S(1)}, bf16[2,192,2048]{2,1,0:T(8,128)(2,1)}, u32[]{:S(2)}, u32[]{:S(2)}) collective-permute-start(bf16[2,192,2048]{2,1,0:T(8,128)(2,1)S(1)} %get-tuple-element.28.refs_0_.refs_4_), channel_id=1, source_target_pairs={{0,2},{1,9},{2,4},{3,11},{4,6},{5,13},{6,0},{7,15},{8,10},{9,17},{... | collective-permute-start | bytes 4718600 | tf_op jit(solution)/shard_map/ppermute | solution.py:42
  39.2 23.7 %collective-permute-start.8 = (bf16[2,192,2048]{2,1,0:T(8,128)(2,1)S(1)}, bf16[2,192,2048]{2,1,0:T(8,128)(2,1)}, u32[]{:S(2)}, u32[]{:S(2)}) collective-permute-start(bf16[2,192,2048]{2,1,0:T(8,128)(2,1)S(1)} %get-tuple-element.28.refs_0_.refs_4_), channel_id=1, source_target_pairs={{0,6},{1,25},{2,0},{3,27},{4,2},{5,29},{6,4},{7,31},{8,14},{9,1},{... | collective-permute-start | bytes 4718600 | tf_op jit(solution)/shard_map/ppermute | solution.py:42
  43.6 22.1 %collective-permute-start.9 = (bf16[2,192,2048]{2,1,0:T(8,128)(2,1)S(1)}, bf16[2,192,2048]{2,1,0:T(8,128)(2,1)}, u32[]{:S(2)}, u32[]{:S(2)}) collective-permute-start(bf16[2,192,2048]{2,1,0:T(8,128)(2,1)S(1)} %get-tuple-element.28.refs_0_.refs_4_), channel_id=1, source_target_pairs={{0,1},{1,0},{2,3},{3,2},{4,5},{5,4},{6,7},{7,6},{8,9},{9,8},{10,11... | collective-permute-start | bytes 4718600 | tf_op jit(solution)/shard_map/ppermute | solution.py:46
  47.4 8.4 %collective-permute-start.6 = (bf16[102,1024]{1,0:T(8,128)(2,1)S(1)}, bf16[102,1024]{1,0:T(8,128)(2,1)S(1)}, u32[]{:S(2)}, u32[]{:S(2)}) collective-permute-start(bf16[102,1024]{1,0:T(8,128)(2,1)S(1)} %get-tuple-element.79), channel_id=1, source_target_pairs={{0,32},{32,64},{64,96},{96,0},{1,33},{33,65},{65,97},{97,1},{2,34}... | collective-permute-start | bytes 626696 | tf_op jit(solution)/shard_map/ppermute | solution.py:58
  48.8 12.6 %collective-permute-start.5 = (bf16[102,1024]{1,0:T(8,128)(2,1)S(1)}, bf16[102,1024]{1,0:T(8,128)(2,1)S(1)}, u32[]{:S(2)}, u32[]{:S(2)}) collective-permute-start(bf16[102,1024]{1,0:T(8,128)(2,1)S(1)} %get-tuple-element.78), channel_id=1, source_target_pairs={{0,64},{32,96},{64,0},{96,32},{1,65},{33,97},{65,1},{97,33},{2,66}... | collective-permute-start | bytes 626696 | tf_op jit(solution)/shard_map/ppermute | solution.py:58
  55.8 6.2 %copy-start.11 = (bf16[102,1024]{1,0:T(8,128)(2,1)}, bf16[102,1024]{1,0:T(8,128)(2,1)S(1)}, u32[]{:S(2)}) copy-start(bf16[102,1024]{1,0:T(8,128)(2,1)S(1)} %collective-permute-done.6) | copy-start | bytes 626692
  55.8 6.2 %collective-permute-start.4 = (bf16[102,1024]{1,0:T(8,128)(2,1)S(1)}, bf16[102,1024]{1,0:T(8,128)(2,1)S(1)}, u32[]{:S(2)}, u32[]{:S(2)}) collective-permute-start(bf16[102,1024]{1,0:T(8,128)(2,1)S(1)} %get-tuple-element.77), channel_id=1, source_target_pairs={{0,96},{32,0},{64,32},{96,64},{1,97},{33,1},{65,33},{97,65},{2,98}... | collective-permute-start | bytes 626696 | tf_op jit(solution)/shard_map/ppermute | solution.py:58
  61.4 0.7 copy-start.10
  65.4 32.2 %copy-start.14 = (s32[4]{0:T(128)S(1)}, s32[4]{0:T(128)}, u32[]{:S(2)}) copy-start(s32[4]{0:T(128)} %constant.115.clone) | copy-start | bytes 52
  65.8 29.3 %collective-permute-start.10 = (bf16[3,192,2048]{2,1,0:T(8,128)(2,1)S(1)}, bf16[3,192,2048]{2,1,0:T(8,128)(2,1)S(1)}, u32[]{:S(2)}, u32[]{:S(2)}) collective-permute-start(bf16[3,192,2048]{2,1,0:T(8,128)(2,1)S(1)} %get-tuple-element.31), channel_id=1, source_target_pairs={{0,2},{1,9},{2,4},{3,11},{4,6},{5,13},{6,0},{7,15},{8,10},{9,17},{... | collective-permute-start | bytes 7077896 | tf_op jit(solution)/shard_map/ppermute | solution.py:42
  66.0 29.0 %collective-permute-start.11 = (bf16[3,192,2048]{2,1,0:T(8,128)(2,1)S(1)}, bf16[3,192,2048]{2,1,0:T(8,128)(2,1)}, u32[]{:S(2)}, u32[]{:S(2)}) collective-permute-start(bf16[3,192,2048]{2,1,0:T(8,128)(2,1)S(1)} %get-tuple-element.32), channel_id=1, source_target_pairs={{0,6},{1,25},{2,0},{3,27},{4,2},{5,29},{6,4},{7,31},{8,14},{9,1},{... | collective-permute-start | bytes 7077896 | tf_op jit(solution)/shard_map/ppermute | solution.py:42
  95.0 16.2 %copy-start = (bf16[3,192,2048]{2,1,0:T(8,128)(2,1)}, bf16[3,192,2048]{2,1,0:T(8,128)(2,1)S(1)}, u32[]{:S(2)}) copy-start(bf16[3,192,2048]{2,1,0:T(8,128)(2,1)S(1)} %collective-permute-done.10.refs_3_.refs_1_.refs_5_) | copy-start | bytes 7077892
  95.1 16.2 %collective-permute-start.14 = (bf16[3,192,2048]{2,1,0:T(8,128)(2,1)S(1)}, bf16[3,192,2048]{2,1,0:T(8,128)(2,1)}, u32[]{:S(2)}, u32[]{:S(2)}) collective-permute-start(bf16[3,192,2048]{2,1,0:T(8,128)(2,1)S(1)} %collective-permute-done.10.refs_3_.refs_1_.refs_5_), channel_id=1, source_target_pairs={{0,1},{1,0},{2,3},{3,2},{4,5},{5,4},{6,7},{7,6},{8,9},{9,8},{10,11... | collective-permute-start | bytes 7077896 | tf_op jit(solution)/shard_map/ppermute | solution.py:46
  97.4 13.8 %collective-permute-start.15 = (bf16[3,192,2048]{2,1,0:T(8,128)(2,1)}, bf16[3,192,2048]{2,1,0:T(8,128)(2,1)}, u32[]{:S(2)}, u32[]{:S(2)}) collective-permute-start(bf16[3,192,2048]{2,1,0:T(8,128)(2,1)} %collective-permute-done.11.refs_7_.refs_2_.refs_6_), channel_id=1, source_target_pairs={{0,1},{1,0},{2,3},{3,2},{4,5},{5,4},{6,7},{7,6},{8,9},{9,8},{10,11... | collective-permute-start | bytes 7077896 | tf_op jit(solution)/shard_map/ppermute | solution.py:46
  97.9 9.7 %collective-permute-start.12 = (bf16[2,192,2048]{2,1,0:T(8,128)(2,1)}, bf16[2,192,2048]{2,1,0:T(8,128)(2,1)}, u32[]{:S(2)}, u32[]{:S(2)}) collective-permute-start(bf16[2,192,2048]{2,1,0:T(8,128)(2,1)} %collective-permute-done.7.refs_1_.refs_5_), channel_id=1, source_target_pairs={{0,1},{1,0},{2,3},{3,2},{4,5},{5,4},{6,7},{7,6},{8,9},{9,8},{10,11... | collective-permute-start | bytes 4718600 | tf_op jit(solution)/shard_map/ppermute | solution.py:46
  98.4 11.5 %collective-permute-start.13 = (bf16[2,192,2048]{2,1,0:T(8,128)(2,1)}, bf16[2,192,2048]{2,1,0:T(8,128)(2,1)}, u32[]{:S(2)}, u32[]{:S(2)}) collective-permute-start(bf16[2,192,2048]{2,1,0:T(8,128)(2,1)} %collective-permute-done.8.refs_2_.refs_6_), channel_id=1, source_target_pairs={{0,1},{1,0},{2,3},{3,2},{4,5},{5,4},{6,7},{7,6},{8,9},{9,8},{10,11... | collective-permute-start | bytes 4718600 | tf_op jit(solution)/shard_map/ppermute | solution.py:46
  102.4 38.7 %collective-permute-start.18 = (bf16[2,192,2048]{2,1,0:T(8,128)(2,1)}, bf16[2,192,2048]{2,1,0:T(8,128)(2,1)}, u32[]{:S(2)}, u32[]{:S(2)}) collective-permute-start(bf16[2,192,2048]{2,1,0:T(8,128)(2,1)} %copy-done.1), channel_id=1, source_target_pairs={{0,1},{1,0},{2,3},{3,2},{4,5},{5,4},{6,7},{7,6},{8,9},{9,8},{10,11... | collective-permute-start | bytes 4718600 | tf_op jit(solution)/shard_map/ppermute | solution.py:46
  107.6 25.6 %collective-permute-start.16 = (bf16[1,192,2048]{2,1,0:T(8,128)(2,1)S(1)}, bf16[1,192,2048]{2,1,0:T(8,128)(2,1)S(1)}, u32[]{:S(2)}, u32[]{:S(2)}) collective-permute-start(bf16[1,192,2048]{2,1,0:T(8,128)(2,1)S(1)} %slice.214), channel_id=1, source_target_pairs={{0,2},{1,9},{2,4},{3,11},{4,6},{5,13},{6,0},{7,15},{8,10},{9,17},{... | collective-permute-start | bytes 2359304 | tf_op jit(solution)/shard_map/ppermute | solution.py:42
  109.8 25.7 %collective-permute-start.17 = (bf16[1,192,2048]{2,1,0:T(8,128)(2,1)S(1)}, bf16[1,192,2048]{2,1,0:T(8,128)(2,1)}, u32[]{:S(2)}, u32[]{:S(2)}) collective-permute-start(bf16[1,192,2048]{2,1,0:T(8,128)(2,1)S(1)} %slice.215), channel_id=1, source_target_pairs={{0,6},{1,25},{2,0},{3,27},{4,2},{5,29},{6,4},{7,31},{8,14},{9,1},{... | collective-permute-start | bytes 2359304 | tf_op jit(solution)/shard_map/ppermute | solution.py:42
  133.1 8.0 %copy-start.5 = (bf16[1,192,2048]{2,1,0:T(8,128)(2,1)}, bf16[1,192,2048]{2,1,0:T(8,128)(2,1)S(1)}, u32[]{:S(2)}) copy-start(bf16[1,192,2048]{2,1,0:T(8,128)(2,1)S(1)} %collective-permute-done.16.refs_3_) | copy-start | bytes 2359300
  133.1 8.0 %collective-permute-start.19 = (bf16[1,192,2048]{2,1,0:T(8,128)(2,1)S(1)}, bf16[1,192,2048]{2,1,0:T(8,128)(2,1)S(1)}, u32[]{:S(2)}, u32[]{:S(2)}) collective-permute-start(bf16[1,192,2048]{2,1,0:T(8,128)(2,1)S(1)} %collective-permute-done.16.refs_3_), channel_id=1, source_target_pairs={{0,1},{1,0},{2,3},{3,2},{4,5},{5,4},{6,7},{7,6},{8,9},{9,8},{10,11... | collective-permute-start | bytes 2359304 | tf_op jit(solution)/shard_map/ppermute | solution.py:46
  135.5 5.6 %collective-permute-start.20 = (bf16[1,192,2048]{2,1,0:T(8,128)(2,1)}, bf16[1,192,2048]{2,1,0:T(8,128)(2,1)S(1)}, u32[]{:S(2)}, u32[]{:S(2)}) collective-permute-start(bf16[1,192,2048]{2,1,0:T(8,128)(2,1)} %collective-permute-done.17.refs_7_), channel_id=1, source_target_pairs={{0,1},{1,0},{2,3},{3,2},{4,5},{5,4},{6,7},{7,6},{8,9},{9,8},{10,11... | collective-permute-start | bytes 2359304 | tf_op jit(solution)/shard_map/ppermute | solution.py:46
  137.1 24.4 %collective-permute-start.23 = (bf16[576,768]{1,0:T(8,128)(2,1)}, bf16[576,768]{1,0:T(8,128)(2,1)S(1)}, u32[]{:S(2)}, u32[]{:S(2)}) collective-permute-start(bf16[576,768]{1,0:T(8,128)(2,1)} %get-tuple-element.33.refs_0_), channel_id=1, source_target_pairs={{0,32},{32,64},{64,96},{96,0},{1,33},{33,65},{65,97},{97,1},{2,34}... | collective-permute-start | bytes 2654216 | tf_op jit(solution)/shard_map/ppermute | solution.py:58
  140.2 21.4 %collective-permute-start.21 = (bf16[576,768]{1,0:T(8,128)(2,1)}, bf16[576,768]{1,0:T(8,128)(2,1)S(1)}, u32[]{:S(2)}, u32[]{:S(2)}) collective-permute-start(bf16[576,768]{1,0:T(8,128)(2,1)} %get-tuple-element.33.refs_0_), channel_id=1, source_target_pairs={{0,96},{32,0},{64,32},{96,64},{1,97},{33,1},{65,33},{97,65},{2,98}... | collective-permute-start | bytes 2654216 | tf_op jit(solution)/shard_map/ppermute | solution.py:58
  141.1 0.9 copy-start.6
  141.1 1.2 copy-start.7
  161.5 2.3 copy-start.4
  161.6 4.0 %copy-start.8 = (bf16[576,768]{1,0:T(8,128)(2,1)}, bf16[576,768]{1,0:T(8,128)(2,1)S(1)}, u32[]{:S(2)}) copy-start(bf16[576,768]{1,0:T(8,128)(2,1)S(1)} %collective-permute-done.23.refs_4_) | copy-start | bytes 2654212
  161.6 3.9 %copy-start.9 = (bf16[576,768]{1,0:T(8,128)(2,1)}, bf16[576,768]{1,0:T(8,128)(2,1)S(1)}, u32[]{:S(2)}) copy-start(bf16[576,768]{1,0:T(8,128)(2,1)S(1)} %collective-permute-done.21.refs_1_) | copy-start | bytes 2654212
  165.5 53.5 %collective-permute-start.22 = (bf16[1440,768]{1,0:T(8,128)(2,1)S(1)}, bf16[1440,768]{1,0:T(8,128)(2,1)}, u32[]{:S(2)}, u32[]{:S(2)}) collective-permute-start(bf16[1440,768]{1,0:T(8,128)(2,1)S(1)} %get-tuple-element.53), channel_id=1, source_target_pairs={{0,96},{32,0},{64,32},{96,64},{1,97},{33,1},{65,33},{97,65},{2,98}... | collective-permute-start | bytes 6635528 | tf_op jit(solution)/shard_map/ppermute | solution.py:58
  167.9 49.9 %collective-permute-start.24 = (bf16[1440,768]{1,0:T(8,128)(2,1)}, bf16[1440,768]{1,0:T(8,128)(2,1)}, u32[]{:S(2)}, u32[]{:S(2)}) collective-permute-start(bf16[1440,768]{1,0:T(8,128)(2,1)} %get-tuple-element.52), channel_id=1, source_target_pairs={{0,32},{32,64},{64,96},{96,0},{1,33},{33,65},{65,97},{97,1},{2,34}... | collective-permute-start | bytes 6635528 | tf_op jit(solution)/shard_map/ppermute | solution.py:58
  184.1 70.3 %all-to-all-start.1 = ((bf16[32,72,1024]{2,1,0:T(8,128)(2,1)}), bf16[32,72,1024]{2,1,0:T(8,128)(2,1)}, u32[]{:S(2)}, u32[]{:S(2)}) async-start(bf16[32,72,1024]{2,1,0:T(8,128)(2,1)} %rowgrad.1), calls=%async_computation.1 | async-start | bytes 9437184 | tf_op jit(solution)/shard_map/all_to_all | solution.py:496
  219.0 20.4 %collective-permute-start.25 = (bf16[576,768]{1,0:T(8,128)(2,1)S(1)}, bf16[576,768]{1,0:T(8,128)(2,1)S(1)}, u32[]{:S(2)}, u32[]{:S(2)}) collective-permute-start(bf16[576,768]{1,0:T(8,128)(2,1)S(1)} %slice.173), channel_id=1, source_target_pairs={{0,32},{32,64},{64,96},{96,0},{1,33},{33,65},{65,97},{97,1},{2,34}... | collective-permute-start | bytes 2654216 | tf_op jit(solution)/shard_map/ppermute | solution.py:58
  220.3 19.3 %collective-permute-start.26 = (bf16[576,768]{1,0:T(8,128)(2,1)S(1)}, bf16[576,768]{1,0:T(8,128)(2,1)S(1)}, u32[]{:S(2)}, u32[]{:S(2)}) collective-permute-start(bf16[576,768]{1,0:T(8,128)(2,1)S(1)} %slice.174), channel_id=1, source_target_pairs={{0,96},{32,0},{64,32},{96,64},{1,97},{33,1},{65,33},{97,65},{2,98}... | collective-permute-start | bytes 2654216 | tf_op jit(solution)/shard_map/ppermute | solution.py:58
Sparse Core Ops, SparseCore 0:
  95.2 85.2 all-gather.1

commit v4 on v3

--- a/solution.py
+++ b/solution.py
@@ -99,9 +99,9 @@
         out_ref[:, pl.ds(pl.multiple_of(rel * width, width), width)] = rows[...]
 
 
-def hidden_kernel(place, slot_own, slot_sib, *refs, half):
+def hidden_kernel(place, slot_own, slot_sib, prob, *refs, half):
     own, sib = refs[0:8], refs[8:16]
-    wg, wu, hid_ref, sg_ref, slope_ref, xi_ref, hot, cat, xs, gate, up = refs[16:]
+    wg, wu, hid_ref, sg_ref, slope_ref, xi_ref, hot, scale_ref, cat, xs, gate, up = refs[16:]
     t = pl.program_id(0)
     rows = hot.shape[2]
 
@@ -110,6 +110,8 @@
         for k in range(2):
             hot[0, k] = one_hot(slot_own[k], rows)
             hot[1, k] = one_hot(slot_sib[k], rows)
+            scale = row_probs(slot_own[k], prob[k], rows)
+            scale_ref[rows * k : rows * (k + 1), :] = jnp.broadcast_to(scale, (rows, 128))
         gate[...] = jnp.zeros_like(gate)
         up[...] = jnp.zeros_like(up)
 
@@ -131,23 +133,19 @@
         slope_ref[...] = u * s * (1.0 + g * (1.0 - s))
 
 
-def cotangent_kernel(place, slot_own, slot_sib, prob, *refs, half):
+def cotangent_kernel(place, hot, scale, *refs, half):
     own, sib = refs[0:8], refs[8:16]
-    wd, sg, slope, dd_ref, yi_ref, hot, prob_row, cat, ys, dh = refs[16:]
+    wd, sg, slope, dd_ref, yi_ref, cat, ys, dh = refs[16:]
     t = pl.program_id(0)
     rows = hot.shape[2]
 
     @pl.when(t == 0)
     def _():
-        for k in range(2):
-            hot[0, k] = one_hot(slot_own[k], rows)
-            hot[1, k] = one_hot(slot_sib[k], rows)
-            prob_row[rows * k : rows * (k + 1), :] = row_probs(slot_own[k], prob[k], rows)
         dh[...] = jnp.zeros_like(dh)
 
     def put(k, got):
         at = slice(rows * k, rows * (k + 1))
-        ys[at, :] = (got * prob_row[at, :]).astype(BF16)
+        ys[at, :] = (got * scale[at, 0:1]).astype(BF16)
 
     pick_rows(t, half, hot, cat, own, sib, put)
     dh[...] += dot(ys[...], wd[...], NT)
@@ -172,7 +170,7 @@
     return here + [spec(b, lambda t: jnp.maximum(t - half, 0)) for b in own]
 
 
-def hidden_rows(place, slot_own, slot_sib, own, sib, wg, wu, rows, half=4):
+def hidden_rows(place, slot_own, slot_sib, prob, own, sib, wg, wu, rows, half=2):
     width, ff = wg.shape
     tile = width // (2 * half)
     toks = own[0][0].shape[1]
@@ -180,15 +178,15 @@
     w_in = pl.BlockSpec((tile, ff), lambda t, s: (tile_of(t, s[0], half), 0))
     const = lambda shape: pl.BlockSpec(shape, lambda t, s: (0,) * len(shape))
     outs = [((total, ff), BF16), ((total, ff), F32), ((total, ff), F32), ((total, width // 4), BF16)]
+    outs += [((2, 2, rows, 4 * toks), BF16), ((total, 128), F32)]
     return pl.pallas_call(
         functools.partial(hidden_kernel, half=half),
         grid_spec=pltpu.PrefetchScalarGridSpec(
             num_scalar_prefetch=1,
             grid=(2 * half,),
-            in_specs=[whole(slot_own), whole(slot_sib)] + ring_specs(own, tile, half) + [w_in, w_in],
+            in_specs=[whole(slot_own), whole(slot_sib), whole(prob)] + ring_specs(own, tile, half) + [w_in, w_in],
             out_specs=[const(shape) for shape, _ in outs],
             scratch_shapes=[
-                pltpu.VMEM((2, 2, rows, 4 * toks), BF16),
                 pltpu.VMEM((4 * toks, tile), BF16),
                 pltpu.VMEM((total, tile), BF16),
                 pltpu.VMEM((total, ff), F32),
@@ -203,10 +201,10 @@
             transcendentals=0,
         ),
         name="hidden_rows",
-    )(place, slot_own, slot_sib, *(b for b, _ in own + sib), wg, wu)
-
-
-def cotangent_rows(place, slot_own, slot_sib, prob, own, sib, wd, sg, slope, rows, half=4):
+    )(place, slot_own, slot_sib, prob, *(b for b, _ in own + sib), wg, wu)
+
+
+def cotangent_rows(place, hot, scale, own, sib, wd, sg, slope, rows, half=2):
     ff, width = wd.shape
     tile = width // (2 * half)
     toks = own[0][0].shape[1]
@@ -219,12 +217,10 @@
         grid_spec=pltpu.PrefetchScalarGridSpec(
             num_scalar_prefetch=1,
             grid=(2 * half,),
-            in_specs=[whole(slot_own), whole(slot_sib), whole(prob)]
+            in_specs=[whole(hot), whole(scale)]
             + ring_specs(own, tile, half) + [w_out, whole(sg), whole(slope)],
             out_specs=[const(shape) for shape, _ in outs],
             scratch_shapes=[
-                pltpu.VMEM((2, 2, rows, 4 * toks), BF16),
-                pltpu.VMEM((total, 1), F32),
                 pltpu.VMEM((4 * toks, tile), BF16),
                 pltpu.VMEM((total, tile), BF16),
                 pltpu.VMEM((total, ff), F32),
@@ -238,7 +234,7 @@
             transcendentals=0,
         ),
         name="cotangent_rows",
-    )(place, slot_own, slot_sib, prob, *(b for b, _ in own + sib), wd, sg, slope)
+    )(place, hot, scale, *(b for b, _ in own + sib), wd, sg, slope)
 
 
 def rowgrad_kernel(h, wg, wu, out_ref, grad, pieces, *, cap):
@@ -442,8 +438,8 @@
     slots = slots.reshape(4, 2, 1, 16 * toks)
     probs = tables[:, :, :, 1].swapaxes(1, 2).reshape(4, 2, 1, 16 * toks)
 
-    ready = lambda v: after(v, sib_x, cols)
-    sib_x = swap_core(col_x)
+    sib_near = (swap_core(col_x), swap_core(after(prev_x, cols)), swap_core(after(succ_x, cols)))
+    ready = lambda v: after(v, sib_near)
     up = step(ready(jnp.concatenate([prev_x[:1], col_y])), 2, 1)
     down = step(ready(jnp.concatenate([succ_x[1:], col_y])), 2, -1)
     far_y = step(up[1:2], 2, 1), step(down[2:], 2, -1)
@@ -456,7 +452,7 @@
 
     sib_up, sib_down = swap_core(up), swap_core(down)
     own_x = blocks_x(col_x, prev_x, succ_x, up, down)
-    sib_x = blocks_x(sib_x, swap_core(prev_x), swap_core(succ_x), sib_up, sib_down)
+    sib_x = blocks_x(*sib_near, sib_up, sib_down)
     own_y = blocks_y(col_y, up, down, *far_y)
 
     table = meta.reshape(16, 2, 2, toks)
@@ -474,14 +470,14 @@
     cols = lax.all_gather(after(cols, up, down), "expert", tiled=True)
     cols = cols.reshape(16, 2, 3, 2, toks, quarter)
 
-    hid, sg, slope, xi = hidden_rows(
-        place, local_slots[0], local_slots[1], own_x, sib_x, wg, wu, rows
+    hid, sg, slope, xi, hot, scale = hidden_rows(
+        place, local_slots[0], local_slots[1], local_probs, own_x, sib_x, wg, wu, rows
     )
     hid_prev, hid_succ = over_groups(hid, 1), over_groups(hid, -1)
     sib_far = [swap_core(after(b, hid)) for b in far_y]
     sib_y = blocks_y(swap_core(col_y), sib_up, sib_down, *sib_far)
     dd, yi = cotangent_rows(
-        after(place, hid), local_slots[0], local_slots[1], local_probs, own_y, sib_y, wd, sg, slope, rows
+        place, hot, scale, own_y, sib_y, wd, sg, slope, rows
     )
 
     half = hid.shape[0] // 2

time: 269 us -> 260 us (0.967)
  waiting for transfers between devices: 68.6 us -> 57.9 us
    ppermute x9, waiting for transfers between devices: 24.7 us -> 17.1 us  [over_groups(): return lax.ppermute(v, 'dp', [(s, (s + shift) % 4) for s in range(4)])]
    ppermute x9, waiting for transfers between devices: 6.18 us -> 3.26 us  [swap_core(): return lax.ppermute(v, 'expert', [(e, e ^ 1) for e in range(32)])]
where the time goes in v4:
time: 260 us; the launch traced here: 256 us
  Pallas kernels  93 us (36%)
  waiting for transfers between devices  57.9 us (22%)
  starting transfers between devices  50.8 us (20%)
  local copies, waits for them, and re-layouts  22.3 us (9%)
  between operations  14.7 us (6%)
  other arithmetic  13.6 us (5%)
  matrix products  3.62 us (1%)
    ppermute x9, waiting for transfers between devices, step(): return lax.ppermute(v, 'expert', expert_pairs(ring, shift))  37.6 us
    pallas_call x1, Pallas kernels, hidden_rows(): pl.pallas_call(functools.partial(hidden_kernel, half=half), grid_spec=plt...  22 us
    pallas_call x2, Pallas kernels, weights(): pl.pallas_call(functools.partial(weight_kernel, count=count), grid=(count...  21.9 us
    pallas_call x1, Pallas kernels, cotangent_rows(): pl.pallas_call(functools.partial(cotangent_kernel, half=half), grid_spec=...  17.5 us
    pallas_call x1, Pallas kernels, gather_columns(): pl.pallas_call(gather_kernel, grid=(2, 2), in_specs=[meta, meta, whole(xi...  17.2 us
    ppermute x9, waiting for transfers between devices, over_groups(): return lax.ppermute(v, 'dp', [(s, (s + shift) % 4) for s in range(4)])  17.1 us
    pallas_call x1, Pallas kernels, rowgrad(): pl.pallas_call(functools.partial(rowgrad_kernel, cap=cap), grid=(4,), in_...  14.4 us
    ppermute x9, starting transfers between devices, step(): return lax.ppermute(v, 'expert', expert_pairs(ring, shift))  13.6 us
  transfers between devices with their start and end apart: 30, of which 12 were waited for; matrix products, arithmetic and copies ran while one was open for 11% of the time, Pallas kernels for 36%

profile of v4, /device:TPU:1, one launch (start us, length us, event | category | flops | bytes accessed | tf_op | source)
XLA Modules:
  0.0 255.9 jit_solution(912475243189700760)
XLA Ops:
  7.2 1.1 fusion.5
  8.3 1.5 collective-permute-start
  11.1 1.4 select_bitcast_fusion.1
  12.6 2.9 %collective-permute-start.3 = (bf16[2,2,48,2048]{3,2,1,0:T(8,128)(2,1)S(1)}, bf16[2,2,48,2048]{3,2,1,0:T(8,128)(2,1)S(1)}, u32[]{:S(2)}, u32[]{:S(2)}) collective-permute-start(bf16[2,2,48,2048]{3,2,1,0:T(8,128)(2,1)S(1)} %pad_maximum_fusion.8), channel_id=1, source_target_pairs={{0,16},{1,5},{2,18},{3,7},{4,20},{5,1},{6,22},{7,3},{8,24},{9,13},... | collective-permute-start | bytes 2359304 | tf_op jit(solution)/shard_map/ppermute | solution.py:42
  17.3 7.7 %all-to-all-start = ((f32[32,2,48]{2,1,0:T(2,128)}), f32[32,2,48]{2,1,0:T(2,128)}, u32[]{:S(2)}, u32[]{:S(2)}) async-start(f32[32,2,48]{2,1,0:T(2,128)} %copy.45), calls=%async_computation | async-start | bytes 65536 | tf_op jit(solution)/shard_map/all_to_all | solution.py:414
  25.1 1.5 collective-permute-start.1
  26.7 7.5 %collective-permute-done.2 = bf16[2,2,48,2048]{3,2,1,0:T(8,128)(2,1)S(1)} collective-permute-done((bf16[2,2,48,2048]{3,2,1,0:T(8,128)(2,1)S(1)}, bf16[2,2,48,2048]{3,2,1,0:T(8,128)(2,1)S(1)}, u32[]{:S(2)}, u32[]{:S(2)}) %collective-permute-start.2) | collective-permute-done | bytes 786464 | tf_op jit(solution)/shard_map/ppermute | solution.py:42
  34.2 3.5 %collective-permute-done.1 = bf16[2,2,48,2048]{3,2,1,0:T(8,128)(2,1)S(1)} collective-permute-done((bf16[2,2,48,2048]{3,2,1,0:T(8,128)(2,1)S(1)}, bf16[2,2,48,2048]{3,2,1,0:T(8,128)(2,1)S(1)}, u32[]{:S(2)}, u32[]{:S(2)}) %collective-permute-start.1) | collective-permute-done | bytes 786464 | tf_op jit(solution)/shard_map/ppermute | solution.py:42
  38.1 1.1 collective-permute-start.7
  39.2 1.6 collective-permute-start.8
  40.9 1.9 pad_maximum_fusion.7
  44.5 1.2 constant_dynamic-slice_fusion.2
  45.7 1.4 collective-permute-start.6
  47.1 2.6 %collective-permute-start.5 = (bf16[102,1024]{1,0:T(8,128)(2,1)S(1)}, bf16[102,1024]{1,0:T(8,128)(2,1)S(1)}, u32[]{:S(2)}, u32[]{:S(2)}) collective-permute-start(bf16[102,1024]{1,0:T(8,128)(2,1)S(1)} %get-tuple-element.84), channel_id=1, source_target_pairs={{0,64},{32,96},{64,0},{96,32},{1,65},{33,97},{65,1},{97,33},{2,66}... | collective-permute-start | bytes 626696 | tf_op jit(solution)/shard_map/ppermute | solution.py:58
  49.7 1.1 collective-permute-start.4
  50.8 1.5 collective-permute-done.6
  52.3 3.6 %collective-permute-start.9 = (bf16[2,192,2048]{2,1,0:T(8,128)(2,1)S(1)}, bf16[2,192,2048]{2,1,0:T(8,128)(2,1)}, u32[]{:S(2)}, u32[]{:S(2)}) collective-permute-start(bf16[2,192,2048]{2,1,0:T(8,128)(2,1)S(1)} %get-tuple-element.31.refs_0_.refs_4_), channel_id=1, source_target_pairs={{0,1},{1,0},{2,3},{3,2},{4,5},{5,4},{6,7},{7,6},{8,9},{9,8},{10,11... | collective-permute-start | bytes 4718600 | tf_op jit(solution)/shard_map/ppermute | solution.py:46
  55.9 2.0 collective-permute-done.5
  59.4 2.7 %collective-permute-start.10 = (bf16[2,192,2048]{2,1,0:T(8,128)(2,1)}, bf16[2,192,2048]{2,1,0:T(8,128)(2,1)S(1)}, u32[]{:S(2)}, u32[]{:S(2)}) collective-permute-start(bf16[2,192,2048]{2,1,0:T(8,128)(2,1)} %collective-permute-done.7.refs_1_.refs_5_), channel_id=1, source_target_pairs={{0,1},{1,0},{2,3},{3,2},{4,5},{5,4},{6,7},{7,6},{8,9},{9,8},{10,11... | collective-permute-start | bytes 4718600 | tf_op jit(solution)/shard_map/ppermute | solution.py:46
  62.2 1.2 slice.211
  63.4 1.2 slice.207
  65.3 2.2 collective-permute-done.11.refs_10_.refs_14_
  67.6 2.7 %collective-permute-start.13 = (bf16[3,192,2048]{2,1,0:T(8,128)(2,1)S(1)}, bf16[3,192,2048]{2,1,0:T(8,128)(2,1)}, u32[]{:S(2)}, u32[]{:S(2)}) collective-permute-start(bf16[3,192,2048]{2,1,0:T(8,128)(2,1)S(1)} %get-tuple-element.37), channel_id=1, source_target_pairs={{0,6},{1,25},{2,0},{3,27},{4,2},{5,29},{6,4},{7,31},{8,14},{9,1},{... | collective-permute-start | bytes 7077896 | tf_op jit(solution)/shard_map/ppermute | solution.py:42
  70.3 26.5 %collective-permute-done.12.refs_3_.refs_1_.refs_5_ = bf16[3,192,2048]{2,1,0:T(8,128)(2,1)S(1)} collective-permute-done((bf16[3,192,2048]{2,1,0:T(8,128)(2,1)S(1)}, bf16[3,192,2048]{2,1,0:T(8,128)(2,1)S(1)}, u32[]{:S(2)}, u32[]{:S(2)}) %collective-permute-start.12) | collective-permute-done | bytes 2359328 | tf_op jit(solution)/shard_map/ppermute | solution.py:42
  96.8 1.3 collective-permute-start.14
  99.8 1.4 gather_fusion
  103.9 1.2 slice.213
  105.1 2.9 %collective-permute-start.17 = (bf16[1,192,2048]{2,1,0:T(8,128)(2,1)S(1)}, bf16[1,192,2048]{2,1,0:T(8,128)(2,1)}, u32[]{:S(2)}, u32[]{:S(2)}) collective-permute-start(bf16[1,192,2048]{2,1,0:T(8,128)(2,1)S(1)} %slice.213), channel_id=1, source_target_pairs={{0,6},{1,25},{2,0},{3,27},{4,2},{5,29},{6,4},{7,31},{8,14},{9,1},{... | collective-permute-start | bytes 2359304 | tf_op jit(solution)/shard_map/ppermute | solution.py:42
  108.0 22.0 %hidden_rows.1 = (bf16[576,768]{1,0:T(8,128)(2,1)}, f32[576,768]{1,0:T(8,128)}, f32[576,768]{1,0:T(8,128)}, bf16[576,1024]{1,0:T(8,128)(2,1)}, bf16[2,2,288,768]{3,2,1,0:T(8,128)(2,1)}, /*index=5*/f32[576,128]{1,0:T(8,128)}) custom-call(s32[2]{0:T(128)} %pad_add_fusion.place, s32[2,1,768]{2,1,0:T(1,128)} %squeeze.70.slot_own, ...), custom_call_target="tpu_custom_call" | custom-call | flops 10871635968 | bytes 25165824 | tf_op jit(solution)/shard_map/hidden_rows/pallas_call | solution.py:182
  132.3 2.2 collective-permute-start.21
  136.4 17.5 %cotangent_rows.1 = (bf16[2,576,768]{2,1,0:T(8,128)(2,1)}, bf16[576,1024]{1,0:T(8,128)(2,1)}) custom-call(s32[2]{0:T(128)} %pad_add_fusion.place, bf16[2,2,288,768]{3,2,1,0:T(8,128)(2,1)} %get-tuple-element.38.hot, f32[576,128]{1,0:T(8,128)} %get-tuple-element.39.scale, bf16[2,192,2048]{2,1,0:T(8,128)(2,1)} %copy-done.1, bf16[3,192,2048]{2,1,0:T(8,128)(2,1)} %copy-done, ...), custom_call_target="tpu_custom_call" | custom-call | flops 7247757312 | bytes 18874368 | tf_op jit(solution)/shard_map/cotangent_rows/pallas_call | solution.py:215
  154.3 1.9 copy-done.6
  156.1 1.6 pad_maximum_fusion.3
  158.2 1.0 collective-permute-start.24
  161.1 14.4 %rowgrad.1 = bf16[32,72,1024]{2,1,0:T(8,128)(2,1)} custom-call(bf16[2,576,768]{2,1,0:T(8,128)(2,1)} %get-tuple-element.45.h.refs_0_, bf16[4096,768]{1,0:T(8,128)(2,1)} %bitcast.120, bf16[4096,768]{1,0:T(8,128)(2,1)} %bitcast.122), custom_call_target="tpu_custom_call" | custom-call | flops 7247757312 | bytes 17301504 | tf_op jit(solution)/shard_map/rowgrad/pallas_call | solution.py:263
  175.5 6.6 %all-to-all-start.1 = ((bf16[32,72,1024]{2,1,0:T(8,128)(2,1)}), bf16[32,72,1024]{2,1,0:T(8,128)(2,1)}, u32[]{:S(2)}, u32[]{:S(2)}) async-start(bf16[32,72,1024]{2,1,0:T(8,128)(2,1)} %rowgrad.1), calls=%async_computation.1 | async-start | bytes 9437184 | tf_op jit(solution)/shard_map/all_to_all | solution.py:492
  182.1 17.2 %gather_columns.1.xy = bf16[2048,2304]{1,0:T(8,128)(2,1)} custom-call(s32[4,2,1,768]{3,2,1,0:T(1,128)} %reshape.607.slot, f32[4,2,1,768]{3,2,1,0:T(1,128)} %reshape.611.prob, bf16[576,1024]{1,0:T(8,128)(2,1)} %get-tuple-element.47.xi, bf16[576,1024]{1,0:T(8,128)(2,1)} %get-tuple-element.48.yi, bf16[16,2,3,2,48,1024]{5,4,3,2,1,0:T(8,128)(2,1)} %bitcast.117), custom_call_target="tpu_custom_call" | custom-call | flops 1 | bytes 1 | tf_op jit(solution)/shard_map/gather_columns/pallas_call | solution.py:315
  200.5 2.1 eq.55
  202.6 5.0 %collective-permute-done.24.refs_2_.refs_4_.refs_5_ = bf16[1440,768]{1,0:T(8,128)(2,1)} collective-permute-done((bf16[1440,768]{1,0:T(8,128)(2,1)}, bf16[1440,768]{1,0:T(8,128)(2,1)}, u32[]{:S(2)}, u32[]{:S(2)}) %collective-permute-start.24) | collective-permute-done | bytes 2211872 | tf_op jit(solution)/shard_map/ppermute | solution.py:58
  207.6 1.2 slice.171
  209.4 1.2 slice.172
  210.6 2.5 collective-permute-start.26
  213.1 8.4 %weight_grads.2 = bf16[768,1024]{1,0:T(8,128)(2,1)} custom-call(bf16[2048,2304]{1,0:T(8,128)(2,1)} %gather_columns.1.xy, bf16[576,768]{1,0:T(8,128)(2,1)} %get-tuple-element.40.refs_0_, bf16[576,768]{1,0:T(8,128)(2,1)} %copy-done.11, bf16[1440,768]{1,0:T(8,128)(2,1)} %collective-permute-done.24.refs_2_.refs_4_.refs_5_, ...), custom_call_target="tpu_custom_call" | custom-call | flops 14495514624 | bytes 8257536 | tf_op jit(solution)/shard_map/weight_grads/pallas_call | solution.py:368
  221.5 7.2 %collective-permute-done.25 = bf16[576,768]{1,0:T(8,128)(2,1)S(1)} collective-permute-done((bf16[576,768]{1,0:T(8,128)(2,1)S(1)}, bf16[576,768]{1,0:T(8,128)(2,1)S(1)}, u32[]{:S(2)}, u32[]{:S(2)}) %collective-permute-start.25) | collective-permute-done | bytes 884768 | tf_op jit(solution)/shard_map/ppermute | solution.py:58
  228.7 1.2 collective-permute-done.26
  229.9 1.4 pad_maximum_fusion.4.refs_3_
  231.3 13.5 %weight_grads.3 = (bf16[1024,768]{1,0:T(8,128)(2,1)}, bf16[1024,768]{1,0:T(8,128)(2,1)}) custom-call(bf16[2048,2304]{1,0:T(8,128)(2,1)} %gather_columns.1.xy, bf16[2,576,768]{2,1,0:T(8,128)(2,1)} %get-tuple-element.45.h.refs_0_, bf16[1440,768]{1,0:T(8,128)(2,1)} %collective-permute-done.22.refs_3_.refs_1_.refs_2_, ...), custom_call_target="tpu_custom_call" | custom-call | flops 28991029248 | bytes 11796480 | tf_op jit(solution)/shard_map/weight_grads/pallas_call | solution.py:368
  244.8 3.4 %convolution_convert_fusion = bf16[192,1024]{1,0:T(8,128)(2,1)S(1)} fusion(pred[192,2304]{1,0:T(32,128)(4,1)S(1)} %eq.55, bf16[2304,1024]{1,0:T(8,128)(2,1)} %bitcast.51), kind=kOutput, calls=%fused_computation.9 | convolution fusion | flops 906166272 | bytes 5554176 | tf_op jit(solution)/shard_map/dot_general | solution.py:22
  (140 shorter events, 21.3 us)
Async XLA Ops:
  7.2 8.3 %copy-start.14 = (s32[48,8]{0,1:T(8,128)S(1)}, s32[48,8]{0,1:T(8,128)}, u32[]{:S(2)}) copy-start(s32[48,8]{0,1:T(8,128)} %param.10) | copy-start | bytes 4612
  7.2 8.3 %copy-start.15 = (f32[48,8]{0,1:T(8,128)S(1)}, f32[48,8]{0,1:T(8,128)}, u32[]{:S(2)}) copy-start(f32[48,8]{0,1:T(8,128)} %param.11) | copy-start | bytes 4612
  8.3 2.9 %collective-permute-start = (bf16[2,48,2048]{2,1,0:T(8,128)(2,1)S(1)}, bf16[2,48,2048]{2,1,0:T(8,128)(2,1)S(1)}, u32[]{:S(2)}, u32[]{:S(2)}) collective-permute-start(bf16[2,48,2048]{2,1,0:T(8,128)(2,1)S(1)} %fusion.5), channel_id=1, source_target_pairs={{0,1},{1,0},{2,3},{3,2},{4,5},{5,4},{6,7},{7,6},{8,9},{9,8},{10,11... | collective-permute-start | bytes 1179656 | tf_op jit(solution)/shard_map/ppermute | solution.py:46
  12.6 14.0 %collective-permute-start.3 = (bf16[2,2,48,2048]{3,2,1,0:T(8,128)(2,1)S(1)}, bf16[2,2,48,2048]{3,2,1,0:T(8,128)(2,1)S(1)}, u32[]{:S(2)}, u32[]{:S(2)}) collective-permute-start(bf16[2,2,48,2048]{3,2,1,0:T(8,128)(2,1)S(1)} %pad_maximum_fusion.8), channel_id=1, source_target_pairs={{0,16},{1,5},{2,18},{3,7},{4,20},{5,1},{6,22},{7,3},{8,24},{9,13},... | collective-permute-start | bytes 2359304 | tf_op jit(solution)/shard_map/ppermute | solution.py:42
  15.8 18.4 %collective-permute-start.2 = (bf16[2,2,48,2048]{3,2,1,0:T(8,128)(2,1)S(1)}, bf16[2,2,48,2048]{3,2,1,0:T(8,128)(2,1)S(1)}, u32[]{:S(2)}, u32[]{:S(2)}) collective-permute-start(bf16[2,2,48,2048]{3,2,1,0:T(8,128)(2,1)S(1)} %pad_maximum_fusion.8), channel_id=1, source_target_pairs={{0,24},{1,7},{2,26},{3,1},{4,28},{5,3},{6,30},{7,5},{8,0},{9,15},{... | collective-permute-start | bytes 2359304 | tf_op jit(solution)/shard_map/ppermute | solution.py:42
  17.3 20.8 %all-to-all-start = ((f32[32,2,48]{2,1,0:T(2,128)}), f32[32,2,48]{2,1,0:T(2,128)}, u32[]{:S(2)}, u32[]{:S(2)}) async-start(f32[32,2,48]{2,1,0:T(2,128)} %copy.45), calls=%async_computation | async-start | bytes 65536 | tf_op jit(solution)/shard_map/all_to_all | solution.py:414
  25.0 157.2 %all-gather.2.cloned.1.call-start = ((), (), s32[]{:S(2)}) async-start(), calls=%async_computation.2 | async-start | bytes 19464192 | tf_op jit(solution)/shard_map/all_gather | solution.py:470
  25.1 12.7 %collective-permute-start.1 = (bf16[2,2,48,2048]{3,2,1,0:T(8,128)(2,1)S(1)}, bf16[2,2,48,2048]{3,2,1,0:T(8,128)(2,1)S(1)}, u32[]{:S(2)}, u32[]{:S(2)}) collective-permute-start(bf16[2,2,48,2048]{3,2,1,0:T(8,128)(2,1)S(1)} %pad_maximum_fusion.8), channel_id=1, source_target_pairs={{0,8},{1,3},{2,10},{3,5},{4,12},{5,7},{6,14},{7,1},{8,16},{9,11},{... | collective-permute-start | bytes 2359304 | tf_op jit(solution)/shard_map/ppermute | solution.py:42
  37.8 3.1 %copy-start.5 = (bf16[48,4096]{1,0:T(8,128)(2,1)S(1)}, bf16[48,4096]{1,0:T(8,128)(2,1)}, u32[]{:S(2)}) copy-start(bf16[48,4096]{1,0:T(8,128)(2,1)} %param.8) | copy-start | bytes 1179652
  38.1 17.8 %copy-start.2 = (bf16[2,192,2048]{2,1,0:T(8,128)(2,1)}, bf16[2,192,2048]{2,1,0:T(8,128)(2,1)S(1)}, u32[]{:S(2)}) copy-start(bf16[2,192,2048]{2,1,0:T(8,128)(2,1)S(1)} %get-tuple-element.31.refs_0_.refs_4_) | copy-start | bytes 4718596
  38.1 26.5 %copy-start.1 = (bf16[2,192,2048]{2,1,0:T(8,128)(2,1)}, bf16[2,192,2048]{2,1,0:T(8,128)(2,1)S(1)}, u32[]{:S(2)}) copy-start(bf16[2,192,2048]{2,1,0:T(8,128)(2,1)S(1)} %get-tuple-element.33.refs_0_.refs_4_) | copy-start | bytes 4718596
  38.1 21.3 %collective-permute-start.7 = (bf16[2,192,2048]{2,1,0:T(8,128)(2,1)S(1)}, bf16[2,192,2048]{2,1,0:T(8,128)(2,1)}, u32[]{:S(2)}, u32[]{:S(2)}) collective-permute-start(bf16[2,192,2048]{2,1,0:T(8,128)(2,1)S(1)} %get-tuple-element.31.refs_0_.refs_4_), channel_id=1, source_target_pairs={{0,2},{1,9},{2,4},{3,11},{4,6},{5,13},{6,0},{7,15},{8,10},{9,17},{... | collective-permute-start | bytes 4718600 | tf_op jit(solution)/shard_map/ppermute | solution.py:42
  39.2 22.9 %collective-permute-start.8 = (bf16[2,192,2048]{2,1,0:T(8,128)(2,1)S(1)}, bf16[2,192,2048]{2,1,0:T(8,128)(2,1)}, u32[]{:S(2)}, u32[]{:S(2)}) collective-permute-start(bf16[2,192,2048]{2,1,0:T(8,128)(2,1)S(1)} %get-tuple-element.31.refs_0_.refs_4_), channel_id=1, source_target_pairs={{0,6},{1,25},{2,0},{3,27},{4,2},{5,29},{6,4},{7,31},{8,14},{9,1},{... | collective-permute-start | bytes 4718600 | tf_op jit(solution)/shard_map/ppermute | solution.py:42
  45.7 6.5 %collective-permute-start.6 = (bf16[102,1024]{1,0:T(8,128)(2,1)S(1)}, bf16[102,1024]{1,0:T(8,128)(2,1)S(1)}, u32[]{:S(2)}, u32[]{:S(2)}) collective-permute-start(bf16[102,1024]{1,0:T(8,128)(2,1)S(1)} %get-tuple-element.85), channel_id=1, source_target_pairs={{0,32},{32,64},{64,96},{96,0},{1,33},{33,65},{65,97},{97,1},{2,34}... | collective-permute-start | bytes 626696 | tf_op jit(solution)/shard_map/ppermute | solution.py:58
  47.1 10.7 %collective-permute-start.5 = (bf16[102,1024]{1,0:T(8,128)(2,1)S(1)}, bf16[102,1024]{1,0:T(8,128)(2,1)S(1)}, u32[]{:S(2)}, u32[]{:S(2)}) collective-permute-start(bf16[102,1024]{1,0:T(8,128)(2,1)S(1)} %get-tuple-element.84), channel_id=1, source_target_pairs={{0,64},{32,96},{64,0},{96,32},{1,65},{33,97},{65,1},{97,33},{2,66}... | collective-permute-start | bytes 626696 | tf_op jit(solution)/shard_map/ppermute | solution.py:58
  49.7 8.1 %collective-permute-start.4 = (bf16[102,1024]{1,0:T(8,128)(2,1)S(1)}, bf16[102,1024]{1,0:T(8,128)(2,1)S(1)}, u32[]{:S(2)}, u32[]{:S(2)}) collective-permute-start(bf16[102,1024]{1,0:T(8,128)(2,1)S(1)} %get-tuple-element.83), channel_id=1, source_target_pairs={{0,96},{32,0},{64,32},{96,64},{1,97},{33,1},{65,33},{97,65},{2,98}... | collective-permute-start | bytes 626696 | tf_op jit(solution)/shard_map/ppermute | solution.py:58
  52.3 5.6 %copy-start.13 = (bf16[102,1024]{1,0:T(8,128)(2,1)}, bf16[102,1024]{1,0:T(8,128)(2,1)S(1)}, u32[]{:S(2)}) copy-start(bf16[102,1024]{1,0:T(8,128)(2,1)S(1)} %collective-permute-done.6) | copy-start | bytes 626692
  52.3 12.7 %collective-permute-start.9 = (bf16[2,192,2048]{2,1,0:T(8,128)(2,1)S(1)}, bf16[2,192,2048]{2,1,0:T(8,128)(2,1)}, u32[]{:S(2)}, u32[]{:S(2)}) collective-permute-start(bf16[2,192,2048]{2,1,0:T(8,128)(2,1)S(1)} %get-tuple-element.31.refs_0_.refs_4_), channel_id=1, source_target_pairs={{0,1},{1,0},{2,3},{3,2},{4,5},{5,4},{6,7},{7,6},{8,9},{9,8},{10,11... | collective-permute-start | bytes 4718600 | tf_op jit(solution)/shard_map/ppermute | solution.py:46
  57.8 0.7 copy-start.12
  59.4 5.9 %collective-permute-start.10 = (bf16[2,192,2048]{2,1,0:T(8,128)(2,1)}, bf16[2,192,2048]{2,1,0:T(8,128)(2,1)S(1)}, u32[]{:S(2)}, u32[]{:S(2)}) collective-permute-start(bf16[2,192,2048]{2,1,0:T(8,128)(2,1)} %collective-permute-done.7.refs_1_.refs_5_), channel_id=1, source_target_pairs={{0,1},{1,0},{2,3},{3,2},{4,5},{5,4},{6,7},{7,6},{8,9},{9,8},{10,11... | collective-permute-start | bytes 4718600 | tf_op jit(solution)/shard_map/ppermute | solution.py:46
  62.1 5.5 %collective-permute-start.11 = (bf16[2,192,2048]{2,1,0:T(8,128)(2,1)}, bf16[2,192,2048]{2,1,0:T(8,128)(2,1)S(1)}, u32[]{:S(2)}, u32[]{:S(2)}) collective-permute-start(bf16[2,192,2048]{2,1,0:T(8,128)(2,1)} %collective-permute-done.8.refs_2_.refs_6_), channel_id=1, source_target_pairs={{0,1},{1,0},{2,3},{3,2},{4,5},{5,4},{6,7},{7,6},{8,9},{9,8},{10,11... | collective-permute-start | bytes 4718600 | tf_op jit(solution)/shard_map/ppermute | solution.py:46
  64.6 33.7 %copy-start.16 = (s32[4]{0:T(128)S(1)}, s32[4]{0:T(128)}, u32[]{:S(2)}) copy-start(s32[4]{0:T(128)} %constant.115.clone) | copy-start | bytes 52
  65.3 31.5 %copy-start.3 = (bf16[2,192,2048]{2,1,0:T(8,128)(2,1)}, bf16[2,192,2048]{2,1,0:T(8,128)(2,1)S(1)}, u32[]{:S(2)}) copy-start(bf16[2,192,2048]{2,1,0:T(8,128)(2,1)S(1)} %collective-permute-done.10.refs_9_.refs_13_) | copy-start | bytes 4718596
  67.6 29.2 %copy-start.4 = (bf16[2,192,2048]{2,1,0:T(8,128)(2,1)}, bf16[2,192,2048]{2,1,0:T(8,128)(2,1)S(1)}, u32[]{:S(2)}) copy-start(bf16[2,192,2048]{2,1,0:T(8,128)(2,1)S(1)} %collective-permute-done.11.refs_10_.refs_14_) | copy-start | bytes 4718596
  67.6 29.2 %collective-permute-start.12 = (bf16[3,192,2048]{2,1,0:T(8,128)(2,1)S(1)}, bf16[3,192,2048]{2,1,0:T(8,128)(2,1)S(1)}, u32[]{:S(2)}, u32[]{:S(2)}) collective-permute-start(bf16[3,192,2048]{2,1,0:T(8,128)(2,1)S(1)} %get-tuple-element.36), channel_id=1, source_target_pairs={{0,2},{1,9},{2,4},{3,11},{4,6},{5,13},{6,0},{7,15},{8,10},{9,17},{... | collective-permute-start | bytes 7077896 | tf_op jit(solution)/shard_map/ppermute | solution.py:42
  67.6 29.2 %collective-permute-start.13 = (bf16[3,192,2048]{2,1,0:T(8,128)(2,1)S(1)}, bf16[3,192,2048]{2,1,0:T(8,128)(2,1)}, u32[]{:S(2)}, u32[]{:S(2)}) collective-permute-start(bf16[3,192,2048]{2,1,0:T(8,128)(2,1)S(1)} %get-tuple-element.37), channel_id=1, source_target_pairs={{0,6},{1,25},{2,0},{3,27},{4,2},{5,29},{6,4},{7,31},{8,14},{9,1},{... | collective-permute-start | bytes 7077896 | tf_op jit(solution)/shard_map/ppermute | solution.py:42
  96.8 11.2 %copy-start = (bf16[3,192,2048]{2,1,0:T(8,128)(2,1)}, bf16[3,192,2048]{2,1,0:T(8,128)(2,1)S(1)}, u32[]{:S(2)}) copy-start(bf16[3,192,2048]{2,1,0:T(8,128)(2,1)S(1)} %collective-permute-done.12.refs_3_.refs_1_.refs_5_) | copy-start | bytes 7077892
  96.8 11.2 %collective-permute-start.14 = (bf16[3,192,2048]{2,1,0:T(8,128)(2,1)S(1)}, bf16[3,192,2048]{2,1,0:T(8,128)(2,1)}, u32[]{:S(2)}, u32[]{:S(2)}) collective-permute-start(bf16[3,192,2048]{2,1,0:T(8,128)(2,1)S(1)} %collective-permute-done.12.refs_3_.refs_1_.refs_5_), channel_id=1, source_target_pairs={{0,1},{1,0},{2,3},{3,2},{4,5},{5,4},{6,7},{7,6},{8,9},{9,8},{10,11... | collective-permute-start | bytes 7077896 | tf_op jit(solution)/shard_map/ppermute | solution.py:46
  98.2 9.9 %collective-permute-start.15 = (bf16[3,192,2048]{2,1,0:T(8,128)(2,1)}, bf16[3,192,2048]{2,1,0:T(8,128)(2,1)}, u32[]{:S(2)}, u32[]{:S(2)}) collective-permute-start(bf16[3,192,2048]{2,1,0:T(8,128)(2,1)} %collective-permute-done.13.refs_7_.refs_2_.refs_6_), channel_id=1, source_target_pairs={{0,1},{1,0},{2,3},{3,2},{4,5},{5,4},{6,7},{7,6},{8,9},{9,8},{10,11... | collective-permute-start | bytes 7077896 | tf_op jit(solution)/shard_map/ppermute | solution.py:46
  103.3 31.9 %collective-permute-start.18 = (bf16[2,192,2048]{2,1,0:T(8,128)(2,1)}, bf16[2,192,2048]{2,1,0:T(8,128)(2,1)}, u32[]{:S(2)}, u32[]{:S(2)}) collective-permute-start(bf16[2,192,2048]{2,1,0:T(8,128)(2,1)} %copy-done.1), channel_id=1, source_target_pairs={{0,1},{1,0},{2,3},{3,2},{4,5},{5,4},{6,7},{7,6},{8,9},{9,8},{10,11... | collective-permute-start | bytes 4718600 | tf_op jit(solution)/shard_map/ppermute | solution.py:46
  103.8 26.2 %collective-permute-start.16 = (bf16[1,192,2048]{2,1,0:T(8,128)(2,1)S(1)}, bf16[1,192,2048]{2,1,0:T(8,128)(2,1)S(1)}, u32[]{:S(2)}, u32[]{:S(2)}) collective-permute-start(bf16[1,192,2048]{2,1,0:T(8,128)(2,1)S(1)} %slice.212), channel_id=1, source_target_pairs={{0,2},{1,9},{2,4},{3,11},{4,6},{5,13},{6,0},{7,15},{8,10},{9,17},{... | collective-permute-start | bytes 2359304 | tf_op jit(solution)/shard_map/ppermute | solution.py:42
  105.1 25.7 %collective-permute-start.17 = (bf16[1,192,2048]{2,1,0:T(8,128)(2,1)S(1)}, bf16[1,192,2048]{2,1,0:T(8,128)(2,1)}, u32[]{:S(2)}, u32[]{:S(2)}) collective-permute-start(bf16[1,192,2048]{2,1,0:T(8,128)(2,1)S(1)} %slice.213), channel_id=1, source_target_pairs={{0,6},{1,25},{2,0},{3,27},{4,2},{5,29},{6,4},{7,31},{8,14},{9,1},{... | collective-permute-start | bytes 2359304 | tf_op jit(solution)/shard_map/ppermute | solution.py:42
  130.0 5.3 %copy-start.7 = (bf16[1,192,2048]{2,1,0:T(8,128)(2,1)}, bf16[1,192,2048]{2,1,0:T(8,128)(2,1)S(1)}, u32[]{:S(2)}) copy-start(bf16[1,192,2048]{2,1,0:T(8,128)(2,1)S(1)} %collective-permute-done.16.refs_3_) | copy-start | bytes 2359300
  130.0 5.2 %collective-permute-start.19 = (bf16[1,192,2048]{2,1,0:T(8,128)(2,1)S(1)}, bf16[1,192,2048]{2,1,0:T(8,128)(2,1)S(1)}, u32[]{:S(2)}, u32[]{:S(2)}) collective-permute-start(bf16[1,192,2048]{2,1,0:T(8,128)(2,1)S(1)} %collective-permute-done.16.refs_3_), channel_id=1, source_target_pairs={{0,1},{1,0},{2,3},{3,2},{4,5},{5,4},{6,7},{7,6},{8,9},{9,8},{10,11... | collective-permute-start | bytes 2359304 | tf_op jit(solution)/shard_map/ppermute | solution.py:46
  130.8 4.4 %collective-permute-start.20 = (bf16[1,192,2048]{2,1,0:T(8,128)(2,1)}, bf16[1,192,2048]{2,1,0:T(8,128)(2,1)S(1)}, u32[]{:S(2)}, u32[]{:S(2)}) collective-permute-start(bf16[1,192,2048]{2,1,0:T(8,128)(2,1)} %collective-permute-done.17.refs_7_), channel_id=1, source_target_pairs={{0,1},{1,0},{2,3},{3,2},{4,5},{5,4},{6,7},{7,6},{8,9},{9,8},{10,11... | collective-permute-start | bytes 2359304 | tf_op jit(solution)/shard_map/ppermute | solution.py:46
  131.8 22.4 %collective-permute-start.23 = (bf16[576,768]{1,0:T(8,128)(2,1)}, bf16[576,768]{1,0:T(8,128)(2,1)S(1)}, u32[]{:S(2)}, u32[]{:S(2)}) collective-permute-start(bf16[576,768]{1,0:T(8,128)(2,1)} %get-tuple-element.40.refs_0_), channel_id=1, source_target_pairs={{0,32},{32,64},{64,96},{96,0},{1,33},{33,65},{65,97},{97,1},{2,34}... | collective-permute-start | bytes 2654216 | tf_op jit(solution)/shard_map/ppermute | solution.py:58
  132.3 21.9 %collective-permute-start.21 = (bf16[576,768]{1,0:T(8,128)(2,1)}, bf16[576,768]{1,0:T(8,128)(2,1)S(1)}, u32[]{:S(2)}, u32[]{:S(2)}) collective-permute-start(bf16[576,768]{1,0:T(8,128)(2,1)} %get-tuple-element.40.refs_0_), channel_id=1, source_target_pairs={{0,96},{32,0},{64,32},{96,64},{1,97},{33,1},{65,33},{97,65},{2,98}... | collective-permute-start | bytes 2654216 | tf_op jit(solution)/shard_map/ppermute | solution.py:58
  135.3 0.9 copy-start.8
  135.3 1.2 copy-start.9
  154.0 2.2 copy-start.6
  154.2 3.6 %copy-start.10 = (bf16[576,768]{1,0:T(8,128)(2,1)}, bf16[576,768]{1,0:T(8,128)(2,1)S(1)}, u32[]{:S(2)}) copy-start(bf16[576,768]{1,0:T(8,128)(2,1)S(1)} %collective-permute-done.23.refs_4_) | copy-start | bytes 2654212
  154.2 3.6 %copy-start.11 = (bf16[576,768]{1,0:T(8,128)(2,1)}, bf16[576,768]{1,0:T(8,128)(2,1)S(1)}, u32[]{:S(2)}) copy-start(bf16[576,768]{1,0:T(8,128)(2,1)S(1)} %collective-permute-done.21.refs_1_) | copy-start | bytes 2654212
  157.8 51.6 %collective-permute-start.22 = (bf16[1440,768]{1,0:T(8,128)(2,1)S(1)}, bf16[1440,768]{1,0:T(8,128)(2,1)}, u32[]{:S(2)}, u32[]{:S(2)}) collective-permute-start(bf16[1440,768]{1,0:T(8,128)(2,1)S(1)} %get-tuple-element.59), channel_id=1, source_target_pairs={{0,96},{32,0},{64,32},{96,64},{1,97},{33,1},{65,33},{97,65},{2,98}... | collective-permute-start | bytes 6635528 | tf_op jit(solution)/shard_map/ppermute | solution.py:58
  158.2 49.4 %collective-permute-start.24 = (bf16[1440,768]{1,0:T(8,128)(2,1)}, bf16[1440,768]{1,0:T(8,128)(2,1)}, u32[]{:S(2)}, u32[]{:S(2)}) collective-permute-start(bf16[1440,768]{1,0:T(8,128)(2,1)} %get-tuple-element.58), channel_id=1, source_target_pairs={{0,32},{32,64},{64,96},{96,0},{1,33},{33,65},{65,97},{97,1},{2,34}... | collective-permute-start | bytes 6635528 | tf_op jit(solution)/shard_map/ppermute | solution.py:58
  175.5 69.3 %all-to-all-start.1 = ((bf16[32,72,1024]{2,1,0:T(8,128)(2,1)}), bf16[32,72,1024]{2,1,0:T(8,128)(2,1)}, u32[]{:S(2)}, u32[]{:S(2)}) async-start(bf16[32,72,1024]{2,1,0:T(8,128)(2,1)} %rowgrad.1), calls=%async_computation.1 | async-start | bytes 9437184 | tf_op jit(solution)/shard_map/all_to_all | solution.py:492
  208.8 19.9 %collective-permute-start.25 = (bf16[576,768]{1,0:T(8,128)(2,1)S(1)}, bf16[576,768]{1,0:T(8,128)(2,1)S(1)}, u32[]{:S(2)}, u32[]{:S(2)}) collective-permute-start(bf16[576,768]{1,0:T(8,128)(2,1)S(1)} %slice.171), channel_id=1, source_target_pairs={{0,32},{32,64},{64,96},{96,0},{1,33},{33,65},{65,97},{97,1},{2,34}... | collective-permute-start | bytes 2654216 | tf_op jit(solution)/shard_map/ppermute | solution.py:58
  210.6 19.3 %collective-permute-start.26 = (bf16[576,768]{1,0:T(8,128)(2,1)S(1)}, bf16[576,768]{1,0:T(8,128)(2,1)S(1)}, u32[]{:S(2)}, u32[]{:S(2)}) collective-permute-start(bf16[576,768]{1,0:T(8,128)(2,1)S(1)} %slice.172), channel_id=1, source_target_pairs={{0,96},{32,0},{64,32},{96,64},{1,97},{33,1},{65,33},{97,65},{2,98}... | collective-permute-start | bytes 2654216 | tf_op jit(solution)/shard_map/ppermute | solution.py:58
Sparse Core Ops, SparseCore 0:
  96.9 80.8 all-gather.1

commit v5 on v4

--- a/solution.py
+++ b/solution.py
@@ -335,17 +335,23 @@
     )(slot, prob, xi, yi, blocks)
 
 
-def weight_kernel(xy, *refs, count):
+def weight_kernel(xy, *refs, count, only):
     outs, cat = refs[-1 - count : -1], refs[-1]
     m = pl.program_id(0)
     at = 0
-    for h in refs[: -1 - count]:
-        if h.ndim == 3:
-            cat[at : at + h.shape[1], :] = h[0]
-            at += h.shape[1]
-        else:
-            cat[at : at + h.shape[0], :] = h[...]
-            at += h.shape[0]
+    for h, step_of in zip(refs[: -1 - count], only):
+        rows = h.shape[-2]
+        if step_of is None:
+            cat[at : at + rows, :] = h[0] if h.ndim == 3 else h[...]
+            at += rows
+            continue
+
+        @pl.when(m == step_of)
+        def _(h=h, to=slice(at, at + rows)):
+            cat[to, :] = h[...]
+
+        if step_of == count - 1:
+            at += rows
     res = dot(xy[...], cat[...]).astype(BF16)
     for i, out in enumerate(outs):
 
@@ -360,13 +366,15 @@
     shape = (ff, wide) if flip else (wide, ff)
 
     def spec(block):
-        array, rows, index = block
+        array, rows, index = block[:3]
         if array.ndim == 3:
             return pl.BlockSpec((1, rows, ff), lambda m: (index(m), 0, 0))
         return pl.BlockSpec((rows, ff), lambda m: (index(m), 0))
 
     return pl.pallas_call(
-        functools.partial(weight_kernel, count=count),
+        functools.partial(
+            weight_kernel, count=count, only=[h[3] if len(h) > 3 else None for h in hs]
+        ),
         grid=(count,),
         in_specs=[pl.BlockSpec((wide, depth), lambda m: (side, 0))] + [spec(h) for h in hs],
         out_specs=[pl.BlockSpec(shape, lambda m: (0, 0))] * count,
@@ -377,7 +385,7 @@
             flops=HEAVY * 2 * depth * wide * ff * count, bytes_accessed=depth * (2 * wide + 2 * ff * count), transcendentals=0
         ),
         name="weight_grads",
-    )(xy, *(h for h, _, _ in hs))
+    )(xy, *(h[0] for h in hs))
 
 
 def on_device(tokens, out_grad, expert_ids, route_probs, w_gate, w_up, w_down):
@@ -494,10 +502,10 @@
     hids = [(hid, 2 * half, at(0)), (hid_succ, 2 * half, at(0)), (from_prev, half, at(0)),
             (from_succ, half, at(0)), (hid_prev, 2 * half, at(0))]
     (down_grad,) = weights(xy, 1, hids, 1, True)
-    far_dd = jnp.stack(after((far_gate, far_up), down_grad))
+    far_gate, far_up = after((far_gate, far_up), down_grad)
     first_half, second_half = (lambda m: 1 + 2 * m), (lambda m: 2 + 2 * m)
     dds = [(dd, 2 * half, lambda m: m), (from_succ, half, first_half), (from_succ, half, second_half),
-           (far_dd, 2 * half, lambda m: m), (from_prev, half, first_half), (from_prev, half, second_half)]
+           (far_gate, 2 * half, at(0), 0), (far_up, 2 * half, at(0), 1), (from_prev, half, first_half), (from_prev, half, second_half)]
     gate_grad, up_grad = weights(xy, 0, dds, 2, False)
     back = after(back, gate_grad)
     piece = cap * jnp.arange(4, dtype=F32)

time: 260 us -> 260 us (level)
  transfers between devices with their start and end apart: 30 -> 30, of which waited for: 12 -> 12; matrix products, arithmetic and copies ran while one was open for 11% -> 11% of each run, Pallas kernels for 36% -> 37%
where the time goes in v5:
time: 260 us; the launch traced here: 256 us
  Pallas kernels  93.3 us (36%)
  waiting for transfers between devices  58 us (22%)
  starting transfers between devices  50.6 us (19%)
  local copies, waits for them, and re-layouts  23.3 us (9%)
  between operations  14.6 us (6%)
  other arithmetic  12.1 us (5%)
  matrix products  3.61 us (1%)
    ppermute x9, waiting for transfers between devices, step(): return lax.ppermute(v, 'expert', expert_pairs(ring, shift))  37.6 us
    pallas_call x2, Pallas kernels, weights(): pl.pallas_call(functools.partial(weight_kernel, count=count, only=[h[3] i...  22.2 us
    pallas_call x1, Pallas kernels, hidden_rows(): pl.pallas_call(functools.partial(hidden_kernel, half=half), grid_spec=plt...  22 us
    pallas_call x1, Pallas kernels, cotangent_rows(): pl.pallas_call(functools.partial(cotangent_kernel, half=half), grid_spec=...  17.5 us
    pallas_call x1, Pallas kernels, gather_columns(): pl.pallas_call(gather_kernel, grid=(2, 2), in_specs=[meta, meta, whole(xi...  17.2 us
    ppermute x9, waiting for transfers between devices, over_groups(): return lax.ppermute(v, 'dp', [(s, (s + shift) % 4) for s in range(4)])  17.1 us
    pallas_call x1, Pallas kernels, rowgrad(): pl.pallas_call(functools.partial(rowgrad_kernel, cap=cap), grid=(4,), in_...  14.4 us
    ppermute x9, starting transfers between devices, step(): return lax.ppermute(v, 'expert', expert_pairs(ring, shift))  13.6 us
  transfers between devices with their start and end apart: 30, of which 12 were waited for; matrix products, arithmetic and copies ran while one was open for 11% of the time, Pallas kernels for 37%

profile of v5, /device:TPU:1, one launch (start us, length us, event | category | flops | bytes accessed | tf_op | source)
XLA Modules:
  0.0 255.6 jit_solution(5046256604577135600)
XLA Ops:
  7.2 1.1 fusion.5
  8.3 1.5 collective-permute-start
  11.1 1.4 select_bitcast_fusion.1
  12.6 2.9 %collective-permute-start.3 = (bf16[2,2,48,2048]{3,2,1,0:T(8,128)(2,1)S(1)}, bf16[2,2,48,2048]{3,2,1,0:T(8,128)(2,1)S(1)}, u32[]{:S(2)}, u32[]{:S(2)}) collective-permute-start(bf16[2,2,48,2048]{3,2,1,0:T(8,128)(2,1)S(1)} %pad_maximum_fusion.7), channel_id=1, source_target_pairs={{0,16},{1,5},{2,18},{3,7},{4,20},{5,1},{6,22},{7,3},{8,24},{9,13},... | collective-permute-start | bytes 2359304 | tf_op jit(solution)/shard_map/ppermute | solution.py:42
  17.3 7.7 %all-to-all-start = ((f32[32,2,48]{2,1,0:T(2,128)}), f32[32,2,48]{2,1,0:T(2,128)}, u32[]{:S(2)}, u32[]{:S(2)}) async-start(f32[32,2,48]{2,1,0:T(2,128)} %copy.45), calls=%async_computation | async-start | bytes 65536 | tf_op jit(solution)/shard_map/all_to_all | solution.py:422
  25.1 1.5 collective-permute-start.1
  26.7 7.5 %collective-permute-done.2 = bf16[2,2,48,2048]{3,2,1,0:T(8,128)(2,1)S(1)} collective-permute-done((bf16[2,2,48,2048]{3,2,1,0:T(8,128)(2,1)S(1)}, bf16[2,2,48,2048]{3,2,1,0:T(8,128)(2,1)S(1)}, u32[]{:S(2)}, u32[]{:S(2)}) %collective-permute-start.2) | collective-permute-done | bytes 786464 | tf_op jit(solution)/shard_map/ppermute | solution.py:42
  34.2 3.5 %collective-permute-done.1 = bf16[2,2,48,2048]{3,2,1,0:T(8,128)(2,1)S(1)} collective-permute-done((bf16[2,2,48,2048]{3,2,1,0:T(8,128)(2,1)S(1)}, bf16[2,2,48,2048]{3,2,1,0:T(8,128)(2,1)S(1)}, u32[]{:S(2)}, u32[]{:S(2)}) %collective-permute-start.1) | collective-permute-done | bytes 786464 | tf_op jit(solution)/shard_map/ppermute | solution.py:42
  38.1 1.1 collective-permute-start.7
  39.2 1.6 collective-permute-start.8
  40.9 1.9 pad_maximum_fusion.6
  44.5 1.2 constant_dynamic-slice_fusion.2
  45.7 1.4 collective-permute-start.6
  47.1 2.6 %collective-permute-start.5 = (bf16[102,1024]{1,0:T(8,128)(2,1)S(1)}, bf16[102,1024]{1,0:T(8,128)(2,1)S(1)}, u32[]{:S(2)}, u32[]{:S(2)}) collective-permute-start(bf16[102,1024]{1,0:T(8,128)(2,1)S(1)} %get-tuple-element.84), channel_id=1, source_target_pairs={{0,64},{32,96},{64,0},{96,32},{1,65},{33,97},{65,1},{97,33},{2,66}... | collective-permute-start | bytes 626696 | tf_op jit(solution)/shard_map/ppermute | solution.py:58
  49.7 1.1 collective-permute-start.4
  50.8 1.5 collective-permute-done.6
  52.3 3.6 %collective-permute-start.9 = (bf16[2,192,2048]{2,1,0:T(8,128)(2,1)S(1)}, bf16[2,192,2048]{2,1,0:T(8,128)(2,1)}, u32[]{:S(2)}, u32[]{:S(2)}) collective-permute-start(bf16[2,192,2048]{2,1,0:T(8,128)(2,1)S(1)} %get-tuple-element.31.refs_0_.refs_4_), channel_id=1, source_target_pairs={{0,1},{1,0},{2,3},{3,2},{4,5},{5,4},{6,7},{7,6},{8,9},{9,8},{10,11... | collective-permute-start | bytes 4718600 | tf_op jit(solution)/shard_map/ppermute | solution.py:46
  55.9 2.0 collective-permute-done.5
  59.4 2.7 %collective-permute-start.10 = (bf16[2,192,2048]{2,1,0:T(8,128)(2,1)}, bf16[2,192,2048]{2,1,0:T(8,128)(2,1)S(1)}, u32[]{:S(2)}, u32[]{:S(2)}) collective-permute-start(bf16[2,192,2048]{2,1,0:T(8,128)(2,1)} %collective-permute-done.7.refs_1_.refs_5_), channel_id=1, source_target_pairs={{0,1},{1,0},{2,3},{3,2},{4,5},{5,4},{6,7},{7,6},{8,9},{9,8},{10,11... | collective-permute-start | bytes 4718600 | tf_op jit(solution)/shard_map/ppermute | solution.py:46
  62.2 1.2 slice.211
  63.4 1.2 slice.207
  65.3 2.2 collective-permute-done.11.refs_10_.refs_14_
  67.6 2.7 %collective-permute-start.13 = (bf16[3,192,2048]{2,1,0:T(8,128)(2,1)S(1)}, bf16[3,192,2048]{2,1,0:T(8,128)(2,1)}, u32[]{:S(2)}, u32[]{:S(2)}) collective-permute-start(bf16[3,192,2048]{2,1,0:T(8,128)(2,1)S(1)} %get-tuple-element.37), channel_id=1, source_target_pairs={{0,6},{1,25},{2,0},{3,27},{4,2},{5,29},{6,4},{7,31},{8,14},{9,1},{... | collective-permute-start | bytes 7077896 | tf_op jit(solution)/shard_map/ppermute | solution.py:42
  70.3 26.5 %collective-permute-done.12.refs_3_.refs_1_.refs_5_ = bf16[3,192,2048]{2,1,0:T(8,128)(2,1)S(1)} collective-permute-done((bf16[3,192,2048]{2,1,0:T(8,128)(2,1)S(1)}, bf16[3,192,2048]{2,1,0:T(8,128)(2,1)S(1)}, u32[]{:S(2)}, u32[]{:S(2)}) %collective-permute-start.12) | collective-permute-done | bytes 2359328 | tf_op jit(solution)/shard_map/ppermute | solution.py:42
  96.9 1.3 collective-permute-start.14
  99.8 1.4 gather_fusion
  103.9 1.2 slice.213
  105.1 2.9 %collective-permute-start.17 = (bf16[1,192,2048]{2,1,0:T(8,128)(2,1)S(1)}, bf16[1,192,2048]{2,1,0:T(8,128)(2,1)}, u32[]{:S(2)}, u32[]{:S(2)}) collective-permute-start(bf16[1,192,2048]{2,1,0:T(8,128)(2,1)S(1)} %slice.213), channel_id=1, source_target_pairs={{0,6},{1,25},{2,0},{3,27},{4,2},{5,29},{6,4},{7,31},{8,14},{9,1},{... | collective-permute-start | bytes 2359304 | tf_op jit(solution)/shard_map/ppermute | solution.py:42
  108.0 22.0 %hidden_rows.1 = (bf16[576,768]{1,0:T(8,128)(2,1)}, f32[576,768]{1,0:T(8,128)}, f32[576,768]{1,0:T(8,128)}, bf16[576,1024]{1,0:T(8,128)(2,1)}, bf16[2,2,288,768]{3,2,1,0:T(8,128)(2,1)}, /*index=5*/f32[576,128]{1,0:T(8,128)}) custom-call(s32[2]{0:T(128)} %pad_add_fusion.place, s32[2,1,768]{2,1,0:T(1,128)} %squeeze.70.slot_own, ...), custom_call_target="tpu_custom_call" | custom-call | flops 10871635968 | bytes 25165824 | tf_op jit(solution)/shard_map/hidden_rows/pallas_call | solution.py:182
  132.3 2.2 collective-permute-start.21
  136.4 17.5 %cotangent_rows.1 = (bf16[2,576,768]{2,1,0:T(8,128)(2,1)}, bf16[576,1024]{1,0:T(8,128)(2,1)}) custom-call(s32[2]{0:T(128)} %pad_add_fusion.place, bf16[2,2,288,768]{3,2,1,0:T(8,128)(2,1)} %get-tuple-element.38.hot, f32[576,128]{1,0:T(8,128)} %get-tuple-element.39.scale, bf16[2,192,2048]{2,1,0:T(8,128)(2,1)} %copy-done.1, bf16[3,192,2048]{2,1,0:T(8,128)(2,1)} %copy-done, ...), custom_call_target="tpu_custom_call" | custom-call | flops 7247757312 | bytes 18874368 | tf_op jit(solution)/shard_map/cotangent_rows/pallas_call | solution.py:215
  154.3 1.9 copy-done.6
  156.1 1.6 pad_maximum_fusion.3
  158.2 1.0 collective-permute-start.24
  161.1 14.4 %rowgrad.1 = bf16[32,72,1024]{2,1,0:T(8,128)(2,1)} custom-call(bf16[2,576,768]{2,1,0:T(8,128)(2,1)} %get-tuple-element.45.h.refs_0_, bf16[4096,768]{1,0:T(8,128)(2,1)} %bitcast.118, bf16[4096,768]{1,0:T(8,128)(2,1)} %bitcast.120), custom_call_target="tpu_custom_call" | custom-call | flops 7247757312 | bytes 17301504 | tf_op jit(solution)/shard_map/rowgrad/pallas_call | solution.py:263
  175.4 6.4 %all-to-all-start.1 = ((bf16[32,72,1024]{2,1,0:T(8,128)(2,1)}), bf16[32,72,1024]{2,1,0:T(8,128)(2,1)}, u32[]{:S(2)}, u32[]{:S(2)}) async-start(bf16[32,72,1024]{2,1,0:T(8,128)(2,1)} %rowgrad.1), calls=%async_computation.1 | async-start | bytes 9437184 | tf_op jit(solution)/shard_map/all_to_all | solution.py:500
  181.9 17.2 %gather_columns.1.xy = bf16[2048,2304]{1,0:T(8,128)(2,1)} custom-call(s32[4,2,1,768]{3,2,1,0:T(1,128)} %reshape.607.slot, f32[4,2,1,768]{3,2,1,0:T(1,128)} %reshape.611.prob, bf16[576,1024]{1,0:T(8,128)(2,1)} %get-tuple-element.47.xi, bf16[576,1024]{1,0:T(8,128)(2,1)} %get-tuple-element.48.yi, bf16[16,2,3,2,48,1024]{5,4,3,2,1,0:T(8,128)(2,1)} %bitcast.115), custom_call_target="tpu_custom_call" | custom-call | flops 1 | bytes 1 | tf_op jit(solution)/shard_map/gather_columns/pallas_call | solution.py:315
  199.3 1.0 iota_compare_fusion
  200.2 2.1 eq.55
  202.3 5.2 %collective-permute-done.24.refs_2_.refs_5_.refs_6_ = bf16[1440,768]{1,0:T(8,128)(2,1)} collective-permute-done((bf16[1440,768]{1,0:T(8,128)(2,1)}, bf16[1440,768]{1,0:T(8,128)(2,1)}, u32[]{:S(2)}, u32[]{:S(2)}) %collective-permute-start.24) | collective-permute-done | bytes 2211872 | tf_op jit(solution)/shard_map/ppermute | solution.py:58
  207.6 1.2 slice.171
  209.3 1.2 slice.172
  210.5 2.6 %collective-permute-start.26 = (bf16[576,768]{1,0:T(8,128)(2,1)S(1)}, bf16[576,768]{1,0:T(8,128)(2,1)S(1)}, u32[]{:S(2)}, u32[]{:S(2)}) collective-permute-start(bf16[576,768]{1,0:T(8,128)(2,1)S(1)} %slice.172), channel_id=1, source_target_pairs={{0,96},{32,0},{64,32},{96,64},{1,97},{33,1},{65,33},{97,65},{2,98}... | collective-permute-start | bytes 2654216 | tf_op jit(solution)/shard_map/ppermute | solution.py:58
  213.1 8.4 %weight_grads.2 = bf16[768,1024]{1,0:T(8,128)(2,1)} custom-call(bf16[2048,2304]{1,0:T(8,128)(2,1)} %gather_columns.1.xy, bf16[576,768]{1,0:T(8,128)(2,1)} %get-tuple-element.40.refs_0_, bf16[576,768]{1,0:T(8,128)(2,1)} %copy-done.11, bf16[1440,768]{1,0:T(8,128)(2,1)} %collective-permute-done.24.refs_2_.refs_5_.refs_6_, ...), custom_call_target="tpu_custom_call" | custom-call | flops 14495514624 | bytes 8257536 | tf_op jit(solution)/shard_map/weight_grads/pallas_call | solution.py:374
  221.4 7.2 %collective-permute-done.25.refs_3_ = bf16[576,768]{1,0:T(8,128)(2,1)S(1)} collective-permute-done((bf16[576,768]{1,0:T(8,128)(2,1)S(1)}, bf16[576,768]{1,0:T(8,128)(2,1)S(1)}, u32[]{:S(2)}, u32[]{:S(2)}) %collective-permute-start.25) | collective-permute-done | bytes 884768 | tf_op jit(solution)/shard_map/ppermute | solution.py:58
  228.7 1.1 collective-permute-done.26.refs_4_
  230.7 13.9 %weight_grads.3 = (bf16[1024,768]{1,0:T(8,128)(2,1)}, bf16[1024,768]{1,0:T(8,128)(2,1)}) custom-call(bf16[2048,2304]{1,0:T(8,128)(2,1)} %gather_columns.1.xy, bf16[2,576,768]{2,1,0:T(8,128)(2,1)} %get-tuple-element.45.h.refs_0_, bf16[1440,768]{1,0:T(8,128)(2,1)} %collective-permute-done.22.refs_3_.refs_1_.refs_2_, ...), custom_call_target="tpu_custom_call" | custom-call | flops 28991029248 | bytes 11796480 | tf_op jit(solution)/shard_map/weight_grads/pallas_call | solution.py:374
  244.6 3.4 %convolution_convert_fusion = bf16[192,1024]{1,0:T(8,128)(2,1)S(1)} fusion(pred[192,2304]{1,0:T(32,128)(4,1)S(1)} %eq.55, bf16[2304,1024]{1,0:T(8,128)(2,1)} %bitcast.49), kind=kOutput, calls=%fused_computation.8 | convolution fusion | flops 906166272 | bytes 5554176 | tf_op jit(solution)/shard_map/dot_general | solution.py:22
  (143 shorter events, 21.2 us)
Async XLA Ops:
  7.2 8.3 %copy-start.14 = (s32[48,8]{0,1:T(8,128)S(1)}, s32[48,8]{0,1:T(8,128)}, u32[]{:S(2)}) copy-start(s32[48,8]{0,1:T(8,128)} %param.10) | copy-start | bytes 4612
  7.2 8.3 %copy-start.15 = (f32[48,8]{0,1:T(8,128)S(1)}, f32[48,8]{0,1:T(8,128)}, u32[]{:S(2)}) copy-start(f32[48,8]{0,1:T(8,128)} %param.11) | copy-start | bytes 4612
  8.3 2.9 %collective-permute-start = (bf16[2,48,2048]{2,1,0:T(8,128)(2,1)S(1)}, bf16[2,48,2048]{2,1,0:T(8,128)(2,1)S(1)}, u32[]{:S(2)}, u32[]{:S(2)}) collective-permute-start(bf16[2,48,2048]{2,1,0:T(8,128)(2,1)S(1)} %fusion.5), channel_id=1, source_target_pairs={{0,1},{1,0},{2,3},{3,2},{4,5},{5,4},{6,7},{7,6},{8,9},{9,8},{10,11... | collective-permute-start | bytes 1179656 | tf_op jit(solution)/shard_map/ppermute | solution.py:46
  12.6 14.0 %collective-permute-start.3 = (bf16[2,2,48,2048]{3,2,1,0:T(8,128)(2,1)S(1)}, bf16[2,2,48,2048]{3,2,1,0:T(8,128)(2,1)S(1)}, u32[]{:S(2)}, u32[]{:S(2)}) collective-permute-start(bf16[2,2,48,2048]{3,2,1,0:T(8,128)(2,1)S(1)} %pad_maximum_fusion.7), channel_id=1, source_target_pairs={{0,16},{1,5},{2,18},{3,7},{4,20},{5,1},{6,22},{7,3},{8,24},{9,13},... | collective-permute-start | bytes 2359304 | tf_op jit(solution)/shard_map/ppermute | solution.py:42
  15.8 18.4 %collective-permute-start.2 = (bf16[2,2,48,2048]{3,2,1,0:T(8,128)(2,1)S(1)}, bf16[2,2,48,2048]{3,2,1,0:T(8,128)(2,1)S(1)}, u32[]{:S(2)}, u32[]{:S(2)}) collective-permute-start(bf16[2,2,48,2048]{3,2,1,0:T(8,128)(2,1)S(1)} %pad_maximum_fusion.7), channel_id=1, source_target_pairs={{0,24},{1,7},{2,26},{3,1},{4,28},{5,3},{6,30},{7,5},{8,0},{9,15},{... | collective-permute-start | bytes 2359304 | tf_op jit(solution)/shard_map/ppermute | solution.py:42
  17.3 20.8 %all-to-all-start = ((f32[32,2,48]{2,1,0:T(2,128)}), f32[32,2,48]{2,1,0:T(2,128)}, u32[]{:S(2)}, u32[]{:S(2)}) async-start(f32[32,2,48]{2,1,0:T(2,128)} %copy.45), calls=%async_computation | async-start | bytes 65536 | tf_op jit(solution)/shard_map/all_to_all | solution.py:422
  25.0 156.9 %all-gather.2.cloned.1.call-start = ((), (), s32[]{:S(2)}) async-start(), calls=%async_computation.2 | async-start | bytes 19464192 | tf_op jit(solution)/shard_map/all_gather | solution.py:478
  25.1 12.7 %collective-permute-start.1 = (bf16[2,2,48,2048]{3,2,1,0:T(8,128)(2,1)S(1)}, bf16[2,2,48,2048]{3,2,1,0:T(8,128)(2,1)S(1)}, u32[]{:S(2)}, u32[]{:S(2)}) collective-permute-start(bf16[2,2,48,2048]{3,2,1,0:T(8,128)(2,1)S(1)} %pad_maximum_fusion.7), channel_id=1, source_target_pairs={{0,8},{1,3},{2,10},{3,5},{4,12},{5,7},{6,14},{7,1},{8,16},{9,11},{... | collective-permute-start | bytes 2359304 | tf_op jit(solution)/shard_map/ppermute | solution.py:42
  37.8 3.1 %copy-start.5 = (bf16[48,4096]{1,0:T(8,128)(2,1)S(1)}, bf16[48,4096]{1,0:T(8,128)(2,1)}, u32[]{:S(2)}) copy-start(bf16[48,4096]{1,0:T(8,128)(2,1)} %param.8) | copy-start | bytes 1179652
  38.1 17.8 %copy-start.2 = (bf16[2,192,2048]{2,1,0:T(8,128)(2,1)}, bf16[2,192,2048]{2,1,0:T(8,128)(2,1)S(1)}, u32[]{:S(2)}) copy-start(bf16[2,192,2048]{2,1,0:T(8,128)(2,1)S(1)} %get-tuple-element.31.refs_0_.refs_4_) | copy-start | bytes 4718596
  38.1 26.5 %copy-start.1 = (bf16[2,192,2048]{2,1,0:T(8,128)(2,1)}, bf16[2,192,2048]{2,1,0:T(8,128)(2,1)S(1)}, u32[]{:S(2)}) copy-start(bf16[2,192,2048]{2,1,0:T(8,128)(2,1)S(1)} %get-tuple-element.33.refs_0_.refs_4_) | copy-start | bytes 4718596
  38.1 21.3 %collective-permute-start.7 = (bf16[2,192,2048]{2,1,0:T(8,128)(2,1)S(1)}, bf16[2,192,2048]{2,1,0:T(8,128)(2,1)}, u32[]{:S(2)}, u32[]{:S(2)}) collective-permute-start(bf16[2,192,2048]{2,1,0:T(8,128)(2,1)S(1)} %get-tuple-element.31.refs_0_.refs_4_), channel_id=1, source_target_pairs={{0,2},{1,9},{2,4},{3,11},{4,6},{5,13},{6,0},{7,15},{8,10},{9,17},{... | collective-permute-start | bytes 4718600 | tf_op jit(solution)/shard_map/ppermute | solution.py:42
  39.2 22.9 %collective-permute-start.8 = (bf16[2,192,2048]{2,1,0:T(8,128)(2,1)S(1)}, bf16[2,192,2048]{2,1,0:T(8,128)(2,1)}, u32[]{:S(2)}, u32[]{:S(2)}) collective-permute-start(bf16[2,192,2048]{2,1,0:T(8,128)(2,1)S(1)} %get-tuple-element.31.refs_0_.refs_4_), channel_id=1, source_target_pairs={{0,6},{1,25},{2,0},{3,27},{4,2},{5,29},{6,4},{7,31},{8,14},{9,1},{... | collective-permute-start | bytes 4718600 | tf_op jit(solution)/shard_map/ppermute | solution.py:42
  45.7 6.5 %collective-permute-start.6 = (bf16[102,1024]{1,0:T(8,128)(2,1)S(1)}, bf16[102,1024]{1,0:T(8,128)(2,1)S(1)}, u32[]{:S(2)}, u32[]{:S(2)}) collective-permute-start(bf16[102,1024]{1,0:T(8,128)(2,1)S(1)} %get-tuple-element.85), channel_id=1, source_target_pairs={{0,32},{32,64},{64,96},{96,0},{1,33},{33,65},{65,97},{97,1},{2,34}... | collective-permute-start | bytes 626696 | tf_op jit(solution)/shard_map/ppermute | solution.py:58
  47.1 10.7 %collective-permute-start.5 = (bf16[102,1024]{1,0:T(8,128)(2,1)S(1)}, bf16[102,1024]{1,0:T(8,128)(2,1)S(1)}, u32[]{:S(2)}, u32[]{:S(2)}) collective-permute-start(bf16[102,1024]{1,0:T(8,128)(2,1)S(1)} %get-tuple-element.84), channel_id=1, source_target_pairs={{0,64},{32,96},{64,0},{96,32},{1,65},{33,97},{65,1},{97,33},{2,66}... | collective-permute-start | bytes 626696 | tf_op jit(solution)/shard_map/ppermute | solution.py:58
  49.7 8.1 %collective-permute-start.4 = (bf16[102,1024]{1,0:T(8,128)(2,1)S(1)}, bf16[102,1024]{1,0:T(8,128)(2,1)S(1)}, u32[]{:S(2)}, u32[]{:S(2)}) collective-permute-start(bf16[102,1024]{1,0:T(8,128)(2,1)S(1)} %get-tuple-element.83), channel_id=1, source_target_pairs={{0,96},{32,0},{64,32},{96,64},{1,97},{33,1},{65,33},{97,65},{2,98}... | collective-permute-start | bytes 626696 | tf_op jit(solution)/shard_map/ppermute | solution.py:58
  52.3 5.6 %copy-start.13 = (bf16[102,1024]{1,0:T(8,128)(2,1)}, bf16[102,1024]{1,0:T(8,128)(2,1)S(1)}, u32[]{:S(2)}) copy-start(bf16[102,1024]{1,0:T(8,128)(2,1)S(1)} %collective-permute-done.6) | copy-start | bytes 626692
  52.3 12.7 %collective-permute-start.9 = (bf16[2,192,2048]{2,1,0:T(8,128)(2,1)S(1)}, bf16[2,192,2048]{2,1,0:T(8,128)(2,1)}, u32[]{:S(2)}, u32[]{:S(2)}) collective-permute-start(bf16[2,192,2048]{2,1,0:T(8,128)(2,1)S(1)} %get-tuple-element.31.refs_0_.refs_4_), channel_id=1, source_target_pairs={{0,1},{1,0},{2,3},{3,2},{4,5},{5,4},{6,7},{7,6},{8,9},{9,8},{10,11... | collective-permute-start | bytes 4718600 | tf_op jit(solution)/shard_map/ppermute | solution.py:46
  59.4 5.9 %collective-permute-start.10 = (bf16[2,192,2048]{2,1,0:T(8,128)(2,1)}, bf16[2,192,2048]{2,1,0:T(8,128)(2,1)S(1)}, u32[]{:S(2)}, u32[]{:S(2)}) collective-permute-start(bf16[2,192,2048]{2,1,0:T(8,128)(2,1)} %collective-permute-done.7.refs_1_.refs_5_), channel_id=1, source_target_pairs={{0,1},{1,0},{2,3},{3,2},{4,5},{5,4},{6,7},{7,6},{8,9},{9,8},{10,11... | collective-permute-start | bytes 4718600 | tf_op jit(solution)/shard_map/ppermute | solution.py:46
  62.1 5.5 %collective-permute-start.11 = (bf16[2,192,2048]{2,1,0:T(8,128)(2,1)}, bf16[2,192,2048]{2,1,0:T(8,128)(2,1)S(1)}, u32[]{:S(2)}, u32[]{:S(2)}) collective-permute-start(bf16[2,192,2048]{2,1,0:T(8,128)(2,1)} %collective-permute-done.8.refs_2_.refs_6_), channel_id=1, source_target_pairs={{0,1},{1,0},{2,3},{3,2},{4,5},{5,4},{6,7},{7,6},{8,9},{9,8},{10,11... | collective-permute-start | bytes 4718600 | tf_op jit(solution)/shard_map/ppermute | solution.py:46
  64.6 33.7 %copy-start.16 = (s32[4]{0:T(128)S(1)}, s32[4]{0:T(128)}, u32[]{:S(2)}) copy-start(s32[4]{0:T(128)} %constant.115.clone) | copy-start | bytes 52
  65.3 31.5 %copy-start.3 = (bf16[2,192,2048]{2,1,0:T(8,128)(2,1)}, bf16[2,192,2048]{2,1,0:T(8,128)(2,1)S(1)}, u32[]{:S(2)}) copy-start(bf16[2,192,2048]{2,1,0:T(8,128)(2,1)S(1)} %collective-permute-done.10.refs_9_.refs_13_) | copy-start | bytes 4718596
  67.6 29.2 %copy-start.4 = (bf16[2,192,2048]{2,1,0:T(8,128)(2,1)}, bf16[2,192,2048]{2,1,0:T(8,128)(2,1)S(1)}, u32[]{:S(2)}) copy-start(bf16[2,192,2048]{2,1,0:T(8,128)(2,1)S(1)} %collective-permute-done.11.refs_10_.refs_14_) | copy-start | bytes 4718596
  67.6 29.2 %collective-permute-start.12 = (bf16[3,192,2048]{2,1,0:T(8,128)(2,1)S(1)}, bf16[3,192,2048]{2,1,0:T(8,128)(2,1)S(1)}, u32[]{:S(2)}, u32[]{:S(2)}) collective-permute-start(bf16[3,192,2048]{2,1,0:T(8,128)(2,1)S(1)} %get-tuple-element.36), channel_id=1, source_target_pairs={{0,2},{1,9},{2,4},{3,11},{4,6},{5,13},{6,0},{7,15},{8,10},{9,17},{... | collective-permute-start | bytes 7077896 | tf_op jit(solution)/shard_map/ppermute | solution.py:42
  67.6 29.2 %collective-permute-start.13 = (bf16[3,192,2048]{2,1,0:T(8,128)(2,1)S(1)}, bf16[3,192,2048]{2,1,0:T(8,128)(2,1)}, u32[]{:S(2)}, u32[]{:S(2)}) collective-permute-start(bf16[3,192,2048]{2,1,0:T(8,128)(2,1)S(1)} %get-tuple-element.37), channel_id=1, source_target_pairs={{0,6},{1,25},{2,0},{3,27},{4,2},{5,29},{6,4},{7,31},{8,14},{9,1},{... | collective-permute-start | bytes 7077896 | tf_op jit(solution)/shard_map/ppermute | solution.py:42
  96.8 11.2 %copy-start = (bf16[3,192,2048]{2,1,0:T(8,128)(2,1)}, bf16[3,192,2048]{2,1,0:T(8,128)(2,1)S(1)}, u32[]{:S(2)}) copy-start(bf16[3,192,2048]{2,1,0:T(8,128)(2,1)S(1)} %collective-permute-done.12.refs_3_.refs_1_.refs_5_) | copy-start | bytes 7077892
  96.9 11.2 %collective-permute-start.14 = (bf16[3,192,2048]{2,1,0:T(8,128)(2,1)S(1)}, bf16[3,192,2048]{2,1,0:T(8,128)(2,1)}, u32[]{:S(2)}, u32[]{:S(2)}) collective-permute-start(bf16[3,192,2048]{2,1,0:T(8,128)(2,1)S(1)} %collective-permute-done.12.refs_3_.refs_1_.refs_5_), channel_id=1, source_target_pairs={{0,1},{1,0},{2,3},{3,2},{4,5},{5,4},{6,7},{7,6},{8,9},{9,8},{10,11... | collective-permute-start | bytes 7077896 | tf_op jit(solution)/shard_map/ppermute | solution.py:46
  98.2 9.9 %collective-permute-start.15 = (bf16[3,192,2048]{2,1,0:T(8,128)(2,1)}, bf16[3,192,2048]{2,1,0:T(8,128)(2,1)}, u32[]{:S(2)}, u32[]{:S(2)}) collective-permute-start(bf16[3,192,2048]{2,1,0:T(8,128)(2,1)} %collective-permute-done.13.refs_7_.refs_2_.refs_6_), channel_id=1, source_target_pairs={{0,1},{1,0},{2,3},{3,2},{4,5},{5,4},{6,7},{7,6},{8,9},{9,8},{10,11... | collective-permute-start | bytes 7077896 | tf_op jit(solution)/shard_map/ppermute | solution.py:46
  103.3 31.9 %collective-permute-start.18 = (bf16[2,192,2048]{2,1,0:T(8,128)(2,1)}, bf16[2,192,2048]{2,1,0:T(8,128)(2,1)}, u32[]{:S(2)}, u32[]{:S(2)}) collective-permute-start(bf16[2,192,2048]{2,1,0:T(8,128)(2,1)} %copy-done.1), channel_id=1, source_target_pairs={{0,1},{1,0},{2,3},{3,2},{4,5},{5,4},{6,7},{7,6},{8,9},{9,8},{10,11... | collective-permute-start | bytes 4718600 | tf_op jit(solution)/shard_map/ppermute | solution.py:46
  103.8 26.2 %collective-permute-start.16 = (bf16[1,192,2048]{2,1,0:T(8,128)(2,1)S(1)}, bf16[1,192,2048]{2,1,0:T(8,128)(2,1)S(1)}, u32[]{:S(2)}, u32[]{:S(2)}) collective-permute-start(bf16[1,192,2048]{2,1,0:T(8,128)(2,1)S(1)} %slice.212), channel_id=1, source_target_pairs={{0,2},{1,9},{2,4},{3,11},{4,6},{5,13},{6,0},{7,15},{8,10},{9,17},{... | collective-permute-start | bytes 2359304 | tf_op jit(solution)/shard_map/ppermute | solution.py:42
  105.1 25.7 %collective-permute-start.17 = (bf16[1,192,2048]{2,1,0:T(8,128)(2,1)S(1)}, bf16[1,192,2048]{2,1,0:T(8,128)(2,1)}, u32[]{:S(2)}, u32[]{:S(2)}) collective-permute-start(bf16[1,192,2048]{2,1,0:T(8,128)(2,1)S(1)} %slice.213), channel_id=1, source_target_pairs={{0,6},{1,25},{2,0},{3,27},{4,2},{5,29},{6,4},{7,31},{8,14},{9,1},{... | collective-permute-start | bytes 2359304 | tf_op jit(solution)/shard_map/ppermute | solution.py:42
  130.0 5.3 %copy-start.7 = (bf16[1,192,2048]{2,1,0:T(8,128)(2,1)}, bf16[1,192,2048]{2,1,0:T(8,128)(2,1)S(1)}, u32[]{:S(2)}) copy-start(bf16[1,192,2048]{2,1,0:T(8,128)(2,1)S(1)} %collective-permute-done.16.refs_3_) | copy-start | bytes 2359300
  130.0 5.2 %collective-permute-start.19 = (bf16[1,192,2048]{2,1,0:T(8,128)(2,1)S(1)}, bf16[1,192,2048]{2,1,0:T(8,128)(2,1)S(1)}, u32[]{:S(2)}, u32[]{:S(2)}) collective-permute-start(bf16[1,192,2048]{2,1,0:T(8,128)(2,1)S(1)} %collective-permute-done.16.refs_3_), channel_id=1, source_target_pairs={{0,1},{1,0},{2,3},{3,2},{4,5},{5,4},{6,7},{7,6},{8,9},{9,8},{10,11... | collective-permute-start | bytes 2359304 | tf_op jit(solution)/shard_map/ppermute | solution.py:46
  130.8 4.4 %collective-permute-start.20 = (bf16[1,192,2048]{2,1,0:T(8,128)(2,1)}, bf16[1,192,2048]{2,1,0:T(8,128)(2,1)S(1)}, u32[]{:S(2)}, u32[]{:S(2)}) collective-permute-start(bf16[1,192,2048]{2,1,0:T(8,128)(2,1)} %collective-permute-done.17.refs_7_), channel_id=1, source_target_pairs={{0,1},{1,0},{2,3},{3,2},{4,5},{5,4},{6,7},{7,6},{8,9},{9,8},{10,11... | collective-permute-start | bytes 2359304 | tf_op jit(solution)/shard_map/ppermute | solution.py:46
  131.7 22.4 %collective-permute-start.23 = (bf16[576,768]{1,0:T(8,128)(2,1)}, bf16[576,768]{1,0:T(8,128)(2,1)S(1)}, u32[]{:S(2)}, u32[]{:S(2)}) collective-permute-start(bf16[576,768]{1,0:T(8,128)(2,1)} %get-tuple-element.40.refs_0_), channel_id=1, source_target_pairs={{0,32},{32,64},{64,96},{96,0},{1,33},{33,65},{65,97},{97,1},{2,34}... | collective-permute-start | bytes 2654216 | tf_op jit(solution)/shard_map/ppermute | solution.py:58
  132.3 21.9 %collective-permute-start.21 = (bf16[576,768]{1,0:T(8,128)(2,1)}, bf16[576,768]{1,0:T(8,128)(2,1)S(1)}, u32[]{:S(2)}, u32[]{:S(2)}) collective-permute-start(bf16[576,768]{1,0:T(8,128)(2,1)} %get-tuple-element.40.refs_0_), channel_id=1, source_target_pairs={{0,96},{32,0},{64,32},{96,64},{1,97},{33,1},{65,33},{97,65},{2,98}... | collective-permute-start | bytes 2654216 | tf_op jit(solution)/shard_map/ppermute | solution.py:58
  135.2 0.9 copy-start.8
  135.3 1.2 copy-start.9
  154.0 2.2 copy-start.6
  154.2 3.6 %copy-start.10 = (bf16[576,768]{1,0:T(8,128)(2,1)}, bf16[576,768]{1,0:T(8,128)(2,1)S(1)}, u32[]{:S(2)}) copy-start(bf16[576,768]{1,0:T(8,128)(2,1)S(1)} %collective-permute-done.23.refs_4_) | copy-start | bytes 2654212
  154.2 3.5 %copy-start.11 = (bf16[576,768]{1,0:T(8,128)(2,1)}, bf16[576,768]{1,0:T(8,128)(2,1)S(1)}, u32[]{:S(2)}) copy-start(bf16[576,768]{1,0:T(8,128)(2,1)S(1)} %collective-permute-done.21.refs_1_) | copy-start | bytes 2654212
  157.7 51.5 %collective-permute-start.22 = (bf16[1440,768]{1,0:T(8,128)(2,1)S(1)}, bf16[1440,768]{1,0:T(8,128)(2,1)}, u32[]{:S(2)}, u32[]{:S(2)}) collective-permute-start(bf16[1440,768]{1,0:T(8,128)(2,1)S(1)} %get-tuple-element.59), channel_id=1, source_target_pairs={{0,96},{32,0},{64,32},{96,64},{1,97},{33,1},{65,33},{97,65},{2,98}... | collective-permute-start | bytes 6635528 | tf_op jit(solution)/shard_map/ppermute | solution.py:58
  158.2 49.4 %collective-permute-start.24 = (bf16[1440,768]{1,0:T(8,128)(2,1)}, bf16[1440,768]{1,0:T(8,128)(2,1)}, u32[]{:S(2)}, u32[]{:S(2)}) collective-permute-start(bf16[1440,768]{1,0:T(8,128)(2,1)} %get-tuple-element.58), channel_id=1, source_target_pairs={{0,32},{32,64},{64,96},{96,0},{1,33},{33,65},{65,97},{97,1},{2,34}... | collective-permute-start | bytes 6635528 | tf_op jit(solution)/shard_map/ppermute | solution.py:58
  175.4 69.1 %all-to-all-start.1 = ((bf16[32,72,1024]{2,1,0:T(8,128)(2,1)}), bf16[32,72,1024]{2,1,0:T(8,128)(2,1)}, u32[]{:S(2)}, u32[]{:S(2)}) async-start(bf16[32,72,1024]{2,1,0:T(8,128)(2,1)} %rowgrad.1), calls=%async_computation.1 | async-start | bytes 9437184 | tf_op jit(solution)/shard_map/all_to_all | solution.py:500
  208.8 19.9 %collective-permute-start.25 = (bf16[576,768]{1,0:T(8,128)(2,1)S(1)}, bf16[576,768]{1,0:T(8,128)(2,1)S(1)}, u32[]{:S(2)}, u32[]{:S(2)}) collective-permute-start(bf16[576,768]{1,0:T(8,128)(2,1)S(1)} %slice.171), channel_id=1, source_target_pairs={{0,32},{32,64},{64,96},{96,0},{1,33},{33,65},{65,97},{97,1},{2,34}... | collective-permute-start | bytes 2654216 | tf_op jit(solution)/shard_map/ppermute | solution.py:58
  210.5 19.2 %collective-permute-start.26 = (bf16[576,768]{1,0:T(8,128)(2,1)S(1)}, bf16[576,768]{1,0:T(8,128)(2,1)S(1)}, u32[]{:S(2)}, u32[]{:S(2)}) collective-permute-start(bf16[576,768]{1,0:T(8,128)(2,1)S(1)} %slice.172), channel_id=1, source_target_pairs={{0,96},{32,0},{64,32},{96,64},{1,97},{33,1},{65,33},{97,65},{2,98}... | collective-permute-start | bytes 2654216 | tf_op jit(solution)/shard_map/ppermute | solution.py:58
  228.6 1.1 copy-start.17
  229.7 1.0 copy-start.18
  (1 other events, 0.7 us)
Sparse Core Ops, SparseCore 0:
  97.0 80.8 all-gather.1
